TPU v7x, 128 devices: a whole 4x4x4 slice. The times are simulated.
128 devices in a mesh: seq: 32 (over z, y_hi, x), exp: 4 (over y_lo, core).
Axes of the slice: x: 4, y: 4 (y_hi: 2, y_lo: 2; y = y_hi * 2 + y_lo), z: 4, core: 2. Of those that a mesh axis runs over, the one named last changes fastest.
Arguments:
- hidden_in: bfloat16 [8192, 1536], P('seq'), may hold values from -6 to 6
- attn_gain: float32 [1536], replicated, may hold values from 0.1 to 1.9
- q_weight: bfloat16 [1536, 1536], P(None, 'exp'), may hold values from -1.25 to 1.25
- k_weight: bfloat16 [1536, 512], P(None, 'exp'), may hold values from -0.625 to 0.625
- v_weight: bfloat16 [1536, 512], P(None, 'exp'), may hold values from -0.15625 to 0.15625
- o_weight: bfloat16 [1536, 1536], P('exp'), may hold values from -0.15625 to 0.15625
- cache_kv: bfloat16 [16384, 1024], P('seq', 'exp'), may hold values from -216 to 216
- moe_gain: float32 [1536], replicated, may hold values from 0.1 to 1.9
- expert_in: bfloat16 [32, 1536, 1024], P('seq'), may hold values from -0.15625 to 0.15625
- expert_out: bfloat16 [32, 512, 1536], P('seq'), may hold values from -0.25 to 0.25
- routes: int32 [8192, 8], P(('seq', 'exp')), may hold values from 0 to 31, all different within a row; in each aligned block of 64 rows (0 to 63, 64 to 127, ...) at most 32 rows name the same one
- route_prob: float32 [8192, 8], P(('seq', 'exp')), may hold values from 0.05 to 1
- page_slot: int32 [1024], replicated, may hold values from 0 to 31, as said below
Outputs:
- hidden_out: bfloat16 [8192, 1536], P(('seq', 'exp'))
- decode_pages: bfloat16 [1024, 8, 2, 512], P('seq', 'exp')
Inputs may be any that keep to these rules, and one draw needn't show every extreme that they name: `routes`: in each aligned block of 64 rows (the rows of one device) no expert is named by more than 32 rows; a row names 8 different experts. `page_slot`: for each r, the 32 blocks b with b mod (32) == r have different slots.
All inputs are finite; a program needn't handle non-finite values.
Results may differ from a plain program's by a relative error of at most 0.0074.
Values may be sent and summed in bfloat16 or wider, within the bound.
A program may use at most 128 MiB of HBM per device.

v0:
```python
import math

import jax
import jax.numpy as jnp
from jax import lax
from jax.sharding import PartitionSpec as P

HEADS = 24
KV_HEADS = 8
HEAD_DIM = 64
EXPERTS = 32
PAGE = 8


norm_epsilon = 1e-06
attention_scale = 0.015625
residual_scale = 0.22
masked_score = -1e30


def rms_norm(values, gain_row):
    widened = values.astype(jnp.float32)
    spread = lax.rsqrt(jnp.mean(widened * widened, axis=-1, keepdims=True) + norm_epsilon)
    return (widened * spread * gain_row).astype(jnp.bfloat16)


def attend_block(carried, query_heads, visible, key_rows, value_rows):
    best_old, total_old, summed_old = carried
    scores = (
        jnp.einsum("tkgd,nkd->kgtn", query_heads, key_rows, preferred_element_type=jnp.float32)
        * attention_scale
    )
    scores = jnp.where(visible, scores, masked_score)
    best_new = jnp.maximum(best_old, jnp.max(scores, axis=-1))
    weights = jnp.where(visible, jnp.exp(scores - best_new[..., None]), 0.0)
    factor = jnp.exp(best_old - best_new)
    total_new = total_old * factor + jnp.sum(weights, axis=-1)
    summed_new = summed_old * factor[..., None] + jnp.einsum(
        "kgtn,nkd->kgtd",
        weights.astype(jnp.bfloat16),
        value_rows,
        preferred_element_type=jnp.float32,
    )
    return (best_new, total_new, summed_new)


def block_size(piece_rows):
    return math.gcd(piece_rows, 512)


def body(
    hidden_in,
    attn_gain,
    q_weight,
    k_weight,
    v_weight,
    o_weight,
    cache_kv,
    moe_gain,
    expert_in,
    expert_out,
    routes,
    route_prob,
    page_slot,
):
    seq_count = lax.axis_size("seq")
    seq_index = lax.axis_index("seq")
    exp_index = lax.axis_index("exp")
    tokens_here = hidden_in.shape[0]
    head_dim = HEAD_DIM
    kv_local = k_weight.shape[1] // head_dim
    group_size = HEADS // KV_HEADS
    prompt_len = tokens_here * seq_count // 2
    first_row = seq_index * tokens_here
    query_rows = first_row + jnp.arange(tokens_here, dtype=jnp.int32)
    query_second = query_rows >= prompt_len
    holds_first = first_row < prompt_len
    normed = rms_norm(hidden_in, attn_gain)
    queries = jnp.dot(normed, q_weight, preferred_element_type=jnp.float32).astype(jnp.bfloat16)
    keys_new = jnp.dot(normed, k_weight, preferred_element_type=jnp.float32).astype(jnp.bfloat16)
    values_new = jnp.dot(normed, v_weight, preferred_element_type=jnp.float32).astype(jnp.bfloat16)
    pair_width = 2 * kv_local * head_dim
    pairs_new = jnp.stack(
        [
            keys_new.reshape(tokens_here, kv_local, head_dim),
            values_new.reshape(tokens_here, kv_local, head_dim),
        ],
        axis=2,
    ).reshape(tokens_here, pair_width)
    query_heads = queries.reshape(tokens_here, kv_local, group_size, head_dim)
    cache_lines = cache_kv.reshape(tokens_here, -1)
    blocks_here = tokens_here // PAGE
    rounds = blocks_here // seq_count
    outgoing = pairs_new.reshape(rounds, seq_count, PAGE * pair_width)
    received = lax.all_to_all(outgoing, "seq", split_axis=1, concat_axis=1, tiled=True)
    block_ids = (
        jnp.arange(seq_count, dtype=jnp.int32)[None, :] * blocks_here
        + jnp.arange(rounds, dtype=jnp.int32)[:, None] * seq_count
        + seq_index
    ).reshape(-1)
    table_ids = jnp.arange(page_slot.shape[0], dtype=jnp.int32)
    page_slots = jnp.sum(
        jnp.where(block_ids[:, None] == table_ids[None, :], page_slot[None, :], 0), axis=1
    )
    local_pages = (
        jnp.zeros((blocks_here, PAGE * pair_width), jnp.bfloat16)
        .at[page_slots]
        .set(received.reshape(blocks_here, -1))
    )
    page_rows = local_pages.reshape(blocks_here, PAGE, kv_local, 2, head_dim).transpose(
        0, 2, 3, 1, 4
    )
    page_rows = page_rows.reshape(blocks_here, kv_local, 2, PAGE * head_dim)
    start_state = (
        jnp.full((kv_local, group_size, tokens_here), masked_score, jnp.float32),
        jnp.zeros((kv_local, group_size, tokens_here), jnp.float32),
        jnp.zeros((kv_local, group_size, tokens_here, head_dim), jnp.float32),
    )

    def new_keys_part(carried, new_block, key_first):
        width_rows = new_block.shape[0]
        key_rows = key_first + jnp.arange(width_rows, dtype=jnp.int32)
        visible = ((key_rows >= prompt_len)[None, :] == query_second[:, None]) & (
            key_rows[None, :] <= query_rows[:, None]
        )
        split_pairs = new_block.reshape(width_rows, kv_local, 2, head_dim)
        return lax.cond(
            jnp.any(visible),
            lambda carried_in: attend_block(
                carried_in, query_heads, visible, split_pairs[:, :, 0], split_pairs[:, :, 1]
            ),
            lambda carried_in: carried_in,
            carried,
        )

    carried = start_state
    new_piece = lax.all_gather(pairs_new, "seq", axis=0, tiled=True)
    cache_piece = lax.all_gather(cache_lines, "seq", axis=0, tiled=True)
    piece_rows = new_piece.shape[0]
    stride = block_size(piece_rows)
    new_blocks = new_piece.reshape(piece_rows // stride, stride, -1)
    cache_blocks = cache_piece.reshape(piece_rows // stride, 2 * stride, kv_local, 2, head_dim)
    offsets = stride * jnp.arange(piece_rows // stride, dtype=jnp.int32)
    everything = jnp.ones((tokens_here, 2 * stride), bool)

    def visit(carried_in, block_part):
        new_block, cache_block, key_first = block_part
        carried_in = new_keys_part(carried_in, new_block, key_first)
        carried_in = lax.cond(
            holds_first,
            lambda inner: attend_block(
                inner, query_heads, everything, cache_block[:, :, 0], cache_block[:, :, 1]
            ),
            lambda inner: inner,
            carried_in,
        )
        return (carried_in, None)

    carried, _ = lax.scan(visit, carried, (new_blocks, cache_blocks, offsets))
    best_final, total_final, summed_final = carried
    attended = (
        (summed_final / total_final[..., None])
        .transpose(2, 0, 1, 3)
        .reshape(tokens_here, -1)
        .astype(jnp.bfloat16)
    )
    mixed_rows = lax.psum_scatter(
        jnp.dot(attended, o_weight, preferred_element_type=jnp.float32).astype(jnp.bfloat16),
        "exp",
        scatter_dimension=0,
        tiled=True,
    ).astype(jnp.float32)
    moe_rows = mixed_rows.shape[0]
    residual = (
        lax.dynamic_slice_in_dim(hidden_in, exp_index * moe_rows, moe_rows, 0).astype(jnp.float32)
        + residual_scale * mixed_rows
    )
    moe_in = rms_norm(residual, moe_gain)
    top_count = routes.shape[1]
    assigns = moe_rows * top_count
    capacity = 2 * moe_rows * top_count // EXPERTS
    flat_ids = routes.reshape(-1)
    hit_table = (flat_ids[:, None] == jnp.arange(EXPERTS, dtype=jnp.int32)[None, :]).astype(
        jnp.int32
    )
    earlier = jnp.cumsum(hit_table, axis=0) - hit_table
    slot_rank = jnp.sum(earlier * hit_table, axis=1)
    dest_slot = flat_ids * capacity + slot_rank
    source = (
        jnp.full((EXPERTS * capacity,), assigns, jnp.int32)
        .at[dest_slot]
        .set(jnp.arange(assigns, dtype=jnp.int32))
    )
    filled = source < assigns
    picked = moe_in[jnp.minimum(source, assigns - 1) // top_count]
    dispatched = jnp.where(filled[:, None], picked, jnp.zeros_like(picked)).reshape(
        seq_count, EXPERTS // seq_count, capacity, -1
    )
    hidden = jnp.einsum(
        "sexd,edf->sexf",
        lax.all_to_all(dispatched, "seq", split_axis=0, concat_axis=0, tiled=True),
        expert_in,
        preferred_element_type=jnp.float32,
    )
    half_width = hidden.shape[-1] // 2
    active = (jax.nn.silu(hidden[..., :half_width]) * hidden[..., half_width:]).astype(jnp.bfloat16)
    produced = jnp.einsum(
        "sexf,efd->sexd", active, expert_out, preferred_element_type=jnp.float32
    ).astype(jnp.bfloat16)
    returned = lax.all_to_all(produced, "seq", split_axis=0, concat_axis=0, tiled=True)
    flat_back = returned.reshape(EXPERTS * capacity, -1)
    per_assign = flat_back[dest_slot].reshape(moe_rows, top_count, -1)
    share = route_prob / jnp.sum(route_prob, axis=-1, keepdims=True)
    moe = jnp.sum(share[..., None] * per_assign.astype(jnp.float32), axis=1)
    hidden_out = (residual + residual_scale * moe).astype(jnp.bfloat16)
    return (hidden_out, page_rows)


def solution(mesh):
    return jax.shard_map(
        body,
        mesh=mesh,
        in_specs=(
            P("seq", None),
            P(),
            P(None, "exp"),
            P(None, "exp"),
            P(None, "exp"),
            P("exp", None),
            P("seq", "exp"),
            P(),
            P("seq", None, None),
            P("seq", None, None),
            P(("seq", "exp"), None),
            P(("seq", "exp"), None),
            P(),
        ),
        out_specs=(P(("seq", "exp"), None), P("seq", "exp", None, None)),
        check_vma=False,
    )
```

profile of v0, /device:TPU:0, one launch (start us, length us, event | category | flops | bytes accessed | tf_op | source)
XLA Modules:
  0.0 643.0 jit_solution(13268402075678019474)
XLA Ops:
  16.2 79.8 %all-gather.3.cloned.1.call-done = bf16[8192,256]{0,1:T(8,128)(2,1)} async-done(((bf16[256,256]{0,1:T(8,128)(2,1)}), bf16[8192,256]{0,1:T(8,128)(2,1)}) %all-gather.3.cloned.1.call-update) | async-done | bytes 4194320 | tf_op jit(solution)/shard_map/all_gather | solution.py:137
  96.0 4.6 copy.129
  100.7 103.1 %all-gather.5.cloned.1.call-done = bf16[8192,512]{1,0:T(8,128)(2,1)} async-done(((bf16[256,512]{1,0:T(8,128)(2,1)}), bf16[8192,512]{1,0:T(8,128)(2,1)}) %all-gather.5.cloned.1.call-update) | async-done | bytes 8388624 | tf_op jit(solution)/shard_map/all_gather | solution.py:138
  203.8 30.3 %reshape.180 = bf16[16,1024,2,2,64]{4,3,2,1,0:T(2,128)(2,1)} reshape(bf16[8192,512]{1,0:T(8,128)(2,1)} %all-gather.5.cloned.1.call-done) | data formatting | bytes 16777216 | tf_op jit(solution)/shard_map/reshape | solution.py:142
  234.1 39.1 %copy.94 = bf16[16,1024,2,2,64]{1,4,2,3,0:T(8,128)(2,1)} copy(bf16[16,1024,2,2,64]{4,3,2,1,0:T(2,128)(2,1)} %reshape.180) | data formatting | bytes 16777216
  274.0 169.9 %while.16 = (s32[]{:T(128)}, f32[2,3,256]{2,1,0:T(4,128)S(1)}, f32[2,3,256]{2,1,0:T(4,128)S(1)}, f32[2,3,256,64]{2,3,1,0:T(8,128)}, pred[]{:T(512)}, /*index=5*/...) while((s32[]{:T(128)}, f32[2,3,256]{2,1,0:T(4,128)S(1)}, ...), condition=%wide.region_11.12_spmd.clone.clone, body=%wide.region_1.11_spmd.clone.clone.sunk | while | flops 627712256 | bytes 40714208 | solution.py:159
  279.1 4.2 conditional.8
  283.3 5.2 conditional.9
  293.6 5.2 conditional.9
  304.0 5.2 conditional.9
  314.4 5.2 conditional.9
  324.7 5.2 conditional.9
  335.1 5.2 conditional.9
  345.4 5.2 conditional.9
  355.8 5.2 conditional.9
  366.2 5.2 conditional.9
  376.5 5.2 conditional.9
  386.9 5.2 conditional.9
  397.2 5.2 conditional.9
  407.6 5.2 conditional.9
  417.9 5.2 conditional.9
  428.3 5.2 conditional.9
  438.7 5.2 conditional.9
  452.5 40.2 %reduce-scatter.2.cloned.1.call-done = bf16[64,1536]{1,0:T(8,128)(2,1)} async-done(((bf16[256,1536]{1,0:T(8,128)(2,1)}), bf16[64,1536]{1,0:T(8,128)(2,1)}) %reduce-scatter.2.cloned.1.call-update) | async-done | bytes 196624 | tf_op jit(solution)/shard_map/reduce_scatter | solution.py:167
  495.1 5.6 gather_fusion
  504.5 9.6 %all-to-all-start = ((bf16[32,1,32,1536]{3,2,1,0:T(8,128)(2,1)}), bf16[32,1,32,1536]{3,2,1,0:T(8,128)(2,1)}, u32[]{:S(2)}, u32[]{:S(2)}) async-start(bf16[32,1,32,1536]{3,2,1,0:T(8,128)(2,1)} %broadcast_select_fusion), calls=%async_computation.1 | async-start | bytes 6291456 | tf_op jit(solution)/shard_map/all_to_all | solution.py:201
  519.2 36.5 %all-to-all-done = bf16[32,1,32,1536]{3,2,1,0:T(8,128)(2,1)} async-done(((bf16[32,1,32,1536]{3,2,1,0:T(8,128)(2,1)}), bf16[32,1,32,1536]{3,2,1,0:T(8,128)(2,1)}, u32[]{:S(2)}, u32[]{:S(2)}) %all-to-all-start) | async-done | bytes 3145760 | tf_op jit(solution)/shard_map/all_to_all | solution.py:201
  555.7 9.1 %all-to-all-start.2 = ((bf16[32,2,1024]{2,1,0:T(2,128)(2,1)}), bf16[32,2,1024]{2,1,0:T(2,128)(2,1)S(1)}, u32[]{:S(2)}, u32[]{:S(2)}) async-start(bf16[32,2,1024]{2,1,0:T(2,128)(2,1)} %reshape.238), calls=%async_computation.3 | async-start | bytes 262144 | tf_op jit(solution)/shard_map/all_to_all | solution.py:95
  564.9 5.4 fusion.32
  575.1 8.8 %all-to-all-start.1 = ((bf16[32,1,32,1536]{3,2,1,0:T(8,128)(2,1)}), bf16[32,1,32,1536]{3,2,1,0:T(8,128)(2,1)}, u32[]{:S(2)}, u32[]{:S(2)}) async-start(bf16[32,1,32,1536]{3,2,1,0:T(8,128)(2,1)} %fusion.27), calls=%async_computation.2 | async-start | bytes 6291456 | tf_op jit(solution)/shard_map/all_to_all | solution.py:210
  588.6 36.6 %all-to-all-done.1 = bf16[32,1,32,1536]{3,2,1,0:T(8,128)(2,1)} async-done(((bf16[32,1,32,1536]{3,2,1,0:T(8,128)(2,1)}), bf16[32,1,32,1536]{3,2,1,0:T(8,128)(2,1)}, u32[]{:S(2)}, u32[]{:S(2)}) %all-to-all-start.1) | async-done | bytes 3145760 | tf_op jit(solution)/shard_map/all_to_all | solution.py:210
  625.2 6.7 %gather_fusion.1 = bf16[512,1536]{1,0:T(8,128)(2,1)} fusion(bf16[1024,1536]{1,0:T(8,128)(2,1)} %bitcast.43, s32[1024]{0:T(1024)S(1)} %pad_clamp_fusion), kind=kCustom, calls=%fused_computation.1 | custom fusion | bytes 3147776 | tf_op jit(solution)/shard_map/gather | solution.py:212
  (400 shorter events, 201.7 us)
Async XLA Ops:
  7.2 557.7 %copy-start = (bf16[1,1536,1024]{2,1,0:T(8,128)(2,1)S(1)}, bf16[1,1536,1024]{2,1,0:T(8,128)(2,1)}, u32[]{:S(2)}) copy-start(bf16[1,1536,1024]{2,1,0:T(8,128)(2,1)} %param.27) | copy-start | bytes 9437188
  7.2 6.7 %copy-start.15 = (f32[1536]{0:T(1024)S(1)}, f32[1536]{0:T(1024)}, u32[]{:S(2)}) copy-start(f32[1536]{0:T(1024)} %param.20) | copy-start | bytes 18436
  7.2 5.8 copy-start.8
  7.2 88.8 %all-gather.3.cloned.1.call-start = ((), (), s32[]{:S(2)}) async-start(), calls=%async_computation.4 | async-start | bytes 4325376 | tf_op jit(solution)/shard_map/all_gather | solution.py:137
  13.0 190.8 %all-gather.5.cloned.1.call-start = ((), (), s32[]{:S(2)}) async-start(), calls=%async_computation.5 | async-start | bytes 8650752 | tf_op jit(solution)/shard_map/all_gather | solution.py:138
  13.8 478.9 %reduce-scatter.2.cloned.1.call-start = ((), (), s32[]{:S(2)}) async-start(), calls=%async_computation.6 | async-start | bytes 983040 | tf_op jit(solution)/shard_map/reduce_scatter | solution.py:167
  279.1 2.5 copy-start.1
  279.1 2.5 copy-start.5
  285.4 1.1 copy-start.3
  295.8 1.1 copy-start.3
  306.2 1.1 copy-start.3
  316.5 1.1 copy-start.3
  326.9 1.1 copy-start.3
  337.2 1.1 copy-start.3
  347.6 1.1 copy-start.3
  358.0 1.1 copy-start.3
  368.3 1.1 copy-start.3
  389.0 1.1 copy-start.3
  399.4 1.1 copy-start.3
  430.5 1.1 copy-start.3
  440.8 1.1 copy-start.3
  443.9 3.8 copy-start.10
  443.9 50.1 %copy-start.12 = (f32[1536]{0:T(1024)S(1)}, f32[1536]{0:T(1024)}, u32[]{:S(2)}) copy-start(f32[1536]{0:T(1024)} %param.26) | copy-start | bytes 18436
  504.5 9.6 %copy-start.7 = (bf16[256,2,2,64]{0,3,2,1:T(8,128)(2,1)S(1)}, bf16[256,2,2,64]{0,3,2,1:T(8,128)(2,1)}, u32[]{:S(2)}) copy-start(bf16[256,2,2,64]{0,3,2,1:T(8,128)(2,1)} %pad_maximum_fusion) | copy-start | bytes 393220
  504.5 51.2 %all-to-all-start = ((bf16[32,1,32,1536]{3,2,1,0:T(8,128)(2,1)}), bf16[32,1,32,1536]{3,2,1,0:T(8,128)(2,1)}, u32[]{:S(2)}, u32[]{:S(2)}) async-start(bf16[32,1,32,1536]{3,2,1,0:T(8,128)(2,1)} %broadcast_select_fusion), calls=%async_computation.1 | async-start | bytes 6291456 | tf_op jit(solution)/shard_map/all_to_all | solution.py:201
  555.7 19.4 %all-to-all-start.2 = ((bf16[32,2,1024]{2,1,0:T(2,128)(2,1)}), bf16[32,2,1024]{2,1,0:T(2,128)(2,1)S(1)}, u32[]{:S(2)}, u32[]{:S(2)}) async-start(bf16[32,2,1024]{2,1,0:T(2,128)(2,1)} %reshape.238), calls=%async_computation.3 | async-start | bytes 262144 | tf_op jit(solution)/shard_map/all_to_all | solution.py:95
  564.8 5.4 copy-start.14
  573.8 10.1 %copy-start.11 = (f32[64,8]{0,1:T(8,128)S(1)}, f32[64,8]{0,1:T(8,128)}, u32[]{:S(2)}) copy-start(f32[64,8]{0,1:T(8,128)} %param.30) | copy-start | bytes 6148
  573.8 10.8 %copy-start.13 = (s32[1024]{0:T(1024)S(1)}, s32[1024]{0:T(1024)}, u32[]{:S(2)}) copy-start(s32[1024]{0:T(1024)} %param.31) | copy-start | bytes 12292
  575.1 50.1 %all-to-all-start.1 = ((bf16[32,1,32,1536]{3,2,1,0:T(8,128)(2,1)}), bf16[32,1,32,1536]{3,2,1,0:T(8,128)(2,1)}, u32[]{:S(2)}, u32[]{:S(2)}) async-start(bf16[32,1,32,1536]{3,2,1,0:T(8,128)(2,1)} %fusion.27), calls=%async_computation.2 | async-start | bytes 6291456 | tf_op jit(solution)/shard_map/all_to_all | solution.py:210
  625.2 6.7 %copy-start.9 = (f32[64,8]{1,0:T(8,128)S(1)}, f32[64,8]{1,0:T(8,128)}, u32[]{:S(2)}) copy-start(f32[64,8]{1,0:T(8,128)} %copy.95) | copy-start | bytes 6148
  625.2 9.6 %copy-start.6 = (bf16[64,1536]{1,0:T(8,128)(2,1)S(1)}, bf16[64,1536]{1,0:T(8,128)(2,1)}, u32[]{:S(2)}) copy-start(bf16[64,1536]{1,0:T(8,128)(2,1)} %reduce-scatter.2.cloned.1.call-done) | copy-start | bytes 589828
  (20 other events, 15.8 us)
Sparse Core Ops, SparseCore 0:
  13.1 82.9 all-gather.2
  99.1 104.6 all-gather.4
  447.8 44.8 reduce-scatter.1
where the time goes:
time: 652 us; the launch traced here: 643 us
  waiting for transfers between devices  298 us (46%)
  local copies, waits for them, and re-layouts  166 us (25%)
  other arithmetic  69.2 us (11%)
  matrix products  56.1 us (9%)
  starting transfers between devices  27.6 us (4%)
  between operations  14.1 us (2%)
  loops' own time  12 us (2%)
    all_gather x1, waiting for transfers between devices, body(): cache_piece = lax.all_gather(cache_lines, 'seq', axis=0, tiled=True)  103 us
    all_gather x1, waiting for transfers between devices, body(): new_piece = lax.all_gather(pairs_new, 'seq', axis=0, tiled=True)  79.8 us
    unnamed x29, local copies, waits for them, and re-layouts  43.1 us
    reduce_scatter x1, waiting for transfers between devices, body(): lax.psum_scatter(jnp.dot(attended, o_weight, preferred_element_type=jnp.f...  40.2 us
    dynamic_slice x32, local copies, waits for them, and re-layouts, body(): carried, _ = lax.scan(visit, carried, (new_blocks, cache_blocks, offsets))  37 us
    all_to_all x1, waiting for transfers between devices, body(): lax.all_to_all(produced, 'seq', split_axis=0, concat_axis=0, tiled=True)  36.6 us
    all_to_all x1, waiting for transfers between devices, body(): lax.all_to_all(dispatched, 'seq', split_axis=0, concat_axis=0, tiled=True)  36.5 us
    reshape x1, local copies, waits for them, and re-layouts, body(): cache_piece.reshape(piece_rows // stride, 2 * stride, kv_local, 2, head_dim)  30.3 us
  transfers between devices with their start and end apart: 6, of which 6 were waited for; matrix products, arithmetic and copies ran while one was open for 5% of the time, Pallas kernels for 0%

commit v1 on v0

v1 whole, which is shorter than its diff:
```python
import functools

import jax
import jax.numpy as jnp
from jax import lax
from jax.experimental import pallas as pl
from jax.experimental.pallas import tpu as pltpu
from jax.sharding import PartitionSpec as P

HEADS_HERE = 6
KV_HERE = 2
GROUP = 3
HEAD_DIM = 64
EXPERTS = 32
CAP = 32
PAGE = 8
PLANES = 4
LINE = 8
ROWS = 256
CACHE_HERE = 512

norm_epsilon = 1e-06
attention_scale = 0.015625
residual_scale = 0.22
masked_score = -1e30

PLANE_GROUPS = [[z * LINE + i for i in range(LINE)] for z in range(PLANES)]
LINE_GROUPS = [[z * LINE + i for z in range(PLANES)] for i in range(LINE)]


def rms_norm(values, gain_row):
    widened = values.astype(jnp.float32)
    spread = lax.rsqrt(jnp.mean(widened * widened, axis=-1, keepdims=True) + norm_epsilon)
    return (widened * spread * gain_row).astype(jnp.bfloat16)


def flash_kernel(q_ref, cache_ref, new_ref, out_ref, cache_val, new_val, qs, best, acc):
    seq_index = lax.axis_index("seq")
    plane = seq_index // LINE
    place = seq_index % LINE
    lane = lax.broadcasted_iota(jnp.int32, (ROWS, 2 * HEAD_DIM), 1)
    low = lane < HEAD_DIM

    def fill(source, target):
        @pl.loop(0, source.shape[0] // ROWS)
        def _(step):
            rows = pl.ds(pl.multiple_of(step * ROWS, ROWS), ROWS)
            for g in range(KV_HERE):
                cols = slice(g * 128, (g + 1) * 128)
                target[rows, cols] = jnp.where(low, jnp.ones((), jnp.bfloat16), source[rows, cols])

    fill(cache_ref, cache_val)
    fill(new_ref, new_val)

    def update(g, key_block, value_block, masked):
        for a in range(GROUP):
            rows = slice(a * ROWS, (a + 1) * ROWS)
            scores = lax.dot_general(
                qs[rows, :], key_block, (((1,), (1,)), ((), ())), preferred_element_type=jnp.float32
            )
            if masked:
                r = lax.broadcasted_iota(jnp.int32, scores.shape, 0)
                c = lax.broadcasted_iota(jnp.int32, scores.shape, 1)
                scores = jnp.where(c <= r, scores, masked_score)
            old = best[rows, :]
            new = jnp.maximum(old, jnp.max(scores, axis=-1, keepdims=True))
            best[rows, :] = new
            weights = jnp.exp(scores - new[:, :1]).astype(jnp.bfloat16)
            acc[rows, :] = acc[rows, :] * jnp.exp(old - new) + jnp.dot(
                weights, value_block, preferred_element_type=jnp.float32
            )

    BK = 1024

    @pl.loop(0, PLANES)
    def _(t):
        is_own = t == plane
        is_full = jnp.logical_and(plane % 2 == 0, t == plane + 1)
        cache_steps = jnp.where(t < 2, PLANES * 1024 // BK, 0)
        full_steps = jnp.where(is_own, place, jnp.where(is_full, LINE, 0))
        heads = []
        for g in range(KV_HERE):
            cols = slice(g * 128, (g + 1) * 128)
            for a in range(GROUP):
                h = g * GROUP + a
                slab = q_ref[t, :, (h // 2) * 128 : (h // 2 + 1) * 128]
                slab = slab.astype(jnp.float32) * attention_scale
                if h % 2:
                    slab = pltpu.roll(slab, HEAD_DIM, 1)
                qs[a * ROWS : (a + 1) * ROWS, :] = jnp.where(low, slab, 0.0).astype(jnp.bfloat16)
            best[...] = jnp.full_like(best, masked_score)
            acc[...] = jnp.zeros_like(acc)

            @pl.loop(0, cache_steps)
            def _(step):
                rows = pl.ds(pl.multiple_of(step * BK, BK), BK)
                update(g, cache_ref[rows, cols], cache_val[rows, cols], False)

            @pl.loop(0, full_steps)
            def _(step):
                rows = pl.ds(pl.multiple_of(step * ROWS, ROWS), ROWS)
                update(g, new_ref[rows, cols], new_val[rows, cols], False)

            @pl.when(is_own)
            def _():
                rows = pl.ds(pl.multiple_of(place * ROWS, ROWS), ROWS)
                update(g, new_ref[rows, cols], new_val[rows, cols], True)

            for a in range(GROUP):
                rows = slice(a * ROWS, (a + 1) * ROWS)
                part = acc[rows, :]
                total = part[:, :1]
                safe = jnp.where(total > 0.0, total, 1.0)
                heads.append((part / safe, jnp.where(total > 0.0, best[rows, :1] + jnp.log(safe), masked_score)))
        for p in range(HEADS_HERE // 2):
            pair = jnp.where(low, pltpu.roll(heads[2 * p][0], HEAD_DIM, 1), heads[2 * p + 1][0])
            out_ref[t, :, p * 128 : (p + 1) * 128] = pair.astype(jnp.bfloat16)
        levels = jnp.zeros((ROWS, 128), jnp.float32)
        for h in range(HEADS_HERE):
            levels = jnp.where(lane % 8 == h, heads[h][1], levels)
        high = levels.astype(jnp.bfloat16).astype(jnp.float32)
        rest = levels - high
        middle = rest.astype(jnp.bfloat16).astype(jnp.float32)
        split = jnp.where(lane < 8, high, jnp.where(lane < 16, middle, rest - middle))
        out_ref[t, :, 384:512] = split.astype(jnp.bfloat16)


def flash(queries, cache_rows, new_rows):
    vmem = pl.BlockSpec(memory_space=pltpu.VMEM)
    return pl.pallas_call(
        flash_kernel,
        out_shape=jax.ShapeDtypeStruct((PLANES, ROWS, 512), jnp.bfloat16),
        in_specs=[vmem] * 3,
        out_specs=vmem,
        scratch_shapes=[
            pltpu.VMEM(cache_rows.shape, jnp.bfloat16),
            pltpu.VMEM(new_rows.shape, jnp.bfloat16),
            pltpu.VMEM((GROUP * ROWS, 128), jnp.bfloat16),
            pltpu.VMEM((GROUP * ROWS, 128), jnp.float32),
            pltpu.VMEM((GROUP * ROWS, 128), jnp.float32),
        ],
        compiler_params=pltpu.CompilerParams(vmem_limit_bytes=48 * 1024 * 1024),
        name="flash",
    )(queries, cache_rows, new_rows)


def pages(pairs_new, page_slot, seq_index):
    seq_count = 32
    blocks_here = ROWS // PAGE
    outgoing = pairs_new.reshape(seq_count, PAGE * 256)
    received = lax.all_to_all(outgoing, "seq", split_axis=0, concat_axis=0, tiled=True)
    slots = lax.dynamic_index_in_dim(page_slot.reshape(seq_count, seq_count), seq_index, 1, keepdims=False)
    place = (slots[None, :] == jnp.arange(blocks_here, dtype=jnp.int32)[:, None]).astype(jnp.bfloat16)
    placed = jnp.dot(place, received, preferred_element_type=jnp.float32).astype(jnp.bfloat16)
    page_rows = placed.reshape(blocks_here, PAGE, KV_HERE, 2, HEAD_DIM).transpose(0, 2, 3, 1, 4)
    return page_rows.reshape(blocks_here, KV_HERE, 2, PAGE * HEAD_DIM)


def body(
    hidden_in,
    attn_gain,
    q_weight,
    k_weight,
    v_weight,
    o_weight,
    cache_kv,
    moe_gain,
    expert_in,
    expert_out,
    routes,
    route_prob,
    page_slot,
):
    seq_index = lax.axis_index("seq")
    exp_index = lax.axis_index("exp")
    cache_rows = lax.all_gather(cache_kv, "seq", axis_index_groups=PLANE_GROUPS, tiled=True)
    normed = rms_norm(hidden_in, attn_gain)
    pair_weight = jnp.concatenate(
        [k_weight[:, :64], v_weight[:, :64], k_weight[:, 64:], v_weight[:, 64:]], axis=1
    )
    pairs_new = jnp.dot(normed, pair_weight, preferred_element_type=jnp.float32).astype(jnp.bfloat16)
    new_rows = lax.all_gather(pairs_new, "seq", axis_index_groups=PLANE_GROUPS, tiled=True)
    queries = jnp.dot(normed, q_weight, preferred_element_type=jnp.float32).astype(jnp.bfloat16)
    line_queries = lax.all_gather(queries, "seq", axis_index_groups=LINE_GROUPS)
    partial = flash(line_queries, cache_rows, new_rows)
    parts = lax.all_to_all(
        partial, "seq", split_axis=0, concat_axis=0, axis_index_groups=LINE_GROUPS, tiled=True
    ).astype(jnp.float32)
    levels = parts[..., 384:390] + parts[..., 392:398] + parts[..., 400:406]
    shares = jnp.exp(levels - jnp.max(levels, axis=0, keepdims=True))
    shares = shares / jnp.sum(shares, axis=0, keepdims=True)
    outs = parts[..., :384].reshape(PLANES, ROWS, HEADS_HERE, HEAD_DIM)
    attended = jnp.sum(outs * shares[..., None], axis=0).reshape(ROWS, 384).astype(jnp.bfloat16)

    page_rows = pages(pairs_new, page_slot, seq_index)

    mixed_rows = lax.psum_scatter(
        jnp.dot(attended, o_weight, preferred_element_type=jnp.float32).astype(jnp.bfloat16),
        "exp",
        scatter_dimension=0,
        tiled=True,
    ).astype(jnp.float32)
    moe_rows = mixed_rows.shape[0]
    residual = (
        lax.dynamic_slice_in_dim(hidden_in, exp_index * moe_rows, moe_rows, 0).astype(jnp.float32)
        + residual_scale * mixed_rows
    )
    moe_in = rms_norm(residual, moe_gain)

    named = (routes[:, :, None] == jnp.arange(EXPERTS, dtype=jnp.int32)).astype(jnp.float32)
    hit = jnp.sum(named, axis=1)
    share = route_prob / jnp.sum(route_prob, axis=-1, keepdims=True)
    share_of = jnp.sum(named * share[..., None], axis=1)
    before = jnp.tril(jnp.ones((moe_rows, moe_rows), jnp.bfloat16), -1)
    rank = jnp.dot(before, hit.astype(jnp.bfloat16), preferred_element_type=jnp.float32)
    slot = jnp.arange(CAP, dtype=jnp.float32)
    chosen = jnp.where(hit[..., None] > 0, (rank[..., None] == slot).astype(jnp.float32), 0.0)
    chosen = chosen.reshape(moe_rows, EXPERTS * CAP)
    mixing = chosen * jnp.repeat(share_of, CAP, axis=1)
    dispatched = lax.dot_general(
        chosen.astype(jnp.bfloat16), moe_in, (((0,), (0,)), ((), ())), preferred_element_type=jnp.float32
    ).astype(jnp.bfloat16)
    arrived = lax.all_to_all(
        dispatched.reshape(EXPERTS, CAP, -1), "seq", split_axis=0, concat_axis=0, tiled=True
    ).reshape(EXPERTS * CAP, -1)
    hidden = jnp.dot(arrived, expert_in[0], preferred_element_type=jnp.float32)
    half_width = hidden.shape[-1] // 2
    active = (jax.nn.silu(hidden[:, :half_width]) * hidden[:, half_width:]).astype(jnp.bfloat16)
    produced = jnp.dot(active, expert_out[0], preferred_element_type=jnp.float32).astype(jnp.bfloat16)
    returned = lax.all_to_all(
        produced.reshape(EXPERTS, CAP, -1), "seq", split_axis=0, concat_axis=0, tiled=True
    ).reshape(EXPERTS * CAP, -1)
    high = mixing.astype(jnp.bfloat16)
    low = (mixing - high.astype(jnp.float32)).astype(jnp.bfloat16)
    moe = jnp.dot(high, returned, preferred_element_type=jnp.float32) + jnp.dot(
        low, returned, preferred_element_type=jnp.float32
    )
    hidden_out = (residual + residual_scale * moe).astype(jnp.bfloat16)
    return (hidden_out, page_rows)


def solution(mesh):
    return jax.shard_map(
        body,
        mesh=mesh,
        in_specs=(
            P("seq", None),
            P(),
            P(None, "exp"),
            P(None, "exp"),
            P(None, "exp"),
            P("exp", None),
            P("seq", "exp"),
            P(),
            P("seq", None, None),
            P("seq", None, None),
            P(("seq", "exp"), None),
            P(("seq", "exp"), None),
            P(),
        ),
        out_specs=(P(("seq", "exp"), None), P("seq", "exp", None, None)),
        check_vma=False,
    )
```

time: 652 us -> 383 us (0.59)
  local copies, waits for them, and re-layouts: 166 us -> 17.7 us
  waiting for transfers between devices: 298 us -> 197 us
  other arithmetic: 69.2 us -> 8.77 us
  Pallas kernels: 0 us -> 55 us
  blocking collectives: 0 us -> 33.5 us
  matrix products: 56.1 us -> 24.7 us
  loops' own time: 12 us -> 0 us
    all_gather x2, waiting for transfers between devices: 183 us -> 87.6 us  [the longest x1 56.1 us: body(): lax.all_gather(cache_kv, 'seq', axis_index_groups=PLANE_GROUPS, tiled=True)]
    pallas_call x0 -> x1, Pallas kernels: none -> 55 us  [flash(): pl.pallas_call(flash_kernel, out_shape=jax.ShapeDtypeStruct((PLANES, ROWS...]
    unnamed x29 -> x38, local copies, waits for them, and re-layouts: 43.1 us -> 6.2 us
    dynamic_slice x32 -> x1, local copies, waits for them, and re-layouts: 37 us -> 0.7 us  [pages(): lax.dynamic_index_in_dim(page_slot.reshape(seq_count, seq_count), seq_ind...]
    reshape x4 -> x3, local copies, waits for them, and re-layouts: 35.9 us -> 2.14 us  [the longest x1 1.83 us: pages(): return page_rows.reshape(blocks_here, KV_HERE, 2, PAGE * HEAD_DIM)]
    dot_general x38 -> x8, matrix products: 51.2 us -> 21.1 us  [the longest x1 5.41 us: body(): hidden = jnp.dot(arrived, expert_in[0], preferred_element_type=jnp.float32)]
    all_to_all x0 -> x1, blocking collectives: none -> 18 us  [body(): lax.all_to_all(partial, 'seq', split_axis=0, concat_axis=0, axis_index_gr...]
    reduce_sum x20 -> x3, other arithmetic: 20.5 us -> 2.91 us  [the longest x1 2.18 us: body(): jnp.sum(outs * shares[..., None], axis=0).reshape(ROWS, 384)]
where the time goes in v1:
time: 383 us; the launch traced here: 378 us
  waiting for transfers between devices  197 us (51%)
  Pallas kernels  55 us (14%)
  blocking collectives  33.5 us (9%)
  starting transfers between devices  27.5 us (7%)
  matrix products  24.7 us (6%)
  local copies, waits for them, and re-layouts  17.7 us (5%)
  between operations  14 us (4%)
  other arithmetic  8.77 us (2%)
    all_gather x1, waiting for transfers between devices, body(): lax.all_gather(cache_kv, 'seq', axis_index_groups=PLANE_GROUPS, tiled=True)  56.1 us
    pallas_call x1, Pallas kernels, flash(): pl.pallas_call(flash_kernel, out_shape=jax.ShapeDtypeStruct((PLANES, ROWS...  55 us
    all_to_all x1, waiting for transfers between devices, body(): lax.all_to_all(dispatched.reshape(EXPERTS, CAP, -1), 'seq', split_axis=0,...  40.2 us
    all_to_all x1, waiting for transfers between devices, body(): lax.all_to_all(produced.reshape(EXPERTS, CAP, -1), 'seq', split_axis=0, c...  37.1 us
    all_gather x1, waiting for transfers between devices, body(): lax.all_gather(pairs_new, 'seq', axis_index_groups=PLANE_GROUPS, tiled=True)  31.5 us
    reduce_scatter x1, waiting for transfers between devices, body(): lax.psum_scatter(jnp.dot(attended, o_weight, preferred_element_type=jnp.f...  30.5 us
    all_to_all x1, blocking collectives, body(): lax.all_to_all(partial, 'seq', split_axis=0, concat_axis=0, axis_index_gr...  18 us
    all_gather x1, blocking collectives, body(): line_queries = lax.all_gather(queries, 'seq', axis_index_groups=LINE_GROUPS)  15.5 us
  transfers between devices with their start and end apart: 6, of which 6 were waited for; matrix products, arithmetic and copies ran while one was open for 5% of the time, Pallas kernels for 0%

profile of v1, /device:TPU:0, one launch (start us, length us, event | category | flops | bytes accessed | tf_op | source)
XLA Modules:
  0.0 378.5 jit_solution(4695110996019126034)
XLA Ops:
  7.2 1.5 fusion.7
  8.8 1.7 fusion.59
  10.5 1.5 convolution_convert_fusion.5
  12.8 2.1 convolution_convert_fusion.4
  14.9 15.5 %all-gather = bf16[1024,384]{1,0:T(8,128)(2,1)} all-gather(bf16[256,384]{1,0:T(8,128)(2,1)S(1)} %convolution_convert_fusion.4), channel_id=2, replica_groups={{0,32,64,96},{4,36,68,100},{8,40,72,104},{12,44,76,108},{16,48,80,112},..., dimensions={0}, use_global_device_ids=true | all-gather | bytes 983040 | tf_op jit(solution)/shard_map/all_gather | solution.py:184
  30.5 31.5 %all-gather.6.cloned.1.call-done.new_ref = bf16[2048,256]{1,0:T(8,128)(2,1)} async-done(((bf16[256,256]{1,0:T(8,128)(2,1)}), bf16[2048,256]{1,0:T(8,128)(2,1)}) %all-gather.6.cloned.1.call-update) | async-done | bytes 1048592 | tf_op jit(solution)/shard_map/all_gather | solution.py:182
  61.9 56.1 %all-gather.4.cloned.1.call-done.cache_ref = bf16[4096,256]{1,0:T(8,128)(2,1)} async-done(((bf16[512,256]{1,0:T(8,128)(2,1)}), bf16[4096,256]{1,0:T(8,128)(2,1)}) %all-gather.4.cloned.1.call-update) | async-done | bytes 2097168 | tf_op jit(solution)/shard_map/all_gather | solution.py:176
  119.2 1.6 copy-done.2
  120.8 1.2 copy-done.3
  122.0 55.0 %flash.1 = bf16[4,256,512]{2,1,0:T(8,128)(2,1)S(1)} custom-call(bf16[4,256,384]{2,1,0:T(8,128)(2,1)S(1)} %bitcast.42, bf16[4096,256]{1,0:T(8,128)(2,1)S(1)} %copy-done.2, bf16[2048,256]{1,0:T(8,128)(2,1)S(1)} %copy-done.3), custom_call_target="tpu_custom_call" | custom-call | tf_op jit(solution)/shard_map/flash/pallas_call | solution.py:130
  177.0 18.0 %all_to_all.28 = bf16[4,256,512]{2,1,0:T(8,128)(2,1)S(1)} all-to-all(bf16[4,256,512]{2,1,0:T(8,128)(2,1)S(1)} %flash.1), channel_id=1, replica_groups={{0,32,64,96},{4,36,68,100},{8,40,72,104},{12,44,76,108},{16,48,80,112},..., dimensions={0} | all-to-all | bytes 2097152 | tf_op jit(solution)/shard_map/all_to_all | solution.py:186
  195.3 1.3 copy-done.4
  197.9 1.2 copy.40
  199.2 1.3 mul.84
  200.4 3.0 copy.41
  203.5 2.2 fusion.10
  205.7 1.5 convolution_convert_fusion.2
  208.4 30.5 %reduce-scatter.2.cloned.1.call-done = bf16[64,1536]{1,0:T(8,128)(2,1)} async-done(((bf16[256,1536]{1,0:T(8,128)(2,1)}), bf16[64,1536]{1,0:T(8,128)(2,1)}) %reduce-scatter.2.cloned.1.call-update) | async-done | bytes 196624 | tf_op jit(solution)/shard_map/reduce_scatter | solution.py:197
  238.9 1.2 multiply_reduce_fusion
  240.1 3.7 convolution_convert_fusion.1
  243.8 9.6 %all-to-all-start.1 = ((bf16[32,32,1536]{2,1,0:T(8,128)(2,1)}), bf16[32,32,1536]{2,1,0:T(8,128)(2,1)}, u32[]{:S(2)}, u32[]{:S(2)}) async-start(bf16[32,32,1536]{2,1,0:T(8,128)(2,1)} %bitcast.43), calls=%async_computation.2 | async-start | bytes 6291456 | tf_op jit(solution)/shard_map/all_to_all | solution.py:223
  254.0 1.4 reduce.3
  256.2 40.2 %all-to-all-done.1 = bf16[32,32,1536]{2,1,0:T(8,128)(2,1)} async-done(((bf16[32,32,1536]{2,1,0:T(8,128)(2,1)}), bf16[32,32,1536]{2,1,0:T(8,128)(2,1)}, u32[]{:S(2)}, u32[]{:S(2)}) %all-to-all-start.1) | async-done | bytes 3145760 | tf_op jit(solution)/shard_map/all_to_all | solution.py:223
  296.3 9.0 %all-to-all-start.3 = ((bf16[32,2,1024]{2,1,0:T(2,128)(2,1)}), bf16[32,2,1024]{2,1,0:T(2,128)(2,1)S(1)}, u32[]{:S(2)}, u32[]{:S(2)}) async-start(bf16[32,2,1024]{2,1,0:T(2,128)(2,1)} %reshape.90), calls=%async_computation.4 | async-start | bytes 262144 | tf_op jit(solution)/shard_map/all_to_all | solution.py:151
  305.3 5.4 %fusion = f32[1024,1024]{1,0:T(8,128)S(1)} fusion(bf16[1024,1536]{1,0:T(8,128)(2,1)} %bitcast.5, bf16[1,1536,1024]{2,1,0:T(8,128)(2,1)S(1)} %copy-done), kind=kOutput, calls=%fused_computation.2 | convolution fusion | flops 3221225472 | bytes 10485760 | tf_op jit(solution)/shard_map/dot_general | solution.py:226
  310.8 3.5 convolution_convert_fusion
  314.2 1.3 all-to-all-done.3
  315.6 8.8 %all-to-all-start.2 = ((bf16[32,32,1536]{2,1,0:T(8,128)(2,1)}), bf16[32,32,1536]{2,1,0:T(8,128)(2,1)}, u32[]{:S(2)}, u32[]{:S(2)}) async-start(bf16[32,32,1536]{2,1,0:T(8,128)(2,1)} %bitcast.45), calls=%async_computation.3 | async-start | bytes 6291456 | tf_op jit(solution)/shard_map/all_to_all | solution.py:230
  327.1 1.8 reshape.85
  328.9 37.1 %all-to-all-done.2 = bf16[32,32,1536]{2,1,0:T(8,128)(2,1)} async-done(((bf16[32,32,1536]{2,1,0:T(8,128)(2,1)}), bf16[32,32,1536]{2,1,0:T(8,128)(2,1)}, u32[]{:S(2)}, u32[]{:S(2)}) %all-to-all-start.2) | async-done | bytes 3145760 | tf_op jit(solution)/shard_map/all_to_all | solution.py:230
  366.0 2.6 convolution_bitcast_fusion.1
  368.7 3.3 fusion.5
  (63 shorter events, 8.9 us)
Async XLA Ops:
  7.2 298.1 %copy-start = (bf16[1,1536,1024]{2,1,0:T(8,128)(2,1)S(1)}, bf16[1,1536,1024]{2,1,0:T(8,128)(2,1)}, u32[]{:S(2)}) copy-start(bf16[1,1536,1024]{2,1,0:T(8,128)(2,1)} %param.21) | copy-start | bytes 9437188
  7.2 3.3 copy-start.17
  7.2 54.7 %all-gather.6.cloned.1.call-start = ((), (), s32[]{:S(2)}) async-start(), calls=%async_computation.6 | async-start | bytes 1179648 | tf_op jit(solution)/shard_map/all_gather | solution.py:182
  7.2 3.3 copy-start.5
  12.0 106.0 %all-gather.4.cloned.1.call-start = ((), (), s32[]{:S(2)}) async-start(), calls=%async_computation.5 | async-start | bytes 2359296 | tf_op jit(solution)/shard_map/all_gather | solution.py:176
  12.8 226.1 %reduce-scatter.2.cloned.1.call-start = ((), (), s32[]{:S(2)}) async-start(), calls=%async_computation.7 | async-start | bytes 983040 | tf_op jit(solution)/shard_map/reduce_scatter | solution.py:197
  118.1 1.1 copy-start.1
  119.2 1.6 copy-start.2
  120.8 1.2 copy-start.3
  195.3 1.3 copy-start.4
  203.5 2.2 copy-start.7
  205.7 1.6 copy-start.12
  205.7 1.6 copy-start.14
  205.7 34.4 %copy-start.13 = (f32[1536]{0:T(1024)S(1)}, f32[1536]{0:T(1024)}, u32[]{:S(2)}) copy-start(f32[1536]{0:T(1024)} %param.20) | copy-start | bytes 18436
  208.0 35.8 %copy-start.10 = (pred[64,32]{0,1:T(8,128)(4,1)}, pred[64,32]{0,1:T(8,128)(4,1)S(1)}, u32[]{:S(2)}) copy-start(pred[64,32]{0,1:T(8,128)(4,1)S(1)} %broadcast_compare_fusion) | copy-start | bytes 6148
  243.8 9.6 %copy-start.8 = (bf16[256,256]{1,0:T(8,128)(2,1)S(1)}, bf16[256,256]{1,0:T(8,128)(2,1)}, u32[]{:S(2)}) copy-start(bf16[256,256]{1,0:T(8,128)(2,1)} %convolution_convert_fusion.5) | copy-start | bytes 393220
  243.8 52.5 %all-to-all-start.1 = ((bf16[32,32,1536]{2,1,0:T(8,128)(2,1)}), bf16[32,32,1536]{2,1,0:T(8,128)(2,1)}, u32[]{:S(2)}, u32[]{:S(2)}) async-start(bf16[32,32,1536]{2,1,0:T(8,128)(2,1)} %bitcast.43), calls=%async_computation.2 | async-start | bytes 6291456 | tf_op jit(solution)/shard_map/all_to_all | solution.py:223
  296.3 19.2 %all-to-all-start.3 = ((bf16[32,2,1024]{2,1,0:T(2,128)(2,1)}), bf16[32,2,1024]{2,1,0:T(2,128)(2,1)S(1)}, u32[]{:S(2)}, u32[]{:S(2)}) async-start(bf16[32,2,1024]{2,1,0:T(2,128)(2,1)} %reshape.90), calls=%async_computation.4 | async-start | bytes 262144 | tf_op jit(solution)/shard_map/all_to_all | solution.py:151
  305.3 5.4 %copy-start.16 = (bf16[1,512,1536]{2,1,0:T(8,128)(2,1)S(1)}, bf16[1,512,1536]{2,1,0:T(8,128)(2,1)}, u32[]{:S(2)}) copy-start(bf16[1,512,1536]{2,1,0:T(8,128)(2,1)} %param.22) | copy-start | bytes 4718596
  315.5 8.8 %copy-start.15 = (s32[1024]{0:T(1024)S(1)}, s32[1024]{0:T(1024)}, u32[]{:S(2)}) copy-start(s32[1024]{0:T(1024)} %param.25) | copy-start | bytes 12292
  315.6 50.5 %all-to-all-start.2 = ((bf16[32,32,1536]{2,1,0:T(8,128)(2,1)}), bf16[32,32,1536]{2,1,0:T(8,128)(2,1)}, u32[]{:S(2)}, u32[]{:S(2)}) async-start(bf16[32,32,1536]{2,1,0:T(8,128)(2,1)} %bitcast.45), calls=%async_computation.3 | async-start | bytes 6291456 | tf_op jit(solution)/shard_map/all_to_all | solution.py:230
  327.1 41.6 %copy-start.6 = (bf16[64,1536]{1,0:T(8,128)(2,1)S(1)}, bf16[64,1536]{1,0:T(8,128)(2,1)}, u32[]{:S(2)}) copy-start(bf16[64,1536]{1,0:T(8,128)(2,1)} %reduce-scatter.2.cloned.1.call-done) | copy-start | bytes 589828
  327.1 41.6 %copy-start.9 = (f32[64,32]{0,1:T(8,128)S(1)}, f32[64,32]{0,1:T(8,128)}, u32[]{:S(2)}) copy-start(f32[64,32]{0,1:T(8,128)} %get-tuple-element.2) | copy-start | bytes 24580
  327.1 41.6 %copy-start.11 = (pred[64,32]{0,1:T(8,128)(4,1)S(1)}, pred[64,32]{0,1:T(8,128)(4,1)}, u32[]{:S(2)}) copy-start(pred[64,32]{0,1:T(8,128)(4,1)} %copy-done.10) | copy-start | bytes 6148
Sparse Core Ops, SparseCore 0:
  12.1 49.7 all-gather.5
  64.2 53.7 all-gather.3
  207.3 31.5 reduce-scatter.1

commit v2 on v1

v2 whole, which is shorter than its diff:
```python
import functools

import jax
import jax.numpy as jnp
from jax import lax
from jax.experimental import pallas as pl
from jax.experimental.pallas import tpu as pltpu
from jax.sharding import PartitionSpec as P

HEADS_HERE = 6
KV_HERE = 2
GROUP = 3
HEAD_DIM = 64
EXPERTS = 32
CAP = 32
PAGE = 8
PLANES = 4
LINE = 8
ROWS = 256
CACHE_HERE = 512

norm_epsilon = 1e-06
attention_scale = 0.015625
residual_scale = 0.22
masked_score = -1e30


def rms_norm(values, gain_row):
    widened = values.astype(jnp.float32)
    spread = lax.rsqrt(jnp.mean(widened * widened, axis=-1, keepdims=True) + norm_epsilon)
    return (widened * spread * gain_row).astype(jnp.bfloat16)


def attend_kernel(
    q_ref, cache_ref, new_ref, out_ref,
    q_all, cache_all, new_all, cache_val, new_val, qs, best, acc, part_send, part_recv,
    q_out, q_in, cache_out, cache_in, new_out, new_in, part_out, part_in,
):
    seq_index = lax.axis_index("seq")
    plane = seq_index // LINE
    place = seq_index % LINE
    even = plane % 2 == 0
    lane = lax.broadcasted_iota(jnp.int32, (ROWS, 2 * HEAD_DIM), 1)
    low = lane < HEAD_DIM
    one = jnp.ones((), jnp.bfloat16)

    def send(source, target, out_sem, in_sem, to):
        return pltpu.make_async_remote_copy(
            src_ref=source, dst_ref=target, send_sem=out_sem, recv_sem=in_sem,
            device_id={"seq": to}, device_id_type=pl.DeviceIdType.MESH,
        )

    def peer(j):
        return plane * LINE + lax.rem(place + j, LINE)

    def line_peer(k):
        return lax.rem(plane + k, PLANES) * LINE + place

    def cache_copy(j):
        return send(cache_ref, cache_all.at[j], cache_out.at[j], cache_in.at[j], peer(j))

    def new_copy(j):
        return send(new_ref, new_all.at[j], new_out.at[j], new_in.at[j], peer(j))

    def query_copy(k):
        return send(q_ref, q_all.at[plane], q_out.at[k], q_in.at[k], line_peer(k))

    def part_copy(k):
        return send(
            part_send.at[k], part_recv.at[k], part_out.at[k], part_in.at[k], line_peer(k)
        )

    def sends_query(k):
        return jnp.logical_or(plane < 2, plane == 3) if k == 3 else plane < 2

    def gets_query(k):
        origin = lax.rem(plane + PLANES - k, PLANES)
        return jnp.logical_or(origin < 2, origin == 3) if k == 3 else origin < 2

    def sends_part(k):
        target = lax.rem(plane + k, PLANES)
        return jnp.logical_or(target < 2, target == 3) if k == 1 else target < 2

    def gets_part(k):
        return jnp.logical_or(plane < 2, plane == 3) if k == 1 else plane < 2

    barrier = pltpu.get_barrier_semaphore()

    @pl.loop(1, LINE)
    def _(j):
        pl.semaphore_signal(barrier, inc=1, device_id={"seq": peer(j)}, device_id_type=pl.DeviceIdType.MESH)

    for k in range(1, PLANES):
        pl.semaphore_signal(
            barrier, inc=1, device_id={"seq": line_peer(k)}, device_id_type=pl.DeviceIdType.MESH
        )

    q_all[plane] = q_ref[...]
    cache_all[0] = cache_ref[...]
    new_all[0] = new_ref[...]
    best[...] = jnp.full_like(best, masked_score)
    acc[...] = jnp.zeros_like(acc)
    for k in range(1, PLANES):
        @pl.when(jnp.logical_not(gets_part(k)))
        def _():
            part_recv[k, :, :384] = jnp.zeros((ROWS, 384), jnp.bfloat16)
            part_recv[k, :, 384:] = jnp.full((ROWS, 128), masked_score, jnp.bfloat16)

    pl.semaphore_wait(barrier, LINE - 1 + PLANES - 1)

    for k in range(1, PLANES):
        @pl.when(sends_query(k))
        def _():
            query_copy(k).start()

    @pl.loop(1, LINE)
    def _(j):
        cache_copy(j).start()
        new_copy(j).start()

    def prepare(t):
        for h in range(HEADS_HERE):
            slab = q_all[t, :, (h // 2) * 128 : (h // 2 + 1) * 128]
            slab = slab.astype(jnp.float32) * attention_scale
            if h % 2:
                slab = pltpu.roll(slab, HEAD_DIM, 1)
            a = h % GROUP
            qs[t, h // GROUP, a * ROWS : (a + 1) * ROWS, :] = jnp.where(low, slab, 0.0).astype(jnp.bfloat16)

    def update(t, g, key_block, value_block, masked):
        for a in range(GROUP):
            rows = slice(a * ROWS, (a + 1) * ROWS)
            scores = lax.dot_general(
                qs[t, g, rows, :], key_block, (((1,), (1,)), ((), ())), preferred_element_type=jnp.float32
            )
            if masked:
                r = lax.broadcasted_iota(jnp.int32, scores.shape, 0)
                c = lax.broadcasted_iota(jnp.int32, scores.shape, 1)
                scores = jnp.where(c <= r, scores, masked_score)
            old = best[t, g, rows, :]
            new = jnp.maximum(old, jnp.max(scores, axis=-1, keepdims=True))
            best[t, g, rows, :] = new
            weights = jnp.exp(scores - new[:, :1]).astype(jnp.bfloat16)
            acc[t, g, rows, :] = acc[t, g, rows, :] * jnp.exp(old - new) + jnp.dot(
                weights, value_block, preferred_element_type=jnp.float32
            )

    def slab_of(g):
        return slice(g * 128, (g + 1) * 128)

    def fill_new(j):
        for g in range(KV_HERE):
            new_val[:, slab_of(g)] = jnp.where(low, one, new_all[j, :, slab_of(g)])

    prepare(plane)
    fill_new(0)
    for g in range(KV_HERE):
        update(plane, g, new_ref[:, slab_of(g)], new_val[:, slab_of(g)], True)

    for k in range(1, PLANES):
        @pl.when(gets_query(k))
        def _():
            query_copy(k).wait_recv()
            prepare(lax.rem(plane + PLANES - k, PLANES))

    @pl.loop(0, LINE)
    def _(j):
        @pl.when(j > 0)
        def _():
            cache_copy(j).wait_recv()
            new_copy(j).wait_recv()

        for half in range(CACHE_HERE // ROWS):
            rows = slice(half * ROWS, (half + 1) * ROWS)
            for g in range(KV_HERE):
                cache_val[rows, slab_of(g)] = jnp.where(low, one, cache_all[j, rows, slab_of(g)])

        @pl.loop(0, 2)
        def _(t):
            for g in range(KV_HERE):
                update(t, g, cache_all[j, :, slab_of(g)], cache_val[:, slab_of(g)], False)

        fill_new(j)
        first = jnp.where(jnp.logical_and(j > 0, j <= place), 0, 1)
        last = jnp.where(even, 2, 1)

        @pl.loop(first, last)
        def _(step):
            for g in range(KV_HERE):
                update(plane + step, g, new_all[j, :, slab_of(g)], new_val[:, slab_of(g)], False)

    def finish(t):
        heads = []
        for h in range(HEADS_HERE):
            g, rows = h // GROUP, slice((h % GROUP) * ROWS, (h % GROUP + 1) * ROWS)
            part = acc[t, g, rows, :]
            total = part[:, :1]
            heads.append((part / total, best[t, g, rows, :] + jnp.log(total)))
        levels = jnp.zeros((ROWS, 128), jnp.float32)
        for h in range(HEADS_HERE):
            levels = jnp.where(lane % 8 == h, heads[h][1], levels)
        return [
            jnp.where(low, pltpu.roll(heads[2 * p][0], HEAD_DIM, 1), heads[2 * p + 1][0])
            for p in range(HEADS_HERE // 2)
        ], levels

    for k in range(1, PLANES):
        @pl.when(sends_part(k))
        def _():
            pairs, levels = finish(lax.rem(plane + k, PLANES))
            for p in range(HEADS_HERE // 2):
                part_send[k, :, p * 128 : (p + 1) * 128] = pairs[p].astype(jnp.bfloat16)
            high = levels.astype(jnp.bfloat16).astype(jnp.float32)
            rest = levels - high
            middle = rest.astype(jnp.bfloat16).astype(jnp.float32)
            split = jnp.where(lane < 8, high, jnp.where(lane < 16, middle, rest - middle))
            part_send[k, :, 384:512] = split.astype(jnp.bfloat16)
            part_copy(k).start()

    pairs, own_level = finish(plane)
    for k in range(1, PLANES):
        @pl.when(gets_part(k))
        def _():
            part_copy(k).wait_recv()
    levels = [own_level]
    for k in range(1, PLANES):
        slab = part_recv[k, :, 384:512].astype(jnp.float32)
        levels.append(slab + pltpu.roll(slab, 120, 1) + pltpu.roll(slab, 112, 1))
    top = functools.reduce(jnp.maximum, levels)
    shares = [jnp.exp(level - top) for level in levels]
    whole = functools.reduce(jnp.add, shares)
    shares = [share / whole for share in shares]

    def spread(share, p):
        return jnp.where(low, share[:, 2 * p : 2 * p + 1], share[:, 2 * p + 1 : 2 * p + 2])

    for p in range(HEADS_HERE // 2):
        cols = slice(p * 128, (p + 1) * 128)
        value = pairs[p] * spread(shares[0], p)
        for k in range(1, PLANES):
            value = value + part_recv[k, :, cols].astype(jnp.float32) * spread(shares[k], p)
        out_ref[:, cols] = value.astype(jnp.bfloat16)

    @pl.loop(1, LINE)
    def _(j):
        cache_copy(j).wait_send()
        new_copy(j).wait_send()

    for k in range(1, PLANES):
        @pl.when(sends_query(k))
        def _():
            query_copy(k).wait_send()

        @pl.when(sends_part(k))
        def _():
            part_copy(k).wait_send()


def attend(queries, cache_rows, new_rows):
    vmem = pl.BlockSpec(memory_space=pltpu.VMEM)
    state = pltpu.VMEM((PLANES, KV_HERE, GROUP * ROWS, 128), jnp.float32)
    return pl.pallas_call(
        attend_kernel,
        out_shape=jax.ShapeDtypeStruct((ROWS, 384), jnp.bfloat16),
        in_specs=[vmem] * 3,
        out_specs=vmem,
        scratch_shapes=[
            pltpu.VMEM((PLANES, ROWS, 384), jnp.bfloat16),
            pltpu.VMEM((LINE, CACHE_HERE, 256), jnp.bfloat16),
            pltpu.VMEM((LINE, ROWS, 256), jnp.bfloat16),
            pltpu.VMEM((CACHE_HERE, 256), jnp.bfloat16),
            pltpu.VMEM((ROWS, 256), jnp.bfloat16),
            pltpu.VMEM((PLANES, KV_HERE, GROUP * ROWS, 128), jnp.bfloat16),
            state,
            state,
            pltpu.VMEM((PLANES, ROWS, 512), jnp.bfloat16),
            pltpu.VMEM((PLANES, ROWS, 512), jnp.bfloat16),
        ]
        + [pltpu.SemaphoreType.DMA((n,)) for n in (4, 4, 8, 8, 8, 8, 4, 4)],
        compiler_params=pltpu.CompilerParams(
            vmem_limit_bytes=48 * 1024 * 1024, collective_id=1, has_side_effects=True
        ),
        name="attend",
    )(queries, cache_rows, new_rows)


def experts_kernel(
    att_ref, ow_ref, hid_ref, gain_ref, chosen_ref, mix_ref, win_ref, wout_ref, out_ref,
    product, sum_send, sum_recv, residual, moe_in, rows_send, rows_recv, made, rows_back, total,
    sum_out, sum_in, go_out, go_in, back_out, back_in,
):
    seq_index = lax.axis_index("seq")
    exp_index = lax.axis_index("exp")
    plane = seq_index // LINE
    place = seq_index % LINE
    MESH = pl.DeviceIdType.MESH

    def ahead(k, j):
        return lax.rem(plane + k, PLANES) * LINE + lax.rem(place + j, LINE)

    def behind(k, j):
        return lax.rem(plane + PLANES - k, PLANES) * LINE + lax.rem(place + LINE - j, LINE)

    def side(k):
        return lax.rem(exp_index + k, 4)

    def sum_copy(k):
        return pltpu.make_async_remote_copy(
            src_ref=sum_send.at[k], dst_ref=sum_recv.at[k], send_sem=sum_out.at[k], recv_sem=sum_in.at[k],
            device_id={"exp": side(k)}, device_id_type=MESH,
        )

    def go_copy(k, j):
        to = ahead(k, j)
        return pltpu.make_async_remote_copy(
            src_ref=rows_send.at[to], dst_ref=rows_recv.at[seq_index],
            send_sem=go_out.at[k * LINE + j], recv_sem=go_in.at[k * LINE + j],
            device_id={"seq": to}, device_id_type=MESH,
        )

    def back_copy(k, j):
        to = behind(k, j)
        return pltpu.make_async_remote_copy(
            src_ref=made.at[to], dst_ref=rows_back.at[seq_index],
            send_sem=back_out.at[k * LINE + j], recv_sem=back_in.at[k * LINE + j],
            device_id={"seq": to}, device_id_type=MESH,
        )

    barrier = pltpu.get_barrier_semaphore()
    for k in range(1, 4):
        pl.semaphore_signal(barrier, inc=1, device_id={"exp": side(k)}, device_id_type=MESH)

    @pl.loop(1, EXPERTS)
    def _(n):
        pl.semaphore_signal(
            barrier, inc=1, device_id={"seq": ahead(n // LINE, n % LINE)}, device_id_type=MESH
        )

    product[...] = jnp.dot(att_ref[...], ow_ref[...], preferred_element_type=jnp.float32).reshape(product.shape)
    for k in range(1, 4):
        sum_send[k] = product[side(k)].astype(jnp.bfloat16)
    pl.semaphore_wait(barrier, 3 + EXPERTS - 1)
    for k in range(1, 4):
        sum_copy(k).start()
    mixed = product[exp_index]
    for k in range(1, 4):
        sum_copy(k).wait_recv()
        mixed = mixed + sum_recv[k].astype(jnp.float32)
    rows = pl.ds(pl.multiple_of(exp_index * 64, 64), 64)
    after = hid_ref[rows, :].astype(jnp.float32) + residual_scale * mixed
    residual[...] = after
    spread = lax.rsqrt(jnp.mean(after * after, axis=-1, keepdims=True) + norm_epsilon)
    moe_in[...] = (after * spread * gain_ref[...]).astype(jnp.bfloat16)

    @pl.loop(0, PLANES)
    def _(k):
        to = lax.rem(plane + k, PLANES)
        pick = chosen_ref[pl.ds(pl.multiple_of(to * 256, 256), 256), :]
        picked = jnp.dot(pick, moe_in[...], preferred_element_type=jnp.float32).astype(jnp.bfloat16)
        rows_send[pl.ds(to * LINE, LINE)] = picked.reshape(LINE, CAP, -1)

        @pl.loop(jnp.where(k == 0, 1, 0), LINE)
        def _(j):
            go_copy(k, j).start()

        @pl.when(k == 0)
        def _():
            rows_recv[seq_index] = rows_send[seq_index]

    @pl.loop(0, PLANES)
    def _(k):
        first = jnp.where(k == 0, 1, 0)
        origin = lax.rem(plane + PLANES - k, PLANES)

        @pl.loop(first, LINE)
        def _(j):
            go_copy(k, j).wait_recv()

        arrived = rows_recv[pl.ds(origin * LINE, LINE)].reshape(LINE * CAP, -1)
        hidden = jnp.dot(arrived, win_ref[...], preferred_element_type=jnp.float32)
        gate, up = hidden[:, :512], hidden[:, 512:]
        active = (gate / (1.0 + jnp.exp(-gate)) * up).astype(jnp.bfloat16)
        done = jnp.dot(active, wout_ref[...], preferred_element_type=jnp.float32).astype(jnp.bfloat16)
        made[pl.ds(origin * LINE, LINE)] = done.reshape(LINE, CAP, -1)

        @pl.loop(first, LINE)
        def _(j):
            back_copy(k, j).start()

        @pl.when(k == 0)
        def _():
            rows_back[seq_index] = made[seq_index]

    total[...] = jnp.zeros_like(total)

    @pl.loop(0, PLANES)
    def _(k):
        @pl.loop(jnp.where(k == 0, 1, 0), LINE)
        def _(j):
            back_copy(k, j).wait_recv()

        owner = lax.rem(plane + k, PLANES)
        mix = mix_ref[:, pl.ds(pl.multiple_of(owner * 256, 256), 256)]
        total[...] += jnp.dot(
            mix, rows_back[pl.ds(owner * LINE, LINE)].reshape(LINE * CAP, -1), preferred_element_type=jnp.float32
        )

    out_ref[...] = (residual[...] + residual_scale * (total[:64] + total[64:])).astype(jnp.bfloat16)

    for k in range(1, 4):
        sum_copy(k).wait_send()

    @pl.loop(1, EXPERTS)
    def _(n):
        go_copy(n // LINE, n % LINE).wait_send()
        back_copy(n // LINE, n % LINE).wait_send()


def experts(*operands):
    vmem = pl.BlockSpec(memory_space=pltpu.VMEM)
    width = 1536
    block = pltpu.VMEM((EXPERTS, CAP, width), jnp.bfloat16)
    return pl.pallas_call(
        experts_kernel,
        out_shape=jax.ShapeDtypeStruct((64, width), jnp.bfloat16),
        in_specs=[vmem] * 8,
        out_specs=vmem,
        scratch_shapes=[
            pltpu.VMEM((4, 64, width), jnp.float32),
            pltpu.VMEM((4, 64, width), jnp.bfloat16),
            pltpu.VMEM((4, 64, width), jnp.bfloat16),
            pltpu.VMEM((64, width), jnp.float32),
            pltpu.VMEM((64, width), jnp.bfloat16),
            block,
            block,
            block,
            block,
            pltpu.VMEM((128, width), jnp.float32),
        ]
        + [pltpu.SemaphoreType.DMA((n,)) for n in (4, 4, 32, 32, 32, 32)],
        compiler_params=pltpu.CompilerParams(
            vmem_limit_bytes=48 * 1024 * 1024, collective_id=2, has_side_effects=True
        ),
        name="experts",
    )(*operands)


def pages(pairs_new, page_slot, seq_index):
    seq_count = 32
    blocks_here = ROWS // PAGE
    outgoing = pairs_new.reshape(seq_count, PAGE * 256)
    received = lax.all_to_all(outgoing, "seq", split_axis=0, concat_axis=0, tiled=True)
    slots = lax.dynamic_index_in_dim(page_slot.reshape(seq_count, seq_count), seq_index, 1, keepdims=False)
    place = (slots[None, :] == jnp.arange(blocks_here, dtype=jnp.int32)[:, None]).astype(jnp.bfloat16)
    placed = jnp.dot(place, received, preferred_element_type=jnp.float32).astype(jnp.bfloat16)
    page_rows = placed.reshape(blocks_here, PAGE, KV_HERE, 2, HEAD_DIM).transpose(0, 2, 3, 1, 4)
    return page_rows.reshape(blocks_here, KV_HERE, 2, PAGE * HEAD_DIM)


def body(
    hidden_in,
    attn_gain,
    q_weight,
    k_weight,
    v_weight,
    o_weight,
    cache_kv,
    moe_gain,
    expert_in,
    expert_out,
    routes,
    route_prob,
    page_slot,
):
    seq_index = lax.axis_index("seq")
    normed = rms_norm(hidden_in, attn_gain)
    pair_weight = jnp.concatenate(
        [k_weight[:, :64], v_weight[:, :64], k_weight[:, 64:], v_weight[:, 64:]], axis=1
    )
    pairs_new = jnp.dot(normed, pair_weight, preferred_element_type=jnp.float32).astype(jnp.bfloat16)
    queries = jnp.dot(normed, q_weight, preferred_element_type=jnp.float32).astype(jnp.bfloat16)
    attended = attend(queries, cache_kv, pairs_new)
    page_rows = pages(pairs_new, page_slot, seq_index)

    moe_rows = routes.shape[0]
    named = (routes[:, :, None] == jnp.arange(EXPERTS, dtype=jnp.int32)).astype(jnp.float32)
    hit = jnp.sum(named, axis=1)
    share = route_prob / jnp.sum(route_prob, axis=-1, keepdims=True)
    share_of = jnp.sum(named * share[..., None], axis=1)
    before = jnp.tril(jnp.ones((moe_rows, moe_rows), jnp.bfloat16), -1)
    rank = jnp.dot(before, hit.astype(jnp.bfloat16), preferred_element_type=jnp.float32)
    slot = jnp.arange(CAP, dtype=jnp.float32)
    chosen = jnp.where(hit[..., None] > 0, (rank[..., None] == slot).astype(jnp.float32), 0.0)
    chosen = chosen.reshape(moe_rows, EXPERTS * CAP)
    mixing = chosen * jnp.repeat(share_of, CAP, axis=1)
    high = mixing.astype(jnp.bfloat16)
    low = (mixing - high.astype(jnp.float32)).astype(jnp.bfloat16)
    hidden_out = experts(
        attended,
        o_weight,
        hidden_in,
        moe_gain[None, :],
        chosen.astype(jnp.bfloat16).T,
        jnp.concatenate([high, low], axis=0),
        expert_in[0],
        expert_out[0],
    )
    return (hidden_out, page_rows)


def solution(mesh):
    return jax.shard_map(
        body,
        mesh=mesh,
        in_specs=(
            P("seq", None),
            P(),
            P(None, "exp"),
            P(None, "exp"),
            P(None, "exp"),
            P("exp", None),
            P("seq", "exp"),
            P(),
            P("seq", None, None),
            P("seq", None, None),
            P(("seq", "exp"), None),
            P(("seq", "exp"), None),
            P(),
        ),
        out_specs=(P(("seq", "exp"), None), P("seq", "exp", None, None)),
        check_vma=False,
    )
```

time: 383 us -> 250 us (0.65)
  the two profiles are of different devices: /device:TPU:0 before, /device:TPU:25 now
where the time goes in v2:
time: 250 us; the launch traced here: 249 us
  Pallas kernels  212 us (85%)
  local copies, waits for them, and re-layouts  15.4 us (6%)
  starting transfers between devices  10.5 us (4%)
  other arithmetic  7.55 us (3%)
  matrix products  2.53 us (1%)
    pallas_call x1, Pallas kernels, experts(): pl.pallas_call(experts_kernel, out_shape=jax.ShapeDtypeStruct((64, width)...  130 us
    pallas_call x1, Pallas kernels, attend(): pl.pallas_call(attend_kernel, out_shape=jax.ShapeDtypeStruct((ROWS, 384),...  82.4 us
    all_to_all x1, starting transfers between devices, pages(): lax.all_to_all(outgoing, 'seq', split_axis=0, concat_axis=0, tiled=True)  10.5 us
    unnamed x35, local copies, waits for them, and re-layouts  7.23 us
  transfers between devices with their start and end apart: 1, of which 0 were waited for; matrix products, arithmetic and copies ran while one was open for 4% of the time, Pallas kernels for 85%

profile of v2, /device:TPU:25, one launch (start us, length us, event | category | flops | bytes accessed | tf_op | source)
XLA Modules:
  0.0 249.2 jit_solution(6572720289051738290)
XLA Ops:
  0.6 0.0 copy-start
  0.6 1.5 fusion
  2.1 1.7 fusion.29
  3.9 0.8 convolution_convert_fusion.2.new_ref
  4.8 0.5 broadcast.34
  5.3 1.4 reduce.2
  6.7 0.7 reshape.48
  7.4 10.5 %all-to-all-start = ((bf16[32,2,1024]{2,1,0:T(2,128)(2,1)}), bf16[32,2,1024]{2,1,0:T(2,128)(2,1)}, u32[]{:S(2)}, u32[]{:S(2)}) async-start(bf16[32,2,1024]{2,1,0:T(2,128)(2,1)} %reshape.48), calls=%async_computation | async-start | bytes 262144 | tf_op jit(solution)/shard_map/all_to_all | solution.py:452
  18.0 1.3 convolution_convert_fusion.1.q_ref
  19.4 0.9 copy.52
  20.3 0.8 copy.51
  21.2 0.2 fusion.19
  21.4 0.9 copy.50
  22.3 0.1 eq.54
  22.4 1.9 fusion.14
  24.3 1.7 subtract_convert_fusion
  26.0 1.7 copy.53.chosen_ref
  27.8 0.9 copy-done.8
  28.7 0.9 copy-done.9
  29.6 0.9 copy-done.10
  30.6 82.4 %attend.1.att_ref = bf16[256,384]{1,0:T(8,128)(2,1)S(1)} custom-call(bf16[256,384]{1,0:T(8,128)(2,1)S(1)} %copy-done.10, bf16[512,256]{1,0:T(8,128)(2,1)S(1)} %copy-done.9, bf16[256,256]{1,0:T(8,128)(2,1)S(1)} %copy-done.8), custom_call_target="tpu_custom_call" | custom-call | tf_op jit(solution)/shard_map/attend/pallas_call | solution.py:262
  113.0 1.0 pad_maximum_fusion.mix_ref
  114.0 0.9 copy-done.4
  114.9 129.9 %experts.1 = bf16[64,1536]{1,0:T(8,128)(2,1)S(1)} custom-call(bf16[256,384]{1,0:T(8,128)(2,1)S(1)} %attend.1.att_ref, bf16[384,1536]{1,0:T(8,128)(2,1)S(1)} %copy-done.3, bf16[256,1536]{1,0:T(8,128)(2,1)S(1)} %copy-done.1, f32[1,1536]{1,0:T(1,128)S(1)} %broadcast_in_dim.38.gain_ref, bf16[1024,64]{1,0:T(8,128)(2,1)S(1)} %copy-done.4, ...), custom_call_target="tpu_custom_call" | custom-call | tf_op jit(solution)/shard_map/experts/pallas_call | solution.py:423
  244.9 0.7 copy-done.5
  245.6 0.1 reshape.44
  245.6 0.2 dynamic-slice_reduce_fusion
  245.8 1.4 reshape.49
  247.2 0.2 convolution_convert_fusion
  247.4 0.2 reshape.45
  247.7 0.8 reshape.46
  248.6 0.7 copy.62
  (40 shorter events, 0.4 us)
Async XLA Ops:
  0.6 17.3 %copy-start = (bf16[1536,384]{1,0:T(8,128)(2,1)S(1)}, bf16[1536,384]{1,0:T(8,128)(2,1)}, u32[]{:S(2)}) copy-start(bf16[1536,384]{1,0:T(8,128)(2,1)} %param.15) | copy-start | bytes 3538948
  2.1 1.7 copy-start.1
  2.1 1.7 copy-start.15
  4.7 14.6 %copy-start.7 = (bf16[256,256]{1,0:T(8,128)(2,1)}, bf16[256,256]{1,0:T(8,128)(2,1)S(1)}, u32[]{:S(2)}) copy-start(bf16[256,256]{1,0:T(8,128)(2,1)S(1)} %convolution_convert_fusion.2.new_ref) | copy-start | bytes 393220
  7.4 11.9 %copy-start.11 = (f32[64,8]{0,1:T(8,128)S(1)}, f32[64,8]{0,1:T(8,128)}, u32[]{:S(2)}) copy-start(f32[64,8]{0,1:T(8,128)} %param.24) | copy-start | bytes 6148
  7.4 11.9 %copy-start.13 = (s32[64,8]{0,1:T(8,128)S(1)}, s32[64,8]{0,1:T(8,128)}, u32[]{:S(2)}) copy-start(s32[64,8]{0,1:T(8,128)} %param.23) | copy-start | bytes 6148
  7.4 238.4 %all-to-all-start = ((bf16[32,2,1024]{2,1,0:T(2,128)(2,1)}), bf16[32,2,1024]{2,1,0:T(2,128)(2,1)}, u32[]{:S(2)}, u32[]{:S(2)}) async-start(bf16[32,2,1024]{2,1,0:T(2,128)(2,1)} %reshape.48), calls=%async_computation | async-start | bytes 262144 | tf_op jit(solution)/shard_map/all_to_all | solution.py:452
  20.3 5.7 %copy-start.12 = (f32[1536]{0:T(1024)S(1)}, f32[1536]{0:T(1024)}, u32[]{:S(2)}) copy-start(f32[1536]{0:T(1024)} %param.20) | copy-start | bytes 18436
  22.4 91.6 %copy-start.2 = (bf16[1,512,1536]{2,1,0:T(8,128)(2,1)S(1)}, bf16[1,512,1536]{2,1,0:T(8,128)(2,1)}, u32[]{:S(2)}) copy-start(bf16[1,512,1536]{2,1,0:T(8,128)(2,1)} %param.22) | copy-start | bytes 4718596
  27.8 0.9 copy-start.8
  28.7 0.9 copy-start.9
  29.6 0.9 copy-start.10
  30.6 83.4 %copy-start.3 = (bf16[384,1536]{1,0:T(8,128)(2,1)S(1)}, bf16[384,1536]{1,0:T(8,128)(2,1)}, u32[]{:S(2)}) copy-start(bf16[384,1536]{1,0:T(8,128)(2,1)} %ow_ref.1) | copy-start | bytes 3538948
  114.0 1.0 copy-start.4
  114.9 130.6 %copy-start.14 = (s32[1024]{0:T(1024)S(1)}, s32[1024]{0:T(1024)}, u32[]{:S(2)}) copy-start(s32[1024]{0:T(1024)} %param.25) | copy-start | bytes 12292
  244.9 0.7 copy-start.5
  245.6 2.9 %copy-start.6 = (bf16[64,1536]{1,0:T(8,128)(2,1)S(1)}, bf16[64,1536]{1,0:T(8,128)(2,1)}, u32[]{:S(2)}) copy-start(bf16[64,1536]{1,0:T(8,128)(2,1)} %copy-done.5) | copy-start | bytes 589828

commit v3 on v2

--- a/solution.py
+++ b/solution.py
@@ -25,21 +25,20 @@
 masked_score = -1e30
 
 
-def rms_norm(values, gain_row):
-    widened = values.astype(jnp.float32)
-    spread = lax.rsqrt(jnp.mean(widened * widened, axis=-1, keepdims=True) + norm_epsilon)
-    return (widened * spread * gain_row).astype(jnp.bfloat16)
+NEAR = ((0, 0), (0, 1), (1, 0), (0, 3), (1, 1), (0, 2), (1, 3), (1, 2))
 
 
 def attend_kernel(
-    q_ref, cache_ref, new_ref, out_ref,
-    q_all, cache_all, new_all, cache_val, new_val, qs, best, acc, part_send, part_recv,
-    q_out, q_in, cache_out, cache_in, new_out, new_in, part_out, part_in,
+    hid_ref, gain_ref, qw_ref, kw_ref, vw_ref, cache_ref, slot_ref, out_ref, page_ref,
+    normed, query, q_all, cache_all, new_own, new_all, cache_val, new_val, qs, best, acc,
+    part_send, part_recv, page_send, page_recv,
+    q_out, q_in, cache_out, cache_in, new_out, new_in, part_out, part_in, page_out, page_in,
 ):
     seq_index = lax.axis_index("seq")
     plane = seq_index // LINE
     place = seq_index % LINE
     even = plane % 2 == 0
+    MESH = pl.DeviceIdType.MESH
     lane = lax.broadcasted_iota(jnp.int32, (ROWS, 2 * HEAD_DIM), 1)
     low = lane < HEAD_DIM
     one = jnp.ones((), jnp.bfloat16)
@@ -47,28 +46,35 @@
     def send(source, target, out_sem, in_sem, to):
         return pltpu.make_async_remote_copy(
             src_ref=source, dst_ref=target, send_sem=out_sem, recv_sem=in_sem,
-            device_id={"seq": to}, device_id_type=pl.DeviceIdType.MESH,
-        )
-
-    def peer(j):
-        return plane * LINE + lax.rem(place + j, LINE)
+            device_id={"seq": to}, device_id_type=MESH,
+        )
+
+    def peer(n):
+        h, x = NEAR[n]
+        return plane * LINE + lax.rem(place // 4 + h, 2) * 4 + lax.rem(place % 4 + x, 4)
 
     def line_peer(k):
         return lax.rem(plane + k, PLANES) * LINE + place
 
-    def cache_copy(j):
-        return send(cache_ref, cache_all.at[j], cache_out.at[j], cache_in.at[j], peer(j))
-
-    def new_copy(j):
-        return send(new_ref, new_all.at[j], new_out.at[j], new_in.at[j], peer(j))
+    def ahead(n):
+        return lax.rem(seq_index + n, 32)
+
+    def cache_copy(n):
+        rows = pl.ds((n % 2) * CACHE_HERE, CACHE_HERE)
+        return send(cache_ref, cache_all.at[n // 2, rows], cache_out.at[n], cache_in.at[n], peer(n))
+
+    def new_copy(n):
+        return send(new_own, new_all.at[place], new_out.at[n], new_in.at[n], peer(n))
 
     def query_copy(k):
-        return send(q_ref, q_all.at[plane], q_out.at[k], q_in.at[k], line_peer(k))
+        return send(query, q_all.at[plane], q_out.at[k], q_in.at[k], line_peer(k))
 
     def part_copy(k):
-        return send(
-            part_send.at[k], part_recv.at[k], part_out.at[k], part_in.at[k], line_peer(k)
-        )
+        return send(part_send.at[k], part_recv.at[k], part_out.at[k], part_in.at[k], line_peer(k))
+
+    def page_copy(n):
+        rows = pl.ds(pl.multiple_of(ahead(n) * PAGE, PAGE), PAGE)
+        return send(page_send.at[rows], page_recv.at[seq_index], page_out.at[n], page_in.at[n], ahead(n))
 
     def sends_query(k):
         return jnp.logical_or(plane < 2, plane == 3) if k == 3 else plane < 2
@@ -86,37 +92,58 @@
 
     barrier = pltpu.get_barrier_semaphore()
 
-    @pl.loop(1, LINE)
-    def _(j):
-        pl.semaphore_signal(barrier, inc=1, device_id={"seq": peer(j)}, device_id_type=pl.DeviceIdType.MESH)
-
-    for k in range(1, PLANES):
-        pl.semaphore_signal(
-            barrier, inc=1, device_id={"seq": line_peer(k)}, device_id_type=pl.DeviceIdType.MESH
-        )
-
-    q_all[plane] = q_ref[...]
-    cache_all[0] = cache_ref[...]
-    new_all[0] = new_ref[...]
+    @pl.loop(1, 32)
+    def _(n):
+        pl.semaphore_signal(barrier, inc=1, device_id={"seq": ahead(n)}, device_id_type=MESH)
+
+    cache_all[0, :CACHE_HERE] = cache_ref[...]
+    for k in range(1, PLANES):
+        @pl.when(jnp.logical_not(gets_part(k)))
+        def _():
+            part_recv[k, :, :384] = jnp.zeros((ROWS, 384), jnp.bfloat16)
+            part_recv[k, :, 384:] = jnp.full((ROWS, 128), masked_score, jnp.bfloat16)
+
+    pl.semaphore_wait(barrier, 31)
+    for n in range(1, 4):
+        cache_copy(n).start()
+
+    @pl.loop(0, ROWS // 64)
+    def _(step):
+        rows = pl.ds(pl.multiple_of(step * 64, 64), 64)
+        wide = hid_ref[rows, :].astype(jnp.float32)
+        spread = lax.rsqrt(jnp.mean(wide * wide, axis=-1, keepdims=True) + norm_epsilon)
+        normed[rows, :] = (wide * spread * gain_ref[...]).astype(jnp.bfloat16)
+
+    query[...] = jnp.dot(normed[...], qw_ref[...], preferred_element_type=jnp.float32).astype(jnp.bfloat16)
+    for k in range(1, PLANES):
+        @pl.when(sends_query(k))
+        def _():
+            query_copy(k).start()
+
+    keys = jnp.dot(normed[...], kw_ref[...], preferred_element_type=jnp.float32)
+    values = jnp.dot(normed[...], vw_ref[...], preferred_element_type=jnp.float32)
+    slabs = [
+        jnp.where(low, keys, pltpu.roll(values, HEAD_DIM, 1)).astype(jnp.bfloat16),
+        jnp.where(low, pltpu.roll(keys, HEAD_DIM, 1), values).astype(jnp.bfloat16),
+    ]
+    for g in range(KV_HERE):
+        new_own[:, g * 128 : (g + 1) * 128] = slabs[g]
+        page_send[:, g * 128 : (g + 1) * 128] = slabs[g].astype(jnp.float32)
+    for n in range(1, LINE):
+        new_copy(n).start()
+    for n in range(4, LINE):
+        cache_copy(n).start()
+
+    @pl.loop(1, 32)
+    def _(n):
+        page_copy(n).start()
+
+    q_all[plane] = query[...]
+    new_all[place] = new_own[...]
+    own_rows = pl.ds(pl.multiple_of(seq_index * PAGE, PAGE), PAGE)
+    page_recv[seq_index] = page_send[own_rows, :]
     best[...] = jnp.full_like(best, masked_score)
     acc[...] = jnp.zeros_like(acc)
-    for k in range(1, PLANES):
-        @pl.when(jnp.logical_not(gets_part(k)))
-        def _():
-            part_recv[k, :, :384] = jnp.zeros((ROWS, 384), jnp.bfloat16)
-            part_recv[k, :, 384:] = jnp.full((ROWS, 128), masked_score, jnp.bfloat16)
-
-    pl.semaphore_wait(barrier, LINE - 1 + PLANES - 1)
-
-    for k in range(1, PLANES):
-        @pl.when(sends_query(k))
-        def _():
-            query_copy(k).start()
-
-    @pl.loop(1, LINE)
-    def _(j):
-        cache_copy(j).start()
-        new_copy(j).start()
 
     def prepare(t):
         for h in range(HEADS_HERE):
@@ -127,67 +154,86 @@
             a = h % GROUP
             qs[t, h // GROUP, a * ROWS : (a + 1) * ROWS, :] = jnp.where(low, slab, 0.0).astype(jnp.bfloat16)
 
-    def update(t, g, key_block, value_block, masked):
-        for a in range(GROUP):
-            rows = slice(a * ROWS, (a + 1) * ROWS)
-            scores = lax.dot_general(
-                qs[t, g, rows, :], key_block, (((1,), (1,)), ((), ())), preferred_element_type=jnp.float32
+    def slab_of(g):
+        return slice(g * 128, (g + 1) * 128)
+
+    def update(turns, keys_of, values_of, first_key=None):
+        chains = [(t, g, slice(a * ROWS, (a + 1) * ROWS)) for t in turns for g in range(KV_HERE) for a in range(GROUP)]
+        raw = [
+            lax.dot_general(
+                qs[t, g, rows, :], keys_of(g), (((1,), (1,)), ((), ())), preferred_element_type=jnp.float32
             )
-            if masked:
+            for t, g, rows in chains
+        ]
+        for (t, g, rows), scores in zip(chains, raw):
+            if first_key is not None:
                 r = lax.broadcasted_iota(jnp.int32, scores.shape, 0)
                 c = lax.broadcasted_iota(jnp.int32, scores.shape, 1)
-                scores = jnp.where(c <= r, scores, masked_score)
+                scores = jnp.where(c - r <= place * ROWS - first_key, scores, masked_score)
             old = best[t, g, rows, :]
             new = jnp.maximum(old, jnp.max(scores, axis=-1, keepdims=True))
             best[t, g, rows, :] = new
             weights = jnp.exp(scores - new[:, :1]).astype(jnp.bfloat16)
             acc[t, g, rows, :] = acc[t, g, rows, :] * jnp.exp(old - new) + jnp.dot(
-                weights, value_block, preferred_element_type=jnp.float32
+                weights, values_of(g), preferred_element_type=jnp.float32
             )
 
-    def slab_of(g):
-        return slice(g * 128, (g + 1) * 128)
-
-    def fill_new(j):
-        for g in range(KV_HERE):
-            new_val[:, slab_of(g)] = jnp.where(low, one, new_all[j, :, slab_of(g)])
-
     prepare(plane)
-    fill_new(0)
-    for g in range(KV_HERE):
-        update(plane, g, new_ref[:, slab_of(g)], new_val[:, slab_of(g)], True)
-
     for k in range(1, PLANES):
         @pl.when(gets_query(k))
         def _():
             query_copy(k).wait_recv()
             prepare(lax.rem(plane + PLANES - k, PLANES))
 
+    def cache_pair(m):
+        for part in range(4):
+            rows = slice(part * ROWS, (part + 1) * ROWS)
+            for g in range(KV_HERE):
+                cache_val[rows, slab_of(g)] = jnp.where(low, one, cache_all[m, rows, slab_of(g)])
+        update((0, 1), lambda g: cache_all[m, :, slab_of(g)], lambda g: cache_val[:, slab_of(g)])
+
+    def cache_pairs(start):
+        @pl.loop(start, start + 2)
+        def _(m):
+            @pl.when(m > 0)
+            def _():
+                send(
+                    cache_ref, cache_all.at[m, pl.ds(0, CACHE_HERE)],
+                    cache_out.at[2 * m], cache_in.at[2 * m], peer(1),
+                ).wait_recv()
+
+            send(
+                cache_ref, cache_all.at[m, pl.ds(CACHE_HERE, CACHE_HERE)],
+                cache_out.at[2 * m + 1], cache_in.at[2 * m + 1], peer(1),
+            ).wait_recv()
+            cache_pair(m)
+
+    cache_pairs(0)
+    for n in range(1, LINE):
+        h, x = NEAR[n]
+        origin = lax.rem(place // 4 + h, 2) * 4 + lax.rem(place % 4 + 4 - x, 4)
+        send(new_own, new_all.at[origin], new_out.at[n], new_in.at[n], peer(n)).wait_recv()
+
     @pl.loop(0, LINE)
-    def _(j):
-        @pl.when(j > 0)
-        def _():
-            cache_copy(j).wait_recv()
-            new_copy(j).wait_recv()
-
-        for half in range(CACHE_HERE // ROWS):
-            rows = slice(half * ROWS, (half + 1) * ROWS)
-            for g in range(KV_HERE):
-                cache_val[rows, slab_of(g)] = jnp.where(low, one, cache_all[j, rows, slab_of(g)])
-
-        @pl.loop(0, 2)
-        def _(t):
-            for g in range(KV_HERE):
-                update(t, g, cache_all[j, :, slab_of(g)], cache_val[:, slab_of(g)], False)
-
-        fill_new(j)
-        first = jnp.where(jnp.logical_and(j > 0, j <= place), 0, 1)
-        last = jnp.where(even, 2, 1)
-
-        @pl.loop(first, last)
-        def _(step):
-            for g in range(KV_HERE):
-                update(plane + step, g, new_all[j, :, slab_of(g)], new_val[:, slab_of(g)], False)
+    def _(n):
+        for g in range(KV_HERE):
+            new_val[n, :, slab_of(g)] = jnp.where(low, one, new_all[n, :, slab_of(g)])
+
+    def new_keys(step):
+        return lambda g: new_all[pl.ds(step * 4, 4), :, slab_of(g)].reshape(1024, 128)
+
+    def new_values(step):
+        return lambda g: new_val[pl.ds(step * 4, 4), :, slab_of(g)].reshape(1024, 128)
+
+    @pl.loop(0, place // 4 + 1)
+    def _(step):
+        update((plane,), new_keys(step), new_values(step), step * 1024)
+
+    @pl.loop(0, jnp.where(even, 2, 0))
+    def _(step):
+        update((plane + 1,), new_keys(step), new_values(step))
+
+    cache_pairs(2)
 
     def finish(t):
         heads = []
@@ -217,6 +263,30 @@
             part_send[k, :, 384:512] = split.astype(jnp.bfloat16)
             part_copy(k).start()
 
+    @pl.loop(1, 32)
+    def _(n):
+        page_copy(n).wait_recv()
+
+    column = lax.broadcasted_iota(jnp.int32, (32, 32), 1)
+    slots = jnp.sum(
+        jnp.where(column == seq_index, slot_ref[...].astype(jnp.float32), 0.0), axis=1, keepdims=True
+    )
+    owner = (slots == column.astype(jnp.float32)).astype(jnp.bfloat16)
+    low_page = lax.broadcasted_iota(jnp.int32, (32, 128), 1) < HEAD_DIM
+    tokens = [
+        lax.dot_general(
+            owner, page_recv[:, n, :].astype(jnp.bfloat16), (((0,), (0,)), ((), ())),
+            preferred_element_type=jnp.float32,
+        )
+        for n in range(PAGE)
+    ]
+    for g in range(KV_HERE):
+        for n in range(0, PAGE, 2):
+            first, second = tokens[n][:, slab_of(g)], tokens[n + 1][:, slab_of(g)]
+            cols = slice(n * HEAD_DIM, (n + 2) * HEAD_DIM)
+            page_ref[2 * g, :, cols] = jnp.where(low_page, first, pltpu.roll(second, HEAD_DIM, 1)).astype(jnp.bfloat16)
+            page_ref[2 * g + 1, :, cols] = jnp.where(low_page, pltpu.roll(first, HEAD_DIM, 1), second).astype(jnp.bfloat16)
+
     pairs, own_level = finish(plane)
     for k in range(1, PLANES):
         @pl.when(gets_part(k))
@@ -241,10 +311,9 @@
             value = value + part_recv[k, :, cols].astype(jnp.float32) * spread(shares[k], p)
         out_ref[:, cols] = value.astype(jnp.bfloat16)
 
-    @pl.loop(1, LINE)
-    def _(j):
-        cache_copy(j).wait_send()
-        new_copy(j).wait_send()
+    for n in range(1, LINE):
+        cache_copy(n).wait_send()
+        new_copy(n).wait_send()
 
     for k in range(1, PLANES):
         @pl.when(sends_query(k))
@@ -255,33 +324,45 @@
         def _():
             part_copy(k).wait_send()
 
-
-def attend(queries, cache_rows, new_rows):
+    @pl.loop(1, 32)
+    def _(n):
+        page_copy(n).wait_send()
+
+
+def attend(*operands):
     vmem = pl.BlockSpec(memory_space=pltpu.VMEM)
     state = pltpu.VMEM((PLANES, KV_HERE, GROUP * ROWS, 128), jnp.float32)
     return pl.pallas_call(
         attend_kernel,
-        out_shape=jax.ShapeDtypeStruct((ROWS, 384), jnp.bfloat16),
-        in_specs=[vmem] * 3,
-        out_specs=vmem,
+        out_shape=[
+            jax.ShapeDtypeStruct((ROWS, 384), jnp.bfloat16),
+            jax.ShapeDtypeStruct((2 * KV_HERE, ROWS // PAGE, PAGE * HEAD_DIM), jnp.bfloat16),
+        ],
+        in_specs=[vmem] * 7,
+        out_specs=[vmem] * 2,
         scratch_shapes=[
+            pltpu.VMEM((ROWS, 1536), jnp.bfloat16),
+            pltpu.VMEM((ROWS, 384), jnp.bfloat16),
             pltpu.VMEM((PLANES, ROWS, 384), jnp.bfloat16),
-            pltpu.VMEM((LINE, CACHE_HERE, 256), jnp.bfloat16),
+            pltpu.VMEM((LINE // 2, 2 * CACHE_HERE, 256), jnp.bfloat16),
+            pltpu.VMEM((ROWS, 256), jnp.bfloat16),
             pltpu.VMEM((LINE, ROWS, 256), jnp.bfloat16),
-            pltpu.VMEM((CACHE_HERE, 256), jnp.bfloat16),
-            pltpu.VMEM((ROWS, 256), jnp.bfloat16),
+            pltpu.VMEM((2 * CACHE_HERE, 256), jnp.bfloat16),
+            pltpu.VMEM((LINE, ROWS, 256), jnp.bfloat16),
             pltpu.VMEM((PLANES, KV_HERE, GROUP * ROWS, 128), jnp.bfloat16),
             state,
             state,
             pltpu.VMEM((PLANES, ROWS, 512), jnp.bfloat16),
             pltpu.VMEM((PLANES, ROWS, 512), jnp.bfloat16),
+            pltpu.VMEM((ROWS, 256), jnp.float32),
+            pltpu.VMEM((ROWS // PAGE, PAGE, 256), jnp.float32),
         ]
-        + [pltpu.SemaphoreType.DMA((n,)) for n in (4, 4, 8, 8, 8, 8, 4, 4)],
+        + [pltpu.SemaphoreType.DMA((n,)) for n in (4, 4, 8, 8, 8, 8, 4, 4, 32, 32)],
         compiler_params=pltpu.CompilerParams(
-            vmem_limit_bytes=48 * 1024 * 1024, collective_id=1, has_side_effects=True
+            vmem_limit_bytes=52 * 1024 * 1024, collective_id=1, has_side_effects=True
         ),
         name="attend",
-    )(queries, cache_rows, new_rows)
+    )(*operands)
 
 
 def experts_kernel(
@@ -445,18 +526,6 @@
     )(*operands)
 
 
-def pages(pairs_new, page_slot, seq_index):
-    seq_count = 32
-    blocks_here = ROWS // PAGE
-    outgoing = pairs_new.reshape(seq_count, PAGE * 256)
-    received = lax.all_to_all(outgoing, "seq", split_axis=0, concat_axis=0, tiled=True)
-    slots = lax.dynamic_index_in_dim(page_slot.reshape(seq_count, seq_count), seq_index, 1, keepdims=False)
-    place = (slots[None, :] == jnp.arange(blocks_here, dtype=jnp.int32)[:, None]).astype(jnp.bfloat16)
-    placed = jnp.dot(place, received, preferred_element_type=jnp.float32).astype(jnp.bfloat16)
-    page_rows = placed.reshape(blocks_here, PAGE, KV_HERE, 2, HEAD_DIM).transpose(0, 2, 3, 1, 4)
-    return page_rows.reshape(blocks_here, KV_HERE, 2, PAGE * HEAD_DIM)
-
-
 def body(
     hidden_in,
     attn_gain,
@@ -472,15 +541,10 @@
     route_prob,
     page_slot,
 ):
-    seq_index = lax.axis_index("seq")
-    normed = rms_norm(hidden_in, attn_gain)
-    pair_weight = jnp.concatenate(
-        [k_weight[:, :64], v_weight[:, :64], k_weight[:, 64:], v_weight[:, 64:]], axis=1
+    attended, page_slabs = attend(
+        hidden_in, attn_gain[None, :], q_weight, k_weight, v_weight, cache_kv, page_slot.reshape(32, 32)
     )
-    pairs_new = jnp.dot(normed, pair_weight, preferred_element_type=jnp.float32).astype(jnp.bfloat16)
-    queries = jnp.dot(normed, q_weight, preferred_element_type=jnp.float32).astype(jnp.bfloat16)
-    attended = attend(queries, cache_kv, pairs_new)
-    page_rows = pages(pairs_new, page_slot, seq_index)
+    page_rows = page_slabs.transpose(1, 0, 2).reshape(ROWS // PAGE, KV_HERE, 2, PAGE * HEAD_DIM)
 
     moe_rows = routes.shape[0]
     named = (routes[:, :, None] == jnp.arange(EXPERTS, dtype=jnp.int32)).astype(jnp.float32)

time: 250 us -> 201 us (0.80)
  the two profiles are of different devices: /device:TPU:25 before, /device:TPU:59 now
where the time goes in v3:
time: 201 us; the launch traced here: 200 us
  Pallas kernels  188 us (94%)
  local copies, waits for them, and re-layouts  8.63 us (4%)
  other arithmetic  3.02 us (2%)
    pallas_call x1, Pallas kernels, experts(): pl.pallas_call(experts_kernel, out_shape=jax.ShapeDtypeStruct((64, width)...  128 us
    pallas_call x1, Pallas kernels, attend(): pl.pallas_call(attend_kernel, out_shape=[jax.ShapeDtypeStruct((ROWS, 384)...  59.1 us
    unnamed x20, local copies, waits for them, and re-layouts  5.37 us

profile of v3, /device:TPU:59, one launch (start us, length us, event | category | flops | bytes accessed | tf_op | source)
XLA Modules:
  0.0 200.2 jit_solution(8380162751499559284)
XLA Ops:
  0.6 0.7 reduce_sum.28
  1.3 0.7 broadcast_divide_fusion
  2.0 0.7 select_reduce_fusion
  2.8 0.2 copy.28
  3.0 0.2 fusion.5
  3.3 0.2 copy.27
  3.5 0.2 copy.29
  3.7 0.1 eq.39
  3.8 0.1 fusion.2
  3.9 0.1 subtract_convert_fusion
  4.0 0.0 copy-start.2
  4.0 0.7 pad_maximum_fusion.mix_ref
  4.7 0.8 copy.30.chosen_ref
  5.5 0.0 copy-start
  5.5 0.0 copy-start.1
  5.5 0.9 reshape.25.slot_ref
  6.4 0.0 copy-start.3
  6.4 0.7 broadcast_in_dim.37.gain_ref
  7.2 1.0 copy-done.5
  8.2 1.0 copy-done.6
  9.2 0.9 copy-done.7
  10.1 59.1 %attend.1 = (bf16[256,384]{1,0:T(8,128)(2,1)S(1)}, bf16[4,32,512]{2,1,0:T(8,128)(2,1)S(1)}) custom-call(bf16[256,1536]{1,0:T(8,128)(2,1)} %hid_ref.3, f32[1,1536]{1,0:T(1,128)S(1)} %broadcast_in_dim.37.gain_ref, bf16[1536,384]{1,0:T(8,128)(2,1)} %qw_ref.1, bf16[1536,128]{1,0:T(8,128)(2,1)S(1)} %copy-done.5, bf16[1536,128]{1,0:T(8,128)(2,1)S(1)} %copy-done.6, ...), custom_call_target="tpu_custom_call" | custom-call | tf_op jit(solution)/shard_map/attend/pallas_call | solution.py:335
  69.3 0.0 copy-done.8
  69.3 0.0 copy-done.2
  69.3 0.0 copy-done
  69.3 0.0 copy-done.1
  69.3 0.0 copy-done.3
  69.3 0.0 copy-start.4
  69.3 0.9 copy-done.4
  70.3 128.4 %experts.1 = bf16[64,1536]{1,0:T(8,128)(2,1)S(1)} custom-call(bf16[256,384]{1,0:T(8,128)(2,1)S(1)} %get-tuple-element.4.att_ref, bf16[384,1536]{1,0:T(8,128)(2,1)S(1)} %copy-done.2, bf16[256,1536]{1,0:T(8,128)(2,1)S(1)} %copy-done, f32[1,1536]{1,0:T(1,128)S(1)} %broadcast_in_dim.38.gain_ref, bf16[1024,64]{1,0:T(8,128)(2,1)S(1)} %copy-done.4, ...), custom_call_target="tpu_custom_call" | custom-call | tf_op jit(solution)/shard_map/experts/pallas_call | solution.py:504
  198.7 0.8 copy.31
  199.5 0.7 copy.33
  (11 shorter events, 0.2 us)
Async XLA Ops:
  4.0 65.3 %copy-start.2 = (bf16[384,1536]{1,0:T(8,128)(2,1)S(1)}, bf16[384,1536]{1,0:T(8,128)(2,1)}, u32[]{:S(2)}) copy-start(bf16[384,1536]{1,0:T(8,128)(2,1)} %ow_ref.1) | copy-start | bytes 3538948
  5.5 63.8 %copy-start = (bf16[256,1536]{1,0:T(8,128)(2,1)S(1)}, bf16[256,1536]{1,0:T(8,128)(2,1)}, u32[]{:S(2)}) copy-start(bf16[256,1536]{1,0:T(8,128)(2,1)} %hid_ref.3) | copy-start | bytes 2359300
  5.5 63.8 %copy-start.1 = (bf16[1,512,1536]{2,1,0:T(8,128)(2,1)S(1)}, bf16[1,512,1536]{2,1,0:T(8,128)(2,1)}, u32[]{:S(2)}) copy-start(bf16[1,512,1536]{2,1,0:T(8,128)(2,1)} %param.22) | copy-start | bytes 4718596
  6.4 62.9 %copy-start.3 = (bf16[128,1024]{1,0:T(8,128)(2,1)S(1)}, bf16[128,1024]{1,0:T(8,128)(2,1)}, u32[]{:S(2)}) copy-start(bf16[128,1024]{1,0:T(8,128)(2,1)} %pad_maximum_fusion.mix_ref) | copy-start | bytes 786436
  7.2 1.0 copy-start.5
  8.2 1.0 copy-start.6
  9.2 0.9 copy-start.7
  10.1 59.1 %copy-start.8 = (f32[1536]{0:T(1024)S(1)}, f32[1536]{0:T(1024)}, u32[]{:S(2)}) copy-start(f32[1536]{0:T(1024)} %param.20) | copy-start | bytes 18436
  69.3 1.0 copy-start.4

commit v4 on v3

--- a/solution.py
+++ b/solution.py
@@ -365,22 +365,29 @@
     )(*operands)
 
 
+HALF = 768
+
+
 def experts_kernel(
-    att_ref, ow_ref, hid_ref, gain_ref, chosen_ref, mix_ref, win_ref, wout_ref, out_ref,
-    product, sum_send, sum_recv, residual, moe_in, rows_send, rows_recv, made, rows_back, total,
-    sum_out, sum_in, go_out, go_in, back_out, back_in,
+    att_ref, ow_ref, hid_ref, gain_ref, routes_ref, prob_ref, win_ref, wout_ref, out_ref,
+    product, sum_send, sum_recv, residual, info_a, info_b, got_a, got_b, send_a, send_b, recv_a, recv_b,
+    made_a, made_b, back_a, back_b, part_a, part_b, red_a, red_b, acc_a, acc_b, last_send, last_recv,
+    sum_out, sum_in, info_out, info_in, y_out, y_in, wide_out, wide_in, go_out, go_in,
+    ret_out, ret_in, red_out, red_in, last_out, last_in,
 ):
     seq_index = lax.axis_index("seq")
     exp_index = lax.axis_index("exp")
-    plane = seq_index // LINE
-    place = seq_index % LINE
+    z, h, x = seq_index // 8, lax.rem(seq_index // 4, 2), lax.rem(seq_index, 4)
     MESH = pl.DeviceIdType.MESH
 
-    def ahead(k, j):
-        return lax.rem(plane + k, PLANES) * LINE + lax.rem(place + j, LINE)
-
-    def behind(k, j):
-        return lax.rem(plane + PLANES - k, PLANES) * LINE + lax.rem(place + LINE - j, LINE)
+    def at(dz, dh, dx):
+        return lax.rem(z + 4 + dz, 4) * 8 + lax.rem(h + dh, 2) * 4 + lax.rem(x + 4 + dx, 4)
+
+    def send(source, target, out_sem, in_sem, to):
+        return pltpu.make_async_remote_copy(
+            src_ref=source, dst_ref=target, send_sem=out_sem, recv_sem=in_sem,
+            device_id={"seq": to}, device_id_type=MESH,
+        )
 
     def side(k):
         return lax.rem(exp_index + k, 4)
@@ -391,38 +398,85 @@
             device_id={"exp": side(k)}, device_id_type=MESH,
         )
 
-    def go_copy(k, j):
-        to = ahead(k, j)
-        return pltpu.make_async_remote_copy(
-            src_ref=rows_send.at[to], dst_ref=rows_recv.at[seq_index],
-            send_sem=go_out.at[k * LINE + j], recv_sem=go_in.at[k * LINE + j],
-            device_id={"seq": to}, device_id_type=MESH,
-        )
-
-    def back_copy(k, j):
-        to = behind(k, j)
-        return pltpu.make_async_remote_copy(
-            src_ref=made.at[to], dst_ref=rows_back.at[seq_index],
-            send_sem=back_out.at[k * LINE + j], recv_sem=back_in.at[k * LINE + j],
-            device_id={"seq": to}, device_id_type=MESH,
-        )
+    z_peers = [(i, m) for i in range(4) for m in range(2) if (i, m) != (0, 0)]
+    x_peers = [(j, m) for j in range(1, 4) for m in range(2)]
+
+    def info_copies():
+        return [
+            send(info_a.at[0, 0], info_a.at[i, m], info_out.at[n], info_in.at[n], at(i, m, 0))
+            for n, (i, m) in enumerate(z_peers)
+        ] + [
+            send(info_a.at[0, 0], info_b.at[j, m], info_out.at[7 + n], info_in.at[7 + n], at(0, m, j))
+            for n, (j, m) in enumerate(x_peers)
+        ]
+
+    def y_copies():
+        return [
+            send(got_a.at[0, 0], got_a.at[0, 1], y_out.at[0], y_in.at[0], at(0, 1, 0)),
+            send(got_b.at[0, 0], got_b.at[0, 1], y_out.at[1], y_in.at[1], at(0, 1, 0)),
+        ]
+
+    def wide_a(i, m):
+        return send(got_a.at[0, m], got_a.at[i, m], wide_out.at[0, m, i], wide_in.at[0, m, i], at(i, 0, 0))
+
+    def wide_b(i, m):
+        return send(got_b.at[0, m], got_b.at[i, m], wide_out.at[1, m, i], wide_in.at[1, m, i], at(0, 0, i))
+
+    def go_a(k, i):
+        return send(send_a.at[k, i], recv_a.at[k, i], go_out.at[0, k, i], go_in.at[0, k, i], at(0, 0, k))
+
+    def go_b(k, i):
+        return send(send_b.at[k, i], recv_b.at[k, i], go_out.at[1, k, i], go_in.at[1, k, i], at(k, 0, 0))
+
+    def ret_a(k, i):
+        return send(made_a.at[k, i], back_a.at[k, i], ret_out.at[k, i], ret_in.at[k, i], at(0, 0, -k))
+
+    def ret_b(i):
+        return send(made_b.at[i], back_b.at[i], ret_out.at[0, i], ret_in.at[0, i], at(-i, 0, 0))
+
+    def sum_a(i):
+        return send(part_a.at[i], red_a.at[i], red_out.at[0, i], red_in.at[0, i], at(-i, 0, 0))
+
+    def sum_b(i):
+        return send(part_b.at[i], red_b.at[i], red_out.at[1, i], red_in.at[1, i], at(0, 0, -i))
+
+    def last_copy(n):
+        return send(last_send.at[n], last_recv.at[n], last_out.at[n], last_in.at[n], at(0, 1, 0))
 
     barrier = pltpu.get_barrier_semaphore()
     for k in range(1, 4):
         pl.semaphore_signal(barrier, inc=1, device_id={"exp": side(k)}, device_id_type=MESH)
-
-    @pl.loop(1, EXPERTS)
-    def _(n):
-        pl.semaphore_signal(
-            barrier, inc=1, device_id={"seq": ahead(n // LINE, n % LINE)}, device_id_type=MESH
-        )
+    for i, m in z_peers:
+        pl.semaphore_signal(barrier, inc=1, device_id={"seq": at(i, m, 0)}, device_id_type=MESH)
+    for j, m in x_peers:
+        pl.semaphore_signal(barrier, inc=1, device_id={"seq": at(0, m, j)}, device_id_type=MESH)
 
     product[...] = jnp.dot(att_ref[...], ow_ref[...], preferred_element_type=jnp.float32).reshape(product.shape)
     for k in range(1, 4):
         sum_send[k] = product[side(k)].astype(jnp.bfloat16)
-    pl.semaphore_wait(barrier, 3 + EXPERTS - 1)
+    pl.semaphore_wait(barrier, 3 + len(z_peers) + len(x_peers))
     for k in range(1, 4):
         sum_copy(k).start()
+
+    chosen = routes_ref[...].astype(jnp.float32)
+    prob = prob_ref[...]
+    prob = prob / jnp.sum(prob, axis=0, keepdims=True)
+    expert = lax.broadcasted_iota(jnp.int32, (EXPERTS, 64), 0).astype(jnp.float32)
+    hit = jnp.zeros((EXPERTS, 64), jnp.float32)
+    share = jnp.zeros((EXPERTS, 64), jnp.float32)
+    for k in range(8):
+        match = chosen[k : k + 1, :] == expert
+        hit = jnp.where(match, 1.0, hit)
+        share = jnp.where(match, prob[k : k + 1, :], share)
+    before = (
+        lax.broadcasted_iota(jnp.int32, (64, 64), 0) <= lax.broadcasted_iota(jnp.int32, (64, 64), 1)
+    ).astype(jnp.bfloat16)
+    rank = jnp.dot(hit.astype(jnp.bfloat16), before, preferred_element_type=jnp.float32)
+    info_a[0, 0, :EXPERTS] = rank * hit
+    info_a[0, 0, EXPERTS:] = share
+    for copy in info_copies():
+        copy.start()
+
     mixed = product[exp_index]
     for k in range(1, 4):
         sum_copy(k).wait_recv()
@@ -431,76 +485,195 @@
     after = hid_ref[rows, :].astype(jnp.float32) + residual_scale * mixed
     residual[...] = after
     spread = lax.rsqrt(jnp.mean(after * after, axis=-1, keepdims=True) + norm_epsilon)
-    moe_in[...] = (after * spread * gain_ref[...]).astype(jnp.bfloat16)
-
-    @pl.loop(0, PLANES)
-    def _(k):
-        to = lax.rem(plane + k, PLANES)
-        pick = chosen_ref[pl.ds(pl.multiple_of(to * 256, 256), 256), :]
-        picked = jnp.dot(pick, moe_in[...], preferred_element_type=jnp.float32).astype(jnp.bfloat16)
-        rows_send[pl.ds(to * LINE, LINE)] = picked.reshape(LINE, CAP, -1)
-
-        @pl.loop(jnp.where(k == 0, 1, 0), LINE)
-        def _(j):
-            go_copy(k, j).start()
-
-        @pl.when(k == 0)
-        def _():
-            rows_recv[seq_index] = rows_send[seq_index]
-
-    @pl.loop(0, PLANES)
-    def _(k):
-        first = jnp.where(k == 0, 1, 0)
-        origin = lax.rem(plane + PLANES - k, PLANES)
-
-        @pl.loop(first, LINE)
-        def _(j):
-            go_copy(k, j).wait_recv()
-
-        arrived = rows_recv[pl.ds(origin * LINE, LINE)].reshape(LINE * CAP, -1)
-        hidden = jnp.dot(arrived, win_ref[...], preferred_element_type=jnp.float32)
+    moe_in = (after * spread * gain_ref[...]).astype(jnp.bfloat16)
+    got_a[0, 0] = moe_in[:, :HALF]
+    got_b[0, 0] = moe_in[:, HALF:]
+    for copy in y_copies():
+        copy.start()
+    for i in (1, 3, 2):
+        wide_a(i, 0).start()
+        wide_b(i, 0).start()
+    for copy in info_copies():
+        copy.wait_recv()
+    info_b[0] = info_a[0]
+
+    slot = lax.broadcasted_iota(jnp.int32, (CAP, 64), 0).astype(jnp.float32) + 1.0
+
+    def experts_a(k):
+        return z * 8 + h * 4 + lax.rem(x + k, 4)
+
+    def experts_b(k):
+        return lax.rem(z + k, 4) * 8 + h * 4 + x
+
+    def picks(info, i, m, experts_of):
+        return jnp.concatenate(
+            [(info[i, m, pl.ds(experts_of(k), 1), :] == slot).astype(jnp.float32) for k in range(4)], axis=0
+        ).astype(jnp.bfloat16)
+
+    def mixes(info, i, m, experts_of):
+        return jnp.concatenate(
+            [
+                jnp.where(
+                    info[i, m, pl.ds(experts_of(k), 1), :] == slot,
+                    info[i, m, pl.ds(EXPERTS + experts_of(k), 1), :],
+                    0.0,
+                )
+                for k in range(4)
+            ],
+            axis=0,
+        ).astype(jnp.bfloat16)
+
+    def pick(info, got, experts_of, sends, recvs, i, m):
+        taken = jnp.dot(
+            picks(info, i, m, experts_of), got[i, m], preferred_element_type=jnp.float32
+        ).astype(jnp.bfloat16)
+        recvs[0, i, m] = taken[:CAP]
+        for k in range(1, 4):
+            sends[k, i, m] = taken[k * CAP : (k + 1) * CAP]
+
+    @pl.loop(0, 4)
+    def _(i):
+        @pl.when(i == 0)
+        def _():
+            for copy in y_copies():
+                copy.wait_recv()
+            for n in (1, 3, 2):
+                wide_a(n, 1).start()
+                wide_b(n, 1).start()
+
+        @pl.when(i > 0)
+        def _():
+            for m in range(2):
+                wide_a(i, m).wait_recv()
+                wide_b(i, m).wait_recv()
+
+        for m in range(2):
+            pick(info_a, got_a, experts_a, send_a, recv_a, i, m)
+        for k in range(1, 4):
+            go_a(k, i).start()
+        for m in range(2):
+            pick(info_b, got_b, experts_b, send_b, recv_b, i, m)
+        for k in range(1, 4):
+            go_b(k, i).start()
+
+    @pl.loop(0, 4)
+    def _(i):
+        for k in range(1, 4):
+            go_a(k, i).wait_recv()
+
+        @pl.when(i > 0)
+        def _():
+            for j in range(4):
+                send(
+                    send_b.at[i, j], recv_b.at[i, j], go_out.at[1, i, j], go_in.at[1, i, j], at(i, 0, 0)
+                ).wait_recv()
+
+        hidden = jnp.dot(
+            recv_a[:, i].reshape(256, HALF), win_ref[:HALF, :], preferred_element_type=jnp.float32
+        ) + jnp.dot(recv_b[i].reshape(256, HALF), win_ref[HALF:, :], preferred_element_type=jnp.float32)
         gate, up = hidden[:, :512], hidden[:, 512:]
         active = (gate / (1.0 + jnp.exp(-gate)) * up).astype(jnp.bfloat16)
         done = jnp.dot(active, wout_ref[...], preferred_element_type=jnp.float32).astype(jnp.bfloat16)
-        made[pl.ds(origin * LINE, LINE)] = done.reshape(LINE, CAP, -1)
-
-        @pl.loop(first, LINE)
-        def _(j):
-            back_copy(k, j).start()
-
-        @pl.when(k == 0)
-        def _():
-            rows_back[seq_index] = made[seq_index]
-
-    total[...] = jnp.zeros_like(total)
-
-    @pl.loop(0, PLANES)
-    def _(k):
-        @pl.loop(jnp.where(k == 0, 1, 0), LINE)
-        def _(j):
-            back_copy(k, j).wait_recv()
-
-        owner = lax.rem(plane + k, PLANES)
-        mix = mix_ref[:, pl.ds(pl.multiple_of(owner * 256, 256), 256)]
-        total[...] += jnp.dot(
-            mix, rows_back[pl.ds(owner * LINE, LINE)].reshape(LINE * CAP, -1), preferred_element_type=jnp.float32
+        done_a = done[:, :HALF].reshape(4, 2, CAP, HALF)
+        back_a[0, i] = done_a[0]
+        for k in range(1, 4):
+            made_a[k, i] = done_a[k]
+            ret_a(k, i).start()
+        made_b[i] = done[:, HALF:].reshape(4, 2, CAP, HALF)
+
+        @pl.when(i > 0)
+        def _():
+            ret_b(i).start()
+
+        @pl.when(i == 0)
+        def _():
+            back_b[0] = made_b[0]
+
+    def mix(info, backs, experts_of, i, m):
+        return lax.dot_general(
+            mixes(info, i, m, experts_of), backs[:, i, m].reshape(4 * CAP, HALF),
+            (((0,), (0,)), ((), ())), preferred_element_type=jnp.float32,
         )
 
-    out_ref[...] = (residual[...] + residual_scale * (total[:64] + total[64:])).astype(jnp.bfloat16)
+    @pl.loop(0, 4)
+    def _(i):
+        for k in range(1, 4):
+            ret_a(k, i).wait_recv()
+        for m in range(2):
+            some = mix(info_a, back_a, experts_a, i, m)
+            part_a[i, m] = some.astype(jnp.bfloat16)
+
+            @pl.when(i == 0)
+            def _():
+                acc_a[m] = some
+
+        @pl.when(i > 0)
+        def _():
+            sum_a(i).start()
+
+    for i in range(1, 4):
+        ret_b(i).wait_recv()
+
+    @pl.loop(0, 4)
+    def _(n):
+        i = 3 - n
+        for m in range(2):
+            some = mix(info_b, back_b, experts_b, i, m)
+            part_b[i, m] = some.astype(jnp.bfloat16)
+
+            @pl.when(i == 0)
+            def _():
+                acc_b[m] = some
+
+        @pl.when(i > 0)
+        def _():
+            sum_b(i).start()
+
+    for n, (copy, acc, red) in enumerate(((sum_a, acc_a, red_a), (sum_b, acc_b, red_b))):
+        for i in range(1, 4):
+            copy(i).wait_recv()
+            acc[...] += red[i].astype(jnp.float32)
+        last_send[n] = acc[1].astype(jnp.bfloat16)
+        last_copy(n).start()
+    for n, acc in enumerate((acc_a, acc_b)):
+        last_copy(n).wait_recv()
+        cols = slice(n * HALF, (n + 1) * HALF)
+        moe = acc[0] + last_recv[n].astype(jnp.float32)
+        out_ref[:, cols] = (residual[:, cols] + residual_scale * moe).astype(jnp.bfloat16)
 
     for k in range(1, 4):
         sum_copy(k).wait_send()
-
-    @pl.loop(1, EXPERTS)
-    def _(n):
-        go_copy(n // LINE, n % LINE).wait_send()
-        back_copy(n // LINE, n % LINE).wait_send()
+    for copy in info_copies() + y_copies():
+        copy.wait_send()
+    for n in range(2):
+        last_copy(n).wait_send()
+
+    @pl.loop(1, 4)
+    def _(i):
+        for m in range(2):
+            wide_a(i, m).wait_send()
+            wide_b(i, m).wait_send()
+        ret_b(i).wait_send()
+        sum_a(i).wait_send()
+        sum_b(i).wait_send()
+
+    @pl.loop(0, 4)
+    def _(i):
+        for k in range(1, 4):
+            go_a(k, i).wait_send()
+            go_b(k, i).wait_send()
+            ret_a(k, i).wait_send()
 
 
 def experts(*operands):
     vmem = pl.BlockSpec(memory_space=pltpu.VMEM)
     width = 1536
-    block = pltpu.VMEM((EXPERTS, CAP, width), jnp.bfloat16)
+    table = pltpu.VMEM((4, 2, 64, 64), jnp.float32)
+    blocks = pltpu.VMEM((4, 2, 64, HALF), jnp.bfloat16)
+    chosen = pltpu.VMEM((4, 4, 2, CAP, HALF), jnp.bfloat16)
+    pair = pltpu.VMEM((2, 64, HALF), jnp.float32)
+    last = pltpu.VMEM((2, 64, HALF), jnp.bfloat16)
+    counts = ((4,), (13,), (2,), (2, 2, 4), (2, 4, 4), (4, 4), (2, 4), (2,))
     return pl.pallas_call(
         experts_kernel,
         out_shape=jax.ShapeDtypeStruct((64, width), jnp.bfloat16),
@@ -511,16 +684,17 @@
             pltpu.VMEM((4, 64, width), jnp.bfloat16),
             pltpu.VMEM((4, 64, width), jnp.bfloat16),
             pltpu.VMEM((64, width), jnp.float32),
-            pltpu.VMEM((64, width), jnp.bfloat16),
-            block,
-            block,
-            block,
-            block,
-            pltpu.VMEM((128, width), jnp.float32),
+            table,
+            table,
+            blocks,
+            blocks,
         ]
-        + [pltpu.SemaphoreType.DMA((n,)) for n in (4, 4, 32, 32, 32, 32)],
+        + [chosen] * 8
+        + [blocks] * 4
+        + [pair, pair, last, last]
+        + [pltpu.SemaphoreType.DMA(n) for n in counts for _ in range(2)],
         compiler_params=pltpu.CompilerParams(
-            vmem_limit_bytes=48 * 1024 * 1024, collective_id=2, has_side_effects=True
+            vmem_limit_bytes=52 * 1024 * 1024, collective_id=2, has_side_effects=True
         ),
         name="experts",
     )(*operands)
@@ -546,28 +720,8 @@
     )
     page_rows = page_slabs.transpose(1, 0, 2).reshape(ROWS // PAGE, KV_HERE, 2, PAGE * HEAD_DIM)
 
-    moe_rows = routes.shape[0]
-    named = (routes[:, :, None] == jnp.arange(EXPERTS, dtype=jnp.int32)).astype(jnp.float32)
-    hit = jnp.sum(named, axis=1)
-    share = route_prob / jnp.sum(route_prob, axis=-1, keepdims=True)
-    share_of = jnp.sum(named * share[..., None], axis=1)
-    before = jnp.tril(jnp.ones((moe_rows, moe_rows), jnp.bfloat16), -1)
-    rank = jnp.dot(before, hit.astype(jnp.bfloat16), preferred_element_type=jnp.float32)
-    slot = jnp.arange(CAP, dtype=jnp.float32)
-    chosen = jnp.where(hit[..., None] > 0, (rank[..., None] == slot).astype(jnp.float32), 0.0)
-    chosen = chosen.reshape(moe_rows, EXPERTS * CAP)
-    mixing = chosen * jnp.repeat(share_of, CAP, axis=1)
-    high = mixing.astype(jnp.bfloat16)
-    low = (mixing - high.astype(jnp.float32)).astype(jnp.bfloat16)
     hidden_out = experts(
-        attended,
-        o_weight,
-        hidden_in,
-        moe_gain[None, :],
-        chosen.astype(jnp.bfloat16).T,
-        jnp.concatenate([high, low], axis=0),
-        expert_in[0],
-        expert_out[0],
+        attended, o_weight, hidden_in, moe_gain[None, :], routes.T, route_prob.T, expert_in[0], expert_out[0]
     )
     return (hidden_out, page_rows)
 

time: 201 us -> 165 us (0.82)
  the two profiles are of different devices: /device:TPU:59 before, /device:TPU:0 now
where the time goes in v4:
time: 165 us
  Pallas kernels  157 us (95%)
  local copies, waits for them, and re-layouts  6.65 us (4%)
    pallas_call x1, Pallas kernels, experts(): pl.pallas_call(experts_kernel, out_shape=jax.ShapeDtypeStruct((64, width)...  89.6 us
    pallas_call x1, Pallas kernels, attend(): pl.pallas_call(attend_kernel, out_shape=[jax.ShapeDtypeStruct((ROWS, 384)...  67.7 us
    unnamed x14, local copies, waits for them, and re-layouts  4.42 us

profile of v4, /device:TPU:0, one launch (start us, length us, event | category | flops | bytes accessed | tf_op | source)
XLA Modules:
  0.0 164.6 jit_solution(3647226132936024928)
XLA Ops:
  0.6 0.0 copy-start
  0.6 0.8 broadcast_in_dim.6.gain_ref
  1.4 0.7 broadcast_in_dim.7.gain_ref
  2.1 0.8 reshape.10.slot_ref
  2.9 0.0 copy-start.1
  2.9 1.0 copy-done.1
  3.9 0.0 copy-start.2
  3.9 1.0 copy-done.2
  4.9 0.0 copy-start.3
  4.9 0.9 copy-done.3
  5.8 0.0 copy-start.4
  5.8 0.0 copy-start.5
  5.8 67.7 %attend.1 = (bf16[256,384]{1,0:T(8,128)(2,1)S(1)}, bf16[4,32,512]{2,1,0:T(8,128)(2,1)S(1)}) custom-call(bf16[256,1536]{1,0:T(8,128)(2,1)} %hid_ref.3, f32[1,1536]{1,0:T(1,128)S(1)} %broadcast_in_dim.6.gain_ref, bf16[1536,384]{1,0:T(8,128)(2,1)} %qw_ref.1, bf16[1536,128]{1,0:T(8,128)(2,1)S(1)} %copy-done.1, bf16[1536,128]{1,0:T(8,128)(2,1)S(1)} %copy-done.2, ...), custom_call_target="tpu_custom_call" | custom-call | tf_op jit(solution)/shard_map/attend/pallas_call | solution.py:335
  73.5 0.0 copy-done
  73.5 0.0 copy-done.4
  73.5 0.0 copy-done.5
  73.5 89.6 %experts.1 = bf16[64,1536]{1,0:T(8,128)(2,1)S(1)} custom-call(bf16[256,384]{1,0:T(8,128)(2,1)S(1)} %get-tuple-element.4.att_ref, bf16[384,1536]{1,0:T(8,128)(2,1)} %ow_ref.1, bf16[256,1536]{1,0:T(8,128)(2,1)S(1)} %copy-done, f32[1,1536]{1,0:T(1,128)S(1)} %broadcast_in_dim.7.gain_ref, s32[8,64]{1,0:T(8,128)S(1)} %bitcast.8, f32[8,64]{1,0:T(8,128)S(1)} %bitcast.9, ...), custom_call_target="tpu_custom_call" | custom-call | tf_op jit(solution)/shard_map/experts/pallas_call | solution.py:677
  163.1 0.8 copy.15
  163.9 0.7 copy.17
Async XLA Ops:
  0.6 72.9 %copy-start = (bf16[256,1536]{1,0:T(8,128)(2,1)S(1)}, bf16[256,1536]{1,0:T(8,128)(2,1)}, u32[]{:S(2)}) copy-start(bf16[256,1536]{1,0:T(8,128)(2,1)} %hid_ref.3) | copy-start | bytes 2359300
  2.9 1.0 copy-start.1
  3.9 1.0 copy-start.2
  4.9 0.9 copy-start.3
  5.8 67.7 %copy-start.4 = (s32[64,8]{0,1:T(8,128)S(1)}, s32[64,8]{0,1:T(8,128)}, u32[]{:S(2)}) copy-start(s32[64,8]{0,1:T(8,128)} %param.23) | copy-start | bytes 6148
  5.8 67.7 %copy-start.5 = (f32[64,8]{0,1:T(8,128)S(1)}, f32[64,8]{0,1:T(8,128)}, u32[]{:S(2)}) copy-start(f32[64,8]{0,1:T(8,128)} %param.24) | copy-start | bytes 6148

commit v5 on v4

--- a/solution.py
+++ b/solution.py
@@ -26,13 +26,20 @@
 
 
 NEAR = ((0, 0), (0, 1), (1, 0), (0, 3), (1, 1), (0, 2), (1, 3), (1, 2))
-
-
-def attend_kernel(
-    hid_ref, gain_ref, qw_ref, kw_ref, vw_ref, cache_ref, slot_ref, out_ref, page_ref,
-    normed, query, q_all, cache_all, new_own, new_all, cache_val, new_val, qs, best, acc,
+HALF = 768
+
+
+def layer_kernel(
+    hid_hbm, attn_gain_ref, qw_hbm, kw_hbm, vw_hbm, cache_hbm, slot_ref,
+    ow_hbm, moe_gain_ref, routes_ref, prob_ref, win_hbm, wout_hbm, out_ref, page_ref,
+    hid_ref, qw_ref, kw_ref, vw_ref, ow_ref, win_ref, wout_ref, att_ref,
+    query, q_all, cache_all, new_own, new_all, cache_val, new_val, qs, best, acc,
     part_send, part_recv, page_send, page_recv,
-    q_out, q_in, cache_out, cache_in, new_out, new_in, part_out, part_in, page_out, page_in,
+    product, sum_send, sum_recv, residual, info_a, info_b, got_a, got_b, send_a, send_b, recv_a, recv_b,
+    made_a, made_b, back_a, back_b, sum_part_a, sum_part_b, red_a, red_b, acc_a, acc_b, last_send, last_recv,
+    load_in, q_out, q_in, cache_out, cache_in, new_out, new_in, part_out, part_in, page_out, page_in,
+    sum_out, sum_in, info_out, info_in, y_out, y_in, wide_out, wide_in, go_out, go_in,
+    ret_out, ret_in, red_out, red_in, last_out, last_in,
 ):
     seq_index = lax.axis_index("seq")
     plane = seq_index // LINE
@@ -61,7 +68,7 @@
 
     def cache_copy(n):
         rows = pl.ds((n % 2) * CACHE_HERE, CACHE_HERE)
-        return send(cache_ref, cache_all.at[n // 2, rows], cache_out.at[n], cache_in.at[n], peer(n))
+        return send(cache_all.at[0, pl.ds(0, CACHE_HERE)], cache_all.at[n // 2, rows], cache_out.at[n], cache_in.at[n], peer(n))
 
     def new_copy(n):
         return send(new_own, new_all.at[place], new_out.at[n], new_in.at[n], peer(n))
@@ -90,38 +97,119 @@
     def gets_part(k):
         return jnp.logical_or(plane < 2, plane == 3) if k == 1 else plane < 2
 
+    exp_index = lax.axis_index("exp")
+    z, h, x = seq_index // 8, lax.rem(seq_index // 4, 2), lax.rem(seq_index, 4)
+
+    def at(dz, dh, dx):
+        return lax.rem(z + 4 + dz, 4) * 8 + lax.rem(h + dh, 2) * 4 + lax.rem(x + 4 + dx, 4)
+
+    def side(k):
+        return lax.rem(exp_index + k, 4)
+
+    def sum_copy(k):
+        return pltpu.make_async_remote_copy(
+            src_ref=sum_send.at[k], dst_ref=sum_recv.at[k], send_sem=sum_out.at[k], recv_sem=sum_in.at[k],
+            device_id={"exp": side(k)}, device_id_type=MESH,
+        )
+
+    z_peers = [(i, m) for i in range(4) for m in range(2) if (i, m) != (0, 0)]
+    x_peers = [(j, m) for j in range(1, 4) for m in range(2)]
+
+    def info_copies():
+        return [
+            send(info_a.at[0, 0], info_a.at[i, m], info_out.at[n], info_in.at[n], at(i, m, 0))
+            for n, (i, m) in enumerate(z_peers)
+        ] + [
+            send(info_a.at[0, 0], info_b.at[j, m], info_out.at[7 + n], info_in.at[7 + n], at(0, m, j))
+            for n, (j, m) in enumerate(x_peers)
+        ]
+
+    def y_copies():
+        return [
+            send(got_a.at[0, 0], got_a.at[0, 1], y_out.at[0], y_in.at[0], at(0, 1, 0)),
+            send(got_b.at[0, 0], got_b.at[0, 1], y_out.at[1], y_in.at[1], at(0, 1, 0)),
+        ]
+
+    def wide_a(i, m):
+        return send(got_a.at[0, m], got_a.at[i, m], wide_out.at[0, m, i], wide_in.at[0, m, i], at(i, 0, 0))
+
+    def wide_b(i, m):
+        return send(got_b.at[0, m], got_b.at[i, m], wide_out.at[1, m, i], wide_in.at[1, m, i], at(0, 0, i))
+
+    def go_a(k, i):
+        return send(send_a.at[k, i], recv_a.at[k, i], go_out.at[0, k, i], go_in.at[0, k, i], at(0, 0, k))
+
+    def go_b(k, i):
+        return send(send_b.at[k, i], recv_b.at[k, i], go_out.at[1, k, i], go_in.at[1, k, i], at(k, 0, 0))
+
+    def ret_a(k, i):
+        return send(made_a.at[k, i], back_a.at[k, i], ret_out.at[k, i], ret_in.at[k, i], at(0, 0, -k))
+
+    def ret_b(i):
+        return send(made_b.at[i], back_b.at[i], ret_out.at[0, i], ret_in.at[0, i], at(-i, 0, 0))
+
+    def sum_a(i):
+        return send(sum_part_a.at[i], red_a.at[i], red_out.at[0, i], red_in.at[0, i], at(-i, 0, 0))
+
+    def sum_b(i):
+        return send(sum_part_b.at[i], red_b.at[i], red_out.at[1, i], red_in.at[1, i], at(0, 0, -i))
+
+    def last_copy(n):
+        return send(last_send.at[n], last_recv.at[n], last_out.at[n], last_in.at[n], at(0, 1, 0))
+
     barrier = pltpu.get_barrier_semaphore()
 
     @pl.loop(1, 32)
     def _(n):
         pl.semaphore_signal(barrier, inc=1, device_id={"seq": ahead(n)}, device_id_type=MESH)
 
-    cache_all[0, :CACHE_HERE] = cache_ref[...]
+    for k in range(1, 4):
+        pl.semaphore_signal(barrier, inc=1, device_id={"exp": side(k)}, device_id_type=MESH)
+
+    loads = [
+        pltpu.make_async_copy(source, target, load_in.at[n])
+        for n, (source, target) in enumerate(
+            (
+                (hid_hbm, hid_ref), (qw_hbm, qw_ref), (kw_hbm, kw_ref), (vw_hbm, vw_ref), (cache_hbm, cache_all.at[0, pl.ds(0, CACHE_HERE)]),
+                (ow_hbm, ow_ref), (win_hbm, win_ref), (wout_hbm, wout_ref),
+            )
+        )
+    ]
+    for load in loads:
+        load.start()
     for k in range(1, PLANES):
         @pl.when(jnp.logical_not(gets_part(k)))
         def _():
             part_recv[k, :, :384] = jnp.zeros((ROWS, 384), jnp.bfloat16)
             part_recv[k, :, 384:] = jnp.full((ROWS, 128), masked_score, jnp.bfloat16)
 
-    pl.semaphore_wait(barrier, 31)
-    for n in range(1, 4):
-        cache_copy(n).start()
+    best[...] = jnp.full_like(best, masked_score)
+    acc[...] = jnp.zeros_like(acc)
+    loads[0].wait()
 
     @pl.loop(0, ROWS // 64)
     def _(step):
         rows = pl.ds(pl.multiple_of(step * 64, 64), 64)
         wide = hid_ref[rows, :].astype(jnp.float32)
         spread = lax.rsqrt(jnp.mean(wide * wide, axis=-1, keepdims=True) + norm_epsilon)
-        normed[rows, :] = (wide * spread * gain_ref[...]).astype(jnp.bfloat16)
-
-    query[...] = jnp.dot(normed[...], qw_ref[...], preferred_element_type=jnp.float32).astype(jnp.bfloat16)
+        sum_send[step] = (wide * spread * attn_gain_ref[...][None, :]).astype(jnp.bfloat16)
+
+    loads[4].wait()
+    loads[1].wait()
+    normed = sum_send[...].reshape(ROWS, 1536)
+    query[...] = jnp.dot(normed, qw_ref[...], preferred_element_type=jnp.float32).astype(jnp.bfloat16)
+    pl.semaphore_wait(barrier, 31 + 3)
     for k in range(1, PLANES):
         @pl.when(sends_query(k))
         def _():
             query_copy(k).start()
 
-    keys = jnp.dot(normed[...], kw_ref[...], preferred_element_type=jnp.float32)
-    values = jnp.dot(normed[...], vw_ref[...], preferred_element_type=jnp.float32)
+    for n in range(1, 4):
+        cache_copy(n).start()
+    loads[2].wait()
+    loads[3].wait()
+    keys = jnp.dot(normed, kw_ref[...], preferred_element_type=jnp.float32)
+    values = jnp.dot(normed, vw_ref[...], preferred_element_type=jnp.float32)
     slabs = [
         jnp.where(low, keys, pltpu.roll(values, HEAD_DIM, 1)).astype(jnp.bfloat16),
         jnp.where(low, pltpu.roll(keys, HEAD_DIM, 1), values).astype(jnp.bfloat16),
@@ -138,12 +226,29 @@
     def _(n):
         page_copy(n).start()
 
+    chosen = routes_ref[...].astype(jnp.float32)
+    prob = prob_ref[...]
+    prob = prob / jnp.sum(prob, axis=0, keepdims=True)
+    expert = lax.broadcasted_iota(jnp.int32, (EXPERTS, 64), 0).astype(jnp.float32)
+    hit = jnp.zeros((EXPERTS, 64), jnp.float32)
+    share = jnp.zeros((EXPERTS, 64), jnp.float32)
+    for k in range(8):
+        match = chosen[k : k + 1, :] == expert
+        hit = jnp.where(match, 1.0, hit)
+        share = jnp.where(match, prob[k : k + 1, :], share)
+    before = (
+        lax.broadcasted_iota(jnp.int32, (64, 64), 0) <= lax.broadcasted_iota(jnp.int32, (64, 64), 1)
+    ).astype(jnp.bfloat16)
+    rank = jnp.dot(hit.astype(jnp.bfloat16), before, preferred_element_type=jnp.float32)
+    info_a[0, 0, :EXPERTS] = rank * hit
+    info_a[0, 0, EXPERTS:] = share
+    for copy in info_copies():
+        copy.start()
+
     q_all[plane] = query[...]
     new_all[place] = new_own[...]
     own_rows = pl.ds(pl.multiple_of(seq_index * PAGE, PAGE), PAGE)
     page_recv[seq_index] = page_send[own_rows, :]
-    best[...] = jnp.full_like(best, masked_score)
-    acc[...] = jnp.zeros_like(acc)
 
     def prepare(t):
         for h in range(HEADS_HERE):
@@ -198,20 +303,20 @@
             @pl.when(m > 0)
             def _():
                 send(
-                    cache_ref, cache_all.at[m, pl.ds(0, CACHE_HERE)],
+                    cache_all.at[0, pl.ds(0, CACHE_HERE)], cache_all.at[m, pl.ds(0, CACHE_HERE)],
                     cache_out.at[2 * m], cache_in.at[2 * m], peer(1),
                 ).wait_recv()
 
             send(
-                cache_ref, cache_all.at[m, pl.ds(CACHE_HERE, CACHE_HERE)],
+                cache_all.at[0, pl.ds(0, CACHE_HERE)], cache_all.at[m, pl.ds(CACHE_HERE, CACHE_HERE)],
                 cache_out.at[2 * m + 1], cache_in.at[2 * m + 1], peer(1),
             ).wait_recv()
             cache_pair(m)
 
     cache_pairs(0)
     for n in range(1, LINE):
-        h, x = NEAR[n]
-        origin = lax.rem(place // 4 + h, 2) * 4 + lax.rem(place % 4 + 4 - x, 4)
+        dh, dx = NEAR[n]
+        origin = lax.rem(place // 4 + dh, 2) * 4 + lax.rem(place % 4 + 4 - dx, 4)
         send(new_own, new_all.at[origin], new_out.at[n], new_in.at[n], peer(n)).wait_recv()
 
     @pl.loop(0, LINE)
@@ -224,10 +329,6 @@
 
     def new_values(step):
         return lambda g: new_val[pl.ds(step * 4, 4), :, slab_of(g)].reshape(1024, 128)
-
-    @pl.loop(0, place // 4 + 1)
-    def _(step):
-        update((plane,), new_keys(step), new_values(step), step * 1024)
 
     @pl.loop(0, jnp.where(even, 2, 0))
     def _(step):
@@ -263,13 +364,24 @@
             part_send[k, :, 384:512] = split.astype(jnp.bfloat16)
             part_copy(k).start()
 
+    @pl.loop(0, place // 4 + 1)
+    def _(step):
+        update((plane,), new_keys(step), new_values(step), step * 1024)
+
     @pl.loop(1, 32)
     def _(n):
         page_copy(n).wait_recv()
 
     column = lax.broadcasted_iota(jnp.int32, (32, 32), 1)
+    block_of = lax.broadcasted_iota(jnp.int32, (32, 1024), 0) * 32 + seq_index
     slots = jnp.sum(
-        jnp.where(column == seq_index, slot_ref[...].astype(jnp.float32), 0.0), axis=1, keepdims=True
+        jnp.where(
+            lax.broadcasted_iota(jnp.int32, (32, 1024), 1) == block_of,
+            slot_ref[...].astype(jnp.float32)[None, :],
+            0.0,
+        ),
+        axis=1,
+        keepdims=True,
     )
     owner = (slots == column.astype(jnp.float32)).astype(jnp.bfloat16)
     low_page = lax.broadcasted_iota(jnp.int32, (32, 128), 1) < HEAD_DIM
@@ -309,7 +421,7 @@
         value = pairs[p] * spread(shares[0], p)
         for k in range(1, PLANES):
             value = value + part_recv[k, :, cols].astype(jnp.float32) * spread(shares[k], p)
-        out_ref[:, cols] = value.astype(jnp.bfloat16)
+        att_ref[:, cols] = value.astype(jnp.bfloat16)
 
     for n in range(1, LINE):
         cache_copy(n).wait_send()
@@ -328,154 +440,12 @@
     def _(n):
         page_copy(n).wait_send()
 
-
-def attend(*operands):
-    vmem = pl.BlockSpec(memory_space=pltpu.VMEM)
-    state = pltpu.VMEM((PLANES, KV_HERE, GROUP * ROWS, 128), jnp.float32)
-    return pl.pallas_call(
-        attend_kernel,
-        out_shape=[
-            jax.ShapeDtypeStruct((ROWS, 384), jnp.bfloat16),
-            jax.ShapeDtypeStruct((2 * KV_HERE, ROWS // PAGE, PAGE * HEAD_DIM), jnp.bfloat16),
-        ],
-        in_specs=[vmem] * 7,
-        out_specs=[vmem] * 2,
-        scratch_shapes=[
-            pltpu.VMEM((ROWS, 1536), jnp.bfloat16),
-            pltpu.VMEM((ROWS, 384), jnp.bfloat16),
-            pltpu.VMEM((PLANES, ROWS, 384), jnp.bfloat16),
-            pltpu.VMEM((LINE // 2, 2 * CACHE_HERE, 256), jnp.bfloat16),
-            pltpu.VMEM((ROWS, 256), jnp.bfloat16),
-            pltpu.VMEM((LINE, ROWS, 256), jnp.bfloat16),
-            pltpu.VMEM((2 * CACHE_HERE, 256), jnp.bfloat16),
-            pltpu.VMEM((LINE, ROWS, 256), jnp.bfloat16),
-            pltpu.VMEM((PLANES, KV_HERE, GROUP * ROWS, 128), jnp.bfloat16),
-            state,
-            state,
-            pltpu.VMEM((PLANES, ROWS, 512), jnp.bfloat16),
-            pltpu.VMEM((PLANES, ROWS, 512), jnp.bfloat16),
-            pltpu.VMEM((ROWS, 256), jnp.float32),
-            pltpu.VMEM((ROWS // PAGE, PAGE, 256), jnp.float32),
-        ]
-        + [pltpu.SemaphoreType.DMA((n,)) for n in (4, 4, 8, 8, 8, 8, 4, 4, 32, 32)],
-        compiler_params=pltpu.CompilerParams(
-            vmem_limit_bytes=52 * 1024 * 1024, collective_id=1, has_side_effects=True
-        ),
-        name="attend",
-    )(*operands)
-
-
-HALF = 768
-
-
-def experts_kernel(
-    att_ref, ow_ref, hid_ref, gain_ref, routes_ref, prob_ref, win_ref, wout_ref, out_ref,
-    product, sum_send, sum_recv, residual, info_a, info_b, got_a, got_b, send_a, send_b, recv_a, recv_b,
-    made_a, made_b, back_a, back_b, part_a, part_b, red_a, red_b, acc_a, acc_b, last_send, last_recv,
-    sum_out, sum_in, info_out, info_in, y_out, y_in, wide_out, wide_in, go_out, go_in,
-    ret_out, ret_in, red_out, red_in, last_out, last_in,
-):
-    seq_index = lax.axis_index("seq")
-    exp_index = lax.axis_index("exp")
-    z, h, x = seq_index // 8, lax.rem(seq_index // 4, 2), lax.rem(seq_index, 4)
-    MESH = pl.DeviceIdType.MESH
-
-    def at(dz, dh, dx):
-        return lax.rem(z + 4 + dz, 4) * 8 + lax.rem(h + dh, 2) * 4 + lax.rem(x + 4 + dx, 4)
-
-    def send(source, target, out_sem, in_sem, to):
-        return pltpu.make_async_remote_copy(
-            src_ref=source, dst_ref=target, send_sem=out_sem, recv_sem=in_sem,
-            device_id={"seq": to}, device_id_type=MESH,
-        )
-
-    def side(k):
-        return lax.rem(exp_index + k, 4)
-
-    def sum_copy(k):
-        return pltpu.make_async_remote_copy(
-            src_ref=sum_send.at[k], dst_ref=sum_recv.at[k], send_sem=sum_out.at[k], recv_sem=sum_in.at[k],
-            device_id={"exp": side(k)}, device_id_type=MESH,
-        )
-
-    z_peers = [(i, m) for i in range(4) for m in range(2) if (i, m) != (0, 0)]
-    x_peers = [(j, m) for j in range(1, 4) for m in range(2)]
-
-    def info_copies():
-        return [
-            send(info_a.at[0, 0], info_a.at[i, m], info_out.at[n], info_in.at[n], at(i, m, 0))
-            for n, (i, m) in enumerate(z_peers)
-        ] + [
-            send(info_a.at[0, 0], info_b.at[j, m], info_out.at[7 + n], info_in.at[7 + n], at(0, m, j))
-            for n, (j, m) in enumerate(x_peers)
-        ]
-
-    def y_copies():
-        return [
-            send(got_a.at[0, 0], got_a.at[0, 1], y_out.at[0], y_in.at[0], at(0, 1, 0)),
-            send(got_b.at[0, 0], got_b.at[0, 1], y_out.at[1], y_in.at[1], at(0, 1, 0)),
-        ]
-
-    def wide_a(i, m):
-        return send(got_a.at[0, m], got_a.at[i, m], wide_out.at[0, m, i], wide_in.at[0, m, i], at(i, 0, 0))
-
-    def wide_b(i, m):
-        return send(got_b.at[0, m], got_b.at[i, m], wide_out.at[1, m, i], wide_in.at[1, m, i], at(0, 0, i))
-
-    def go_a(k, i):
-        return send(send_a.at[k, i], recv_a.at[k, i], go_out.at[0, k, i], go_in.at[0, k, i], at(0, 0, k))
-
-    def go_b(k, i):
-        return send(send_b.at[k, i], recv_b.at[k, i], go_out.at[1, k, i], go_in.at[1, k, i], at(k, 0, 0))
-
-    def ret_a(k, i):
-        return send(made_a.at[k, i], back_a.at[k, i], ret_out.at[k, i], ret_in.at[k, i], at(0, 0, -k))
-
-    def ret_b(i):
-        return send(made_b.at[i], back_b.at[i], ret_out.at[0, i], ret_in.at[0, i], at(-i, 0, 0))
-
-    def sum_a(i):
-        return send(part_a.at[i], red_a.at[i], red_out.at[0, i], red_in.at[0, i], at(-i, 0, 0))
-
-    def sum_b(i):
-        return send(part_b.at[i], red_b.at[i], red_out.at[1, i], red_in.at[1, i], at(0, 0, -i))
-
-    def last_copy(n):
-        return send(last_send.at[n], last_recv.at[n], last_out.at[n], last_in.at[n], at(0, 1, 0))
-
-    barrier = pltpu.get_barrier_semaphore()
-    for k in range(1, 4):
-        pl.semaphore_signal(barrier, inc=1, device_id={"exp": side(k)}, device_id_type=MESH)
-    for i, m in z_peers:
-        pl.semaphore_signal(barrier, inc=1, device_id={"seq": at(i, m, 0)}, device_id_type=MESH)
-    for j, m in x_peers:
-        pl.semaphore_signal(barrier, inc=1, device_id={"seq": at(0, m, j)}, device_id_type=MESH)
-
+    loads[5].wait()
     product[...] = jnp.dot(att_ref[...], ow_ref[...], preferred_element_type=jnp.float32).reshape(product.shape)
     for k in range(1, 4):
         sum_send[k] = product[side(k)].astype(jnp.bfloat16)
-    pl.semaphore_wait(barrier, 3 + len(z_peers) + len(x_peers))
     for k in range(1, 4):
         sum_copy(k).start()
-
-    chosen = routes_ref[...].astype(jnp.float32)
-    prob = prob_ref[...]
-    prob = prob / jnp.sum(prob, axis=0, keepdims=True)
-    expert = lax.broadcasted_iota(jnp.int32, (EXPERTS, 64), 0).astype(jnp.float32)
-    hit = jnp.zeros((EXPERTS, 64), jnp.float32)
-    share = jnp.zeros((EXPERTS, 64), jnp.float32)
-    for k in range(8):
-        match = chosen[k : k + 1, :] == expert
-        hit = jnp.where(match, 1.0, hit)
-        share = jnp.where(match, prob[k : k + 1, :], share)
-    before = (
-        lax.broadcasted_iota(jnp.int32, (64, 64), 0) <= lax.broadcasted_iota(jnp.int32, (64, 64), 1)
-    ).astype(jnp.bfloat16)
-    rank = jnp.dot(hit.astype(jnp.bfloat16), before, preferred_element_type=jnp.float32)
-    info_a[0, 0, :EXPERTS] = rank * hit
-    info_a[0, 0, EXPERTS:] = share
-    for copy in info_copies():
-        copy.start()
 
     mixed = product[exp_index]
     for k in range(1, 4):
@@ -484,8 +454,8 @@
     rows = pl.ds(pl.multiple_of(exp_index * 64, 64), 64)
     after = hid_ref[rows, :].astype(jnp.float32) + residual_scale * mixed
     residual[...] = after
-    spread = lax.rsqrt(jnp.mean(after * after, axis=-1, keepdims=True) + norm_epsilon)
-    moe_in = (after * spread * gain_ref[...]).astype(jnp.bfloat16)
+    inverse = lax.rsqrt(jnp.mean(after * after, axis=-1, keepdims=True) + norm_epsilon)
+    moe_in = (after * inverse * moe_gain_ref[...][None, :]).astype(jnp.bfloat16)
     got_a[0, 0] = moe_in[:, :HALF]
     got_b[0, 0] = moe_in[:, HALF:]
     for copy in y_copies():
@@ -556,6 +526,9 @@
         for k in range(1, 4):
             go_b(k, i).start()
 
+    loads[6].wait()
+    loads[7].wait()
+
     @pl.loop(0, 4)
     def _(i):
         for k in range(1, 4):
@@ -569,11 +542,11 @@
                 ).wait_recv()
 
         hidden = jnp.dot(
-            recv_a[:, i].reshape(256, HALF), win_ref[:HALF, :], preferred_element_type=jnp.float32
-        ) + jnp.dot(recv_b[i].reshape(256, HALF), win_ref[HALF:, :], preferred_element_type=jnp.float32)
+            recv_a[:, i].reshape(256, HALF), win_ref[0, :HALF, :], preferred_element_type=jnp.float32
+        ) + jnp.dot(recv_b[i].reshape(256, HALF), win_ref[0, HALF:, :], preferred_element_type=jnp.float32)
         gate, up = hidden[:, :512], hidden[:, 512:]
         active = (gate / (1.0 + jnp.exp(-gate)) * up).astype(jnp.bfloat16)
-        done = jnp.dot(active, wout_ref[...], preferred_element_type=jnp.float32).astype(jnp.bfloat16)
+        done = jnp.dot(active, wout_ref[0], preferred_element_type=jnp.float32).astype(jnp.bfloat16)
         done_a = done[:, :HALF].reshape(4, 2, CAP, HALF)
         back_a[0, i] = done_a[0]
         for k in range(1, 4):
@@ -601,7 +574,7 @@
             ret_a(k, i).wait_recv()
         for m in range(2):
             some = mix(info_a, back_a, experts_a, i, m)
-            part_a[i, m] = some.astype(jnp.bfloat16)
+            sum_part_a[i, m] = some.astype(jnp.bfloat16)
 
             @pl.when(i == 0)
             def _():
@@ -619,7 +592,7 @@
         i = 3 - n
         for m in range(2):
             some = mix(info_b, back_b, experts_b, i, m)
-            part_b[i, m] = some.astype(jnp.bfloat16)
+            sum_part_b[i, m] = some.astype(jnp.bfloat16)
 
             @pl.when(i == 0)
             def _():
@@ -629,16 +602,16 @@
         def _():
             sum_b(i).start()
 
-    for n, (copy, acc, red) in enumerate(((sum_a, acc_a, red_a), (sum_b, acc_b, red_b))):
+    for n, (copy, half_acc, red) in enumerate(((sum_a, acc_a, red_a), (sum_b, acc_b, red_b))):
         for i in range(1, 4):
             copy(i).wait_recv()
-            acc[...] += red[i].astype(jnp.float32)
-        last_send[n] = acc[1].astype(jnp.bfloat16)
+            half_acc[...] += red[i].astype(jnp.float32)
+        last_send[n] = half_acc[1].astype(jnp.bfloat16)
         last_copy(n).start()
-    for n, acc in enumerate((acc_a, acc_b)):
+    for n, half_acc in enumerate((acc_a, acc_b)):
         last_copy(n).wait_recv()
         cols = slice(n * HALF, (n + 1) * HALF)
-        moe = acc[0] + last_recv[n].astype(jnp.float32)
+        moe = half_acc[0] + last_recv[n].astype(jnp.float32)
         out_ref[:, cols] = (residual[:, cols] + residual_scale * moe).astype(jnp.bfloat16)
 
     for k in range(1, 4):
@@ -665,25 +638,57 @@
             ret_a(k, i).wait_send()
 
 
-def experts(*operands):
+def layer(*operands):
     vmem = pl.BlockSpec(memory_space=pltpu.VMEM)
+    hbm = pl.BlockSpec(memory_space=pl.ANY)
+    specs = [hbm, vmem, hbm, hbm, hbm, hbm, vmem, hbm, vmem, vmem, vmem, hbm, hbm]
     width = 1536
-    table = pltpu.VMEM((4, 2, 64, 64), jnp.float32)
-    blocks = pltpu.VMEM((4, 2, 64, HALF), jnp.bfloat16)
-    chosen = pltpu.VMEM((4, 4, 2, CAP, HALF), jnp.bfloat16)
-    pair = pltpu.VMEM((2, 64, HALF), jnp.float32)
-    last = pltpu.VMEM((2, 64, HALF), jnp.bfloat16)
-    counts = ((4,), (13,), (2,), (2, 2, 4), (2, 4, 4), (4, 4), (2, 4), (2,))
+
+    def half(*shape):
+        return pltpu.VMEM(shape, jnp.bfloat16)
+
+    def full(*shape):
+        return pltpu.VMEM(shape, jnp.float32)
+
+    state = full(PLANES, KV_HERE, GROUP * ROWS, 128)
+    table = full(4, 2, 64, 64)
+    blocks = half(4, 2, 64, HALF)
+    chosen = half(4, 4, 2, CAP, HALF)
+    pair = full(2, 64, HALF)
+    counts = [(8,)] + [
+        n
+        for n in ((4,), (8,), (8,), (4,), (32,), (4,), (13,), (2,), (2, 2, 4), (2, 4, 4), (4, 4), (2, 4), (2,))
+        for _ in range(2)
+    ]
     return pl.pallas_call(
-        experts_kernel,
-        out_shape=jax.ShapeDtypeStruct((64, width), jnp.bfloat16),
-        in_specs=[vmem] * 8,
-        out_specs=vmem,
-        scratch_shapes=[
-            pltpu.VMEM((4, 64, width), jnp.float32),
-            pltpu.VMEM((4, 64, width), jnp.bfloat16),
-            pltpu.VMEM((4, 64, width), jnp.bfloat16),
-            pltpu.VMEM((64, width), jnp.float32),
+        layer_kernel,
+        out_shape=[
+            jax.ShapeDtypeStruct((64, width), jnp.bfloat16),
+            jax.ShapeDtypeStruct((2 * KV_HERE, ROWS // PAGE, PAGE * HEAD_DIM), jnp.bfloat16),
+        ],
+        in_specs=specs,
+        out_specs=[vmem] * 2,
+        scratch_shapes=[half(*operands[n].shape) for n in (0, 2, 3, 4, 7, 11, 12)]
+        + [
+            half(ROWS, 384),
+            half(ROWS, 384),
+            half(PLANES, ROWS, 384),
+            half(LINE // 2, 2 * CACHE_HERE, 256),
+            half(ROWS, 256),
+            half(LINE, ROWS, 256),
+            half(2 * CACHE_HERE, 256),
+            half(LINE, ROWS, 256),
+            half(PLANES, KV_HERE, GROUP * ROWS, 128),
+            state,
+            state,
+            half(PLANES, ROWS, 512),
+            half(PLANES, ROWS, 512),
+            full(ROWS, 256),
+            full(ROWS // PAGE, PAGE, 256),
+            full(4, 64, width),
+            half(4, 64, width),
+            half(4, 64, width),
+            full(64, width),
             table,
             table,
             blocks,
@@ -691,12 +696,12 @@
         ]
         + [chosen] * 8
         + [blocks] * 4
-        + [pair, pair, last, last]
-        + [pltpu.SemaphoreType.DMA(n) for n in counts for _ in range(2)],
+        + [pair, pair, half(2, 64, HALF), half(2, 64, HALF)]
+        + [pltpu.SemaphoreType.DMA(n) for n in counts],
         compiler_params=pltpu.CompilerParams(
-            vmem_limit_bytes=52 * 1024 * 1024, collective_id=2, has_side_effects=True
+            vmem_limit_bytes=62 * 1024 * 1024, collective_id=1, has_side_effects=True
         ),
-        name="experts",
+        name="layer",
     )(*operands)
 
 
@@ -715,14 +720,11 @@
     route_prob,
     page_slot,
 ):
-    attended, page_slabs = attend(
-        hidden_in, attn_gain[None, :], q_weight, k_weight, v_weight, cache_kv, page_slot.reshape(32, 32)
+    hidden_out, page_slabs = layer(
+        hidden_in, attn_gain, q_weight, k_weight, v_weight, cache_kv, page_slot,
+        o_weight, moe_gain, routes.T, route_prob.T, expert_in, expert_out,
     )
     page_rows = page_slabs.transpose(1, 0, 2).reshape(ROWS // PAGE, KV_HERE, 2, PAGE * HEAD_DIM)
-
-    hidden_out = experts(
-        attended, o_weight, hidden_in, moe_gain[None, :], routes.T, route_prob.T, expert_in[0], expert_out[0]
-    )
     return (hidden_out, page_rows)
 
 

time: 165 us -> 154 us (0.933)
  Pallas kernels: 157 us -> 149 us
  local copies, waits for them, and re-layouts: 6.65 us -> 3.31 us
    pallas_call x2 -> x1, Pallas kernels: 157 us -> 149 us  [layer(): pl.pallas_call(layer_kernel, out_shape=[jax.ShapeDtypeStruct((64, width),...]
    unnamed x14 -> x2, local copies, waits for them, and re-layouts: 4.42 us -> 3.31 us
where the time goes in v5:
time: 154 us; the launch traced here: 153 us
  Pallas kernels  149 us (97%)
  local copies, waits for them, and re-layouts  3.31 us (2%)
    pallas_call x1, Pallas kernels, layer(): pl.pallas_call(layer_kernel, out_shape=[jax.ShapeDtypeStruct((64, width),...  149 us
    unnamed x2, local copies, waits for them, and re-layouts  3.31 us

profile of v5, /device:TPU:0, one launch (start us, length us, event | category | flops | bytes accessed | tf_op | source)
XLA Modules:
  0.0 153.3 jit_solution(12448754681554520293)
XLA Ops:
  0.6 149.4 %layer.1 = (bf16[64,1536]{1,0:T(8,128)(2,1)}, bf16[4,32,512]{2,1,0:T(8,128)(2,1)}) custom-call(bf16[256,1536]{1,0:T(8,128)(2,1)} %hid_hbm.1, f32[1536]{0:T(1024)} %attn_gain_ref.1, bf16[1536,384]{1,0:T(8,128)(2,1)} %qw_hbm.1, bf16[1536,128]{1,0:T(8,128)(2,1)} %kw_hbm.1, bf16[1536,128]{1,0:T(8,128)(2,1)} %vw_hbm.1, bf16[512,256]{1,0:T(8,128)(2,1)} %cache_hbm.1, ...), custom_call_target="tpu_custom_call" | custom-call | tf_op jit(solution)/shard_map/layer/pallas_call | solution.py:663
  150.0 1.7 %copy.15 = bf16[32,2,2,512]{3,2,1,0:T(2,128)(2,1)} copy(bf16[32,2,2,512]{3,0,2,1:T(8,128)(2,1)} %bitcast.5) | data formatting | bytes 262144
  151.7 1.6 %copy.17 = bf16[64,1536]{1,0:T(8,128)(2,1)} copy(bf16[64,1536]{1,0:T(8,128)(2,1)} %get-tuple-element.10) | data formatting | bytes 393216

commit v6 on v5

--- a/solution.py
+++ b/solution.py
@@ -25,7 +25,9 @@
 masked_score = -1e30
 
 
-NEAR = ((0, 0), (0, 1), (1, 0), (0, 3), (1, 1), (0, 2), (1, 3), (1, 2))
+ORDER = ((0, 0), (0, 1), (1, 0), (0, 3), (0, 2), (1, 1), (1, 3), (1, 2))
+
+
 HALF = 768
 
 
@@ -33,10 +35,10 @@
     hid_hbm, attn_gain_ref, qw_hbm, kw_hbm, vw_hbm, cache_hbm, slot_ref,
     ow_hbm, moe_gain_ref, routes_ref, prob_ref, win_hbm, wout_hbm, out_ref, page_ref,
     hid_ref, qw_ref, kw_ref, vw_ref, ow_ref, win_ref, wout_ref, att_ref,
-    query, q_all, cache_all, new_own, new_all, cache_val, new_val, qs, best, acc,
+    query, q_all, cache_all, new_all, cache_val, qs, best, acc,
     part_send, part_recv, page_send, page_recv,
-    product, sum_send, sum_recv, residual, info_a, info_b, got_a, got_b, send_a, send_b, recv_a, recv_b,
-    made_a, made_b, back_a, back_b, sum_part_a, sum_part_b, red_a, red_b, acc_a, acc_b, last_send, last_recv,
+    sum_send, sum_recv, residual, info_a, info_b, got_a, got_b, send_a, send_b, recv_a, recv_b,
+    back_a, back_b, sum_part_a, sum_part_b, red_a, red_b, acc_a, acc_b, last_send, last_recv,
     load_in, q_out, q_in, cache_out, cache_in, new_out, new_in, part_out, part_in, page_out, page_in,
     sum_out, sum_in, info_out, info_in, y_out, y_in, wide_out, wide_in, go_out, go_in,
     ret_out, ret_in, red_out, red_in, last_out, last_in,
@@ -56,22 +58,40 @@
             device_id={"seq": to}, device_id_type=MESH,
         )
 
-    def peer(n):
-        h, x = NEAR[n]
-        return plane * LINE + lax.rem(place // 4 + h, 2) * 4 + lax.rem(place % 4 + x, 4)
-
     def line_peer(k):
         return lax.rem(plane + k, PLANES) * LINE + place
 
     def ahead(n):
         return lax.rem(seq_index + n, 32)
 
-    def cache_copy(n):
-        rows = pl.ds((n % 2) * CACHE_HERE, CACHE_HERE)
-        return send(cache_all.at[0, pl.ds(0, CACHE_HERE)], cache_all.at[n // 2, rows], cache_out.at[n], cache_in.at[n], peer(n))
-
-    def new_copy(n):
-        return send(new_own, new_all.at[place], new_out.at[n], new_in.at[n], peer(n))
+    def route(g, n):
+        m, j = ORDER[n]
+        if g == 0:
+            return ((0, 0), (0, 0, j)) if m == 0 else ((0, j), (0, 1, 0))
+        if j == 0:
+            return (0, 0), (0, 1, 0)
+        return (m, 0), (0, 0, j)
+
+    def cache_at(g, n):
+        return cache_all.at[g, n // 2, pl.ds((n % 2) * CACHE_HERE, CACHE_HERE)]
+
+    def cache_copy(g, n):
+        origin, to = route(g, n)
+        return send(
+            cache_at(g, ORDER.index(origin)), cache_at(g, n), cache_out.at[g, n], cache_in.at[g, n], at(*to)
+        )
+
+    def new_at(g, m, j):
+        return new_all.at[g, lax.rem(h + m, 2) * 4 + lax.rem(x + 4 - j, 4)]
+
+    def new_copy(g, n):
+        origin, to = route(g, n)
+        block = new_at(g, *origin)
+        return send(block, block, new_out.at[g, n], new_in.at[g, n], at(*to))
+
+    def new_wait(g, n):
+        block = new_at(g, *ORDER[n])
+        send(block, block, new_out.at[g, n], new_in.at[g, n], at(0, 1, 0)).wait_recv()
 
     def query_copy(k):
         return send(query, q_all.at[plane], q_out.at[k], q_in.at[k], line_peer(k))
@@ -143,10 +163,10 @@
         return send(send_b.at[k, i], recv_b.at[k, i], go_out.at[1, k, i], go_in.at[1, k, i], at(k, 0, 0))
 
     def ret_a(k, i):
-        return send(made_a.at[k, i], back_a.at[k, i], ret_out.at[k, i], ret_in.at[k, i], at(0, 0, -k))
+        return send(send_a.at[k, i], back_a.at[k, i], ret_out.at[k, i], ret_in.at[k, i], at(0, 0, -k))
 
     def ret_b(i):
-        return send(made_b.at[i], back_b.at[i], ret_out.at[0, i], ret_in.at[0, i], at(-i, 0, 0))
+        return send(send_b.at[i], back_b.at[i], ret_out.at[0, i], ret_in.at[0, i], at(-i, 0, 0))
 
     def sum_a(i):
         return send(sum_part_a.at[i], red_a.at[i], red_out.at[0, i], red_in.at[0, i], at(-i, 0, 0))
@@ -170,7 +190,8 @@
         pltpu.make_async_copy(source, target, load_in.at[n])
         for n, (source, target) in enumerate(
             (
-                (hid_hbm, hid_ref), (qw_hbm, qw_ref), (kw_hbm, kw_ref), (vw_hbm, vw_ref), (cache_hbm, cache_all.at[0, pl.ds(0, CACHE_HERE)]),
+                (hid_hbm, hid_ref), (qw_hbm, qw_ref), (kw_hbm, kw_ref), (vw_hbm, vw_ref), (cache_hbm.at[:, pl.ds(0, 128)], cache_all.at[0, 0, pl.ds(0, CACHE_HERE)]),
+                (cache_hbm.at[:, pl.ds(128, 128)], cache_all.at[1, 0, pl.ds(0, CACHE_HERE)]),
                 (ow_hbm, ow_ref), (win_hbm, win_ref), (wout_hbm, wout_ref),
             )
         )
@@ -195,6 +216,7 @@
         sum_send[step] = (wide * spread * attn_gain_ref[...][None, :]).astype(jnp.bfloat16)
 
     loads[4].wait()
+    loads[5].wait()
     loads[1].wait()
     normed = sum_send[...].reshape(ROWS, 1536)
     query[...] = jnp.dot(normed, qw_ref[...], preferred_element_type=jnp.float32).astype(jnp.bfloat16)
@@ -204,8 +226,9 @@
         def _():
             query_copy(k).start()
 
-    for n in range(1, 4):
-        cache_copy(n).start()
+    first_sends = ((1, 2), (0, 1), (0, 3), (0, 4), (0, 2), (1, 1), (1, 3), (1, 4))
+    for g, n in first_sends:
+        cache_copy(g, n).start()
     loads[2].wait()
     loads[3].wait()
     keys = jnp.dot(normed, kw_ref[...], preferred_element_type=jnp.float32)
@@ -215,12 +238,10 @@
         jnp.where(low, pltpu.roll(keys, HEAD_DIM, 1), values).astype(jnp.bfloat16),
     ]
     for g in range(KV_HERE):
-        new_own[:, g * 128 : (g + 1) * 128] = slabs[g]
+        new_all[g, place] = slabs[g]
         page_send[:, g * 128 : (g + 1) * 128] = slabs[g].astype(jnp.float32)
-    for n in range(1, LINE):
-        new_copy(n).start()
-    for n in range(4, LINE):
-        cache_copy(n).start()
+    for g, n in first_sends:
+        new_copy(g, n).start()
 
     @pl.loop(1, 32)
     def _(n):
@@ -246,7 +267,6 @@
         copy.start()
 
     q_all[plane] = query[...]
-    new_all[place] = new_own[...]
     own_rows = pl.ds(pl.multiple_of(seq_index * PAGE, PAGE), PAGE)
     page_recv[seq_index] = page_send[own_rows, :]
 
@@ -290,51 +310,62 @@
             query_copy(k).wait_recv()
             prepare(lax.rem(plane + PLANES - k, PLANES))
 
-    def cache_pair(m):
-        for part in range(4):
-            rows = slice(part * ROWS, (part + 1) * ROWS)
-            for g in range(KV_HERE):
-                cache_val[rows, slab_of(g)] = jnp.where(low, one, cache_all[m, rows, slab_of(g)])
-        update((0, 1), lambda g: cache_all[m, :, slab_of(g)], lambda g: cache_val[:, slab_of(g)])
-
-    def cache_pairs(start):
-        @pl.loop(start, start + 2)
-        def _(m):
-            @pl.when(m > 0)
+    def pass_on_cache(*steps):
+        for g, n, onward in steps:
+            cache_copy(g, n).wait_recv()
+            for later in onward:
+                cache_copy(g, later).start()
+
+    def pass_on_new(*steps):
+        for g, n, onward in steps:
+            new_wait(g, n)
+            for later in onward:
+                new_copy(g, later).start()
+
+    def new_keys(step):
+        return lambda g: new_all[g, pl.ds(step * 4, 4)].reshape(1024, 128)
+
+    def new_values(step):
+        for g in range(KV_HERE):
+            for part in range(4):
+                rows = slice(part * ROWS, (part + 1) * ROWS)
+                cache_val[g, rows, :] = jnp.where(low, one, new_all[g, step * 4 + part])
+        return lambda g: cache_val[g]
+
+    pass_on_cache((1, 2, (5, 6, 7)), (0, 1, (5,)))
+    needed = (((1, 1),), ((0, 2), (1, 3)), ((1, 4), (0, 5), (1, 5)), ((0, 6), (1, 6), (0, 7), (1, 7)))
+
+    @pl.loop(0, 4)
+    def _(pair):
+        for number, waits in enumerate(needed):
+            @pl.when(pair == number)
             def _():
-                send(
-                    cache_all.at[0, pl.ds(0, CACHE_HERE)], cache_all.at[m, pl.ds(0, CACHE_HERE)],
-                    cache_out.at[2 * m], cache_in.at[2 * m], peer(1),
-                ).wait_recv()
-
-            send(
-                cache_all.at[0, pl.ds(0, CACHE_HERE)], cache_all.at[m, pl.ds(CACHE_HERE, CACHE_HERE)],
-                cache_out.at[2 * m + 1], cache_in.at[2 * m + 1], peer(1),
-            ).wait_recv()
-            cache_pair(m)
-
-    cache_pairs(0)
-    for n in range(1, LINE):
-        dh, dx = NEAR[n]
-        origin = lax.rem(place // 4 + dh, 2) * 4 + lax.rem(place % 4 + 4 - dx, 4)
-        send(new_own, new_all.at[origin], new_out.at[n], new_in.at[n], peer(n)).wait_recv()
-
-    @pl.loop(0, LINE)
-    def _(n):
+                for g, n in waits:
+                    cache_copy(g, n).wait_recv()
+
         for g in range(KV_HERE):
-            new_val[n, :, slab_of(g)] = jnp.where(low, one, new_all[n, :, slab_of(g)])
-
-    def new_keys(step):
-        return lambda g: new_all[pl.ds(step * 4, 4), :, slab_of(g)].reshape(1024, 128)
-
-    def new_values(step):
-        return lambda g: new_val[pl.ds(step * 4, 4), :, slab_of(g)].reshape(1024, 128)
-
-    @pl.loop(0, jnp.where(even, 2, 0))
-    def _(step):
-        update((plane + 1,), new_keys(step), new_values(step))
-
-    cache_pairs(2)
+            for part in range(4):
+                rows = slice(part * ROWS, (part + 1) * ROWS)
+                cache_val[g, rows, :] = jnp.where(low, one, cache_all[g, pair, rows, :])
+        update((0, 1), lambda g: cache_all[g, pair], lambda g: cache_val[g])
+
+        @pl.when(pair == 0)
+        def _():
+            pass_on_cache((0, 3, (6,)), (0, 4, (7,)))
+            pass_on_new((1, 2, (5, 6, 7)), (0, 1, (5,)))
+
+        @pl.when(pair == 1)
+        def _():
+            pass_on_new((0, 3, (6,)), (0, 4, (7,)))
+
+        @pl.when(pair == 2)
+        def _():
+            for g, n in ((0, 2), (1, 1), (1, 3), (1, 4), (0, 5), (1, 5), (0, 6), (1, 6), (0, 7), (1, 7)):
+                new_wait(g, n)
+
+            @pl.loop(0, jnp.where(even, 2, 0))
+            def _(step):
+                update((plane + 1,), new_keys(step), new_values(step))
 
     def finish(t):
         heads = []
@@ -424,8 +455,9 @@
         att_ref[:, cols] = value.astype(jnp.bfloat16)
 
     for n in range(1, LINE):
-        cache_copy(n).wait_send()
-        new_copy(n).wait_send()
+        for g in range(KV_HERE):
+            cache_copy(g, n).wait_send()
+            new_copy(g, n).wait_send()
 
     for k in range(1, PLANES):
         @pl.when(sends_query(k))
@@ -440,14 +472,15 @@
     def _(n):
         page_copy(n).wait_send()
 
-    loads[5].wait()
-    product[...] = jnp.dot(att_ref[...], ow_ref[...], preferred_element_type=jnp.float32).reshape(product.shape)
-    for k in range(1, 4):
-        sum_send[k] = product[side(k)].astype(jnp.bfloat16)
-    for k in range(1, 4):
+    loads[6].wait()
+    def project(k):
+        rows = pl.ds(pl.multiple_of(side(k) * 64, 64), 64)
+        return jnp.dot(att_ref[rows, :], ow_ref[...], preferred_element_type=jnp.float32)
+
+    for k in (2, 1, 3):
+        sum_send[k] = project(k).astype(jnp.bfloat16)
         sum_copy(k).start()
-
-    mixed = product[exp_index]
+    mixed = project(0)
     for k in range(1, 4):
         sum_copy(k).wait_recv()
         mixed = mixed + sum_recv[k].astype(jnp.float32)
@@ -526,20 +559,23 @@
         for k in range(1, 4):
             go_b(k, i).start()
 
-    loads[6].wait()
     loads[7].wait()
+    loads[8].wait()
 
     @pl.loop(0, 4)
     def _(i):
         for k in range(1, 4):
             go_a(k, i).wait_recv()
+            go_a(k, i).wait_send()
 
         @pl.when(i > 0)
         def _():
             for j in range(4):
-                send(
+                copy = send(
                     send_b.at[i, j], recv_b.at[i, j], go_out.at[1, i, j], go_in.at[1, i, j], at(i, 0, 0)
-                ).wait_recv()
+                )
+                copy.wait_recv()
+                copy.wait_send()
 
         hidden = jnp.dot(
             recv_a[:, i].reshape(256, HALF), win_ref[0, :HALF, :], preferred_element_type=jnp.float32
@@ -550,9 +586,9 @@
         done_a = done[:, :HALF].reshape(4, 2, CAP, HALF)
         back_a[0, i] = done_a[0]
         for k in range(1, 4):
-            made_a[k, i] = done_a[k]
+            send_a[k, i] = done_a[k]
             ret_a(k, i).start()
-        made_b[i] = done[:, HALF:].reshape(4, 2, CAP, HALF)
+        send_b[i] = done[:, HALF:].reshape(4, 2, CAP, HALF)
 
         @pl.when(i > 0)
         def _():
@@ -560,7 +596,7 @@
 
         @pl.when(i == 0)
         def _():
-            back_b[0] = made_b[0]
+            back_b[0] = send_b[0]
 
     def mix(info, backs, experts_of, i, m):
         return lax.dot_general(
@@ -633,8 +669,6 @@
     @pl.loop(0, 4)
     def _(i):
         for k in range(1, 4):
-            go_a(k, i).wait_send()
-            go_b(k, i).wait_send()
             ret_a(k, i).wait_send()
 
 
@@ -655,9 +689,9 @@
     blocks = half(4, 2, 64, HALF)
     chosen = half(4, 4, 2, CAP, HALF)
     pair = full(2, 64, HALF)
-    counts = [(8,)] + [
+    counts = [(9,)] + [
         n
-        for n in ((4,), (8,), (8,), (4,), (32,), (4,), (13,), (2,), (2, 2, 4), (2, 4, 4), (4, 4), (2, 4), (2,))
+        for n in ((4,), (2, 8), (2, 8), (4,), (32,), (4,), (13,), (2,), (2, 2, 4), (2, 4, 4), (4, 4), (2, 4), (2,))
         for _ in range(2)
     ]
     return pl.pallas_call(
@@ -673,11 +707,9 @@
             half(ROWS, 384),
             half(ROWS, 384),
             half(PLANES, ROWS, 384),
-            half(LINE // 2, 2 * CACHE_HERE, 256),
-            half(ROWS, 256),
-            half(LINE, ROWS, 256),
-            half(2 * CACHE_HERE, 256),
-            half(LINE, ROWS, 256),
+            half(KV_HERE, LINE // 2, 2 * CACHE_HERE, 128),
+            half(KV_HERE, LINE, ROWS, 128),
+            half(KV_HERE, 2 * CACHE_HERE, 128),
             half(PLANES, KV_HERE, GROUP * ROWS, 128),
             state,
             state,
@@ -685,7 +717,6 @@
             half(PLANES, ROWS, 512),
             full(ROWS, 256),
             full(ROWS // PAGE, PAGE, 256),
-            full(4, 64, width),
             half(4, 64, width),
             half(4, 64, width),
             full(64, width),
@@ -694,7 +725,7 @@
             blocks,
             blocks,
         ]
-        + [chosen] * 8
+        + [chosen] * 6
         + [blocks] * 4
         + [pair, pair, half(2, 64, HALF), half(2, 64, HALF)]
         + [pltpu.SemaphoreType.DMA(n) for n in counts],

time: 154 us -> 148 us (0.961)
  Pallas kernels: 149 us -> 143 us
    pallas_call x1, Pallas kernels: 149 us -> 143 us  [layer(): pl.pallas_call(layer_kernel, out_shape=[jax.ShapeDtypeStruct((64, width),...]
where the time goes in v6:
time: 148 us; the launch traced here: 147 us
  Pallas kernels  143 us (97%)
  local copies, waits for them, and re-layouts  3.31 us (2%)
    pallas_call x1, Pallas kernels, layer(): pl.pallas_call(layer_kernel, out_shape=[jax.ShapeDtypeStruct((64, width),...  143 us
    unnamed x2, local copies, waits for them, and re-layouts  3.31 us

profile of v6, /device:TPU:0, one launch (start us, length us, event | category | flops | bytes accessed | tf_op | source)
XLA Modules:
  0.0 147.4 jit_solution(11726619251397251893)
XLA Ops:
  0.6 143.4 %layer.1 = (bf16[64,1536]{1,0:T(8,128)(2,1)}, bf16[4,32,512]{2,1,0:T(8,128)(2,1)}) custom-call(bf16[256,1536]{1,0:T(8,128)(2,1)} %hid_hbm.1, f32[1536]{0:T(1024)} %attn_gain_ref.1, bf16[1536,384]{1,0:T(8,128)(2,1)} %qw_hbm.1, bf16[1536,128]{1,0:T(8,128)(2,1)} %kw_hbm.1, bf16[1536,128]{1,0:T(8,128)(2,1)} %vw_hbm.1, bf16[512,256]{1,0:T(8,128)(2,1)} %cache_hbm.1, ...), custom_call_target="tpu_custom_call" | custom-call | tf_op jit(solution)/shard_map/layer/pallas_call | solution.py:697
  144.1 1.7 %copy.15 = bf16[32,2,2,512]{3,2,1,0:T(2,128)(2,1)} copy(bf16[32,2,2,512]{3,0,2,1:T(8,128)(2,1)} %bitcast.5) | data formatting | bytes 262144
  145.7 1.6 %copy.17 = bf16[64,1536]{1,0:T(8,128)(2,1)} copy(bf16[64,1536]{1,0:T(8,128)(2,1)} %get-tuple-element.10) | data formatting | bytes 393216

commit v7 on v6

--- a/solution.py
+++ b/solution.py
@@ -36,10 +36,10 @@
     ow_hbm, moe_gain_ref, routes_ref, prob_ref, win_hbm, wout_hbm, out_ref, page_ref,
     hid_ref, qw_ref, kw_ref, vw_ref, ow_ref, win_ref, wout_ref, att_ref,
     query, q_all, cache_all, new_all, cache_val, qs, best, acc,
-    part_send, part_recv, page_send, page_recv,
-    sum_send, sum_recv, residual, info_a, info_b, got_a, got_b, send_a, send_b, recv_a, recv_b,
+    part_send, part_recv, level_send, level_recv, page_send, page_recv,
+    core_send, core_recv, chip_send, chip_recv, normed, residual, info_a, info_b, got_a, got_b, send_a, send_b, recv_a, recv_b,
     back_a, back_b, sum_part_a, sum_part_b, red_a, red_b, acc_a, acc_b, last_send, last_recv,
-    load_in, q_out, q_in, cache_out, cache_in, new_out, new_in, part_out, part_in, page_out, page_in,
+    load_in, q_out, q_in, cache_out, cache_in, new_out, new_in, part_out, part_in, level_out, level_in, page_out, page_in,
     sum_out, sum_in, info_out, info_in, y_out, y_in, wide_out, wide_in, go_out, go_in,
     ret_out, ret_in, red_out, red_in, last_out, last_in,
 ):
@@ -99,6 +99,9 @@
     def part_copy(k):
         return send(part_send.at[k], part_recv.at[k], part_out.at[k], part_in.at[k], line_peer(k))
 
+    def level_copy(k):
+        return send(level_send.at[k], level_recv.at[k], level_out.at[k], level_in.at[k], line_peer(k))
+
     def page_copy(n):
         rows = pl.ds(pl.multiple_of(ahead(n) * PAGE, PAGE), PAGE)
         return send(page_send.at[rows], page_recv.at[seq_index], page_out.at[n], page_in.at[n], ahead(n))
@@ -126,10 +129,15 @@
     def side(k):
         return lax.rem(exp_index + k, 4)
 
-    def sum_copy(k):
+    core = lax.rem(exp_index, 2)
+    chip = exp_index // 2
+
+    def sum_copy(n):
+        to = chip * 2 + 1 - core if n == 0 else (1 - chip) * 2 + core
+        source, target = ((core_send, core_recv), (chip_send, chip_recv))[n]
         return pltpu.make_async_remote_copy(
-            src_ref=sum_send.at[k], dst_ref=sum_recv.at[k], send_sem=sum_out.at[k], recv_sem=sum_in.at[k],
-            device_id={"exp": side(k)}, device_id_type=MESH,
+            src_ref=source, dst_ref=target, send_sem=sum_out.at[n], recv_sem=sum_in.at[n],
+            device_id={"exp": to}, device_id_type=MESH,
         )
 
     z_peers = [(i, m) for i in range(4) for m in range(2) if (i, m) != (0, 0)]
@@ -201,8 +209,8 @@
     for k in range(1, PLANES):
         @pl.when(jnp.logical_not(gets_part(k)))
         def _():
-            part_recv[k, :, :384] = jnp.zeros((ROWS, 384), jnp.bfloat16)
-            part_recv[k, :, 384:] = jnp.full((ROWS, 128), masked_score, jnp.bfloat16)
+            part_recv[k] = jnp.zeros((ROWS, 384), jnp.bfloat16)
+            level_recv[k] = jnp.full((8, ROWS), masked_score, jnp.float32)
 
     best[...] = jnp.full_like(best, masked_score)
     acc[...] = jnp.zeros_like(acc)
@@ -213,13 +221,12 @@
         rows = pl.ds(pl.multiple_of(step * 64, 64), 64)
         wide = hid_ref[rows, :].astype(jnp.float32)
         spread = lax.rsqrt(jnp.mean(wide * wide, axis=-1, keepdims=True) + norm_epsilon)
-        sum_send[step] = (wide * spread * attn_gain_ref[...][None, :]).astype(jnp.bfloat16)
+        normed[rows, :] = (wide * spread * attn_gain_ref[...][None, :]).astype(jnp.bfloat16)
 
     loads[4].wait()
     loads[5].wait()
     loads[1].wait()
-    normed = sum_send[...].reshape(ROWS, 1536)
-    query[...] = jnp.dot(normed, qw_ref[...], preferred_element_type=jnp.float32).astype(jnp.bfloat16)
+    query[...] = jnp.dot(normed[...], qw_ref[...], preferred_element_type=jnp.float32).astype(jnp.bfloat16)
     pl.semaphore_wait(barrier, 31 + 3)
     for k in range(1, PLANES):
         @pl.when(sends_query(k))
@@ -231,8 +238,8 @@
         cache_copy(g, n).start()
     loads[2].wait()
     loads[3].wait()
-    keys = jnp.dot(normed, kw_ref[...], preferred_element_type=jnp.float32)
-    values = jnp.dot(normed, vw_ref[...], preferred_element_type=jnp.float32)
+    keys = jnp.dot(normed[...], kw_ref[...], preferred_element_type=jnp.float32)
+    values = jnp.dot(normed[...], vw_ref[...], preferred_element_type=jnp.float32)
     slabs = [
         jnp.where(low, keys, pltpu.roll(values, HEAD_DIM, 1)).astype(jnp.bfloat16),
         jnp.where(low, pltpu.roll(keys, HEAD_DIM, 1), values).astype(jnp.bfloat16),
@@ -388,11 +395,8 @@
             pairs, levels = finish(lax.rem(plane + k, PLANES))
             for p in range(HEADS_HERE // 2):
                 part_send[k, :, p * 128 : (p + 1) * 128] = pairs[p].astype(jnp.bfloat16)
-            high = levels.astype(jnp.bfloat16).astype(jnp.float32)
-            rest = levels - high
-            middle = rest.astype(jnp.bfloat16).astype(jnp.float32)
-            split = jnp.where(lane < 8, high, jnp.where(lane < 16, middle, rest - middle))
-            part_send[k, :, 384:512] = split.astype(jnp.bfloat16)
+            level_send[k] = levels.T[:8, :]
+            level_copy(k).start()
             part_copy(k).start()
 
     @pl.loop(0, place // 4 + 1)
@@ -435,10 +439,10 @@
         @pl.when(gets_part(k))
         def _():
             part_copy(k).wait_recv()
+            level_copy(k).wait_recv()
     levels = [own_level]
     for k in range(1, PLANES):
-        slab = part_recv[k, :, 384:512].astype(jnp.float32)
-        levels.append(slab + pltpu.roll(slab, 120, 1) + pltpu.roll(slab, 112, 1))
+        levels.append(jnp.concatenate([level_recv[k]] * 16, axis=0).T)
     top = functools.reduce(jnp.maximum, levels)
     shares = [jnp.exp(level - top) for level in levels]
     whole = functools.reduce(jnp.add, shares)
@@ -467,23 +471,28 @@
         @pl.when(sends_part(k))
         def _():
             part_copy(k).wait_send()
+            level_copy(k).wait_send()
 
     @pl.loop(1, 32)
     def _(n):
         page_copy(n).wait_send()
 
     loads[6].wait()
-    def project(k):
-        rows = pl.ds(pl.multiple_of(side(k) * 64, 64), 64)
+    def project(of_chip, of_core):
+        rows = pl.ds(pl.multiple_of((of_chip * 2 + of_core) * 64, 64), 64)
         return jnp.dot(att_ref[rows, :], ow_ref[...], preferred_element_type=jnp.float32)
 
-    for k in (2, 1, 3):
-        sum_send[k] = project(k).astype(jnp.bfloat16)
-        sum_copy(k).start()
-    mixed = project(0)
-    for k in range(1, 4):
-        sum_copy(k).wait_recv()
-        mixed = mixed + sum_recv[k].astype(jnp.float32)
+    core_send[0] = project(1 - chip, 1 - core).astype(jnp.bfloat16)
+    core_send[1] = project(chip, 1 - core).astype(jnp.bfloat16)
+    sum_copy(0).start()
+    away = project(1 - chip, core)
+    mixed = project(chip, core)
+    sum_copy(0).wait_recv()
+    chip_send[...] = (away + core_recv[0].astype(jnp.float32)).astype(jnp.bfloat16)
+    sum_copy(1).start()
+    mixed = mixed + core_recv[1].astype(jnp.float32)
+    sum_copy(1).wait_recv()
+    mixed = mixed + chip_recv[...].astype(jnp.float32)
     rows = pl.ds(pl.multiple_of(exp_index * 64, 64), 64)
     after = hid_ref[rows, :].astype(jnp.float32) + residual_scale * mixed
     residual[...] = after
@@ -650,8 +659,8 @@
         moe = half_acc[0] + last_recv[n].astype(jnp.float32)
         out_ref[:, cols] = (residual[:, cols] + residual_scale * moe).astype(jnp.bfloat16)
 
-    for k in range(1, 4):
-        sum_copy(k).wait_send()
+    for n in range(2):
+        sum_copy(n).wait_send()
     for copy in info_copies() + y_copies():
         copy.wait_send()
     for n in range(2):
@@ -691,7 +700,7 @@
     pair = full(2, 64, HALF)
     counts = [(9,)] + [
         n
-        for n in ((4,), (2, 8), (2, 8), (4,), (32,), (4,), (13,), (2,), (2, 2, 4), (2, 4, 4), (4, 4), (2, 4), (2,))
+        for n in ((4,), (2, 8), (2, 8), (4,), (4,), (32,), (2,), (13,), (2,), (2, 2, 4), (2, 4, 4), (4, 4), (2, 4), (2,))
         for _ in range(2)
     ]
     return pl.pallas_call(
@@ -713,12 +722,17 @@
             half(PLANES, KV_HERE, GROUP * ROWS, 128),
             state,
             state,
-            half(PLANES, ROWS, 512),
-            half(PLANES, ROWS, 512),
+            half(PLANES, ROWS, 384),
+            half(PLANES, ROWS, 384),
+            full(PLANES, 8, ROWS),
+            full(PLANES, 8, ROWS),
             full(ROWS, 256),
             full(ROWS // PAGE, PAGE, 256),
-            half(4, 64, width),
-            half(4, 64, width),
+            half(2, 64, width),
+            half(2, 64, width),
+            half(64, width),
+            half(64, width),
+            half(ROWS, width),
             full(64, width),
             table,
             table,

time: 148 us -> 145 us (0.980)
  Pallas kernels: 143 us -> 141 us
    pallas_call x1, Pallas kernels: 143 us -> 141 us  [layer(): pl.pallas_call(layer_kernel, out_shape=[jax.ShapeDtypeStruct((64, width),...]
where the time goes in v7:
time: 145 us
  Pallas kernels  141 us (97%)
  local copies, waits for them, and re-layouts  3.31 us (2%)
    pallas_call x1, Pallas kernels, layer(): pl.pallas_call(layer_kernel, out_shape=[jax.ShapeDtypeStruct((64, width),...  141 us
    unnamed x2, local copies, waits for them, and re-layouts  3.31 us

profile of v7, /device:TPU:0, one launch (start us, length us, event | category | flops | bytes accessed | tf_op | source)
XLA Modules:
  0.0 144.7 jit_solution(13756541922084111305)
XLA Ops:
  0.6 140.8 %layer.1 = (bf16[64,1536]{1,0:T(8,128)(2,1)}, bf16[4,32,512]{2,1,0:T(8,128)(2,1)}) custom-call(bf16[256,1536]{1,0:T(8,128)(2,1)} %hid_hbm.1, f32[1536]{0:T(1024)} %attn_gain_ref.1, bf16[1536,384]{1,0:T(8,128)(2,1)} %qw_hbm.1, bf16[1536,128]{1,0:T(8,128)(2,1)} %kw_hbm.1, bf16[1536,128]{1,0:T(8,128)(2,1)} %vw_hbm.1, bf16[512,256]{1,0:T(8,128)(2,1)} %cache_hbm.1, ...), custom_call_target="tpu_custom_call" | custom-call | tf_op jit(solution)/shard_map/layer/pallas_call | solution.py:706
  141.4 1.7 %copy.15 = bf16[32,2,2,512]{3,2,1,0:T(2,128)(2,1)} copy(bf16[32,2,2,512]{3,0,2,1:T(8,128)(2,1)} %bitcast.5) | data formatting | bytes 262144
  143.1 1.6 %copy.17 = bf16[64,1536]{1,0:T(8,128)(2,1)} copy(bf16[64,1536]{1,0:T(8,128)(2,1)} %get-tuple-element.10) | data formatting | bytes 393216

commit v8 on v7

--- a/solution.py
+++ b/solution.py
@@ -365,15 +365,6 @@
         def _():
             pass_on_new((0, 3, (6,)), (0, 4, (7,)))
 
-        @pl.when(pair == 2)
-        def _():
-            for g, n in ((0, 2), (1, 1), (1, 3), (1, 4), (0, 5), (1, 5), (0, 6), (1, 6), (0, 7), (1, 7)):
-                new_wait(g, n)
-
-            @pl.loop(0, jnp.where(even, 2, 0))
-            def _(step):
-                update((plane + 1,), new_keys(step), new_values(step))
-
     def finish(t):
         heads = []
         for h in range(HEADS_HERE):
@@ -389,7 +380,7 @@
             for p in range(HEADS_HERE // 2)
         ], levels
 
-    for k in range(1, PLANES):
+    def send_part(k):
         @pl.when(sends_part(k))
         def _():
             pairs, levels = finish(lax.rem(plane + k, PLANES))
@@ -398,6 +389,17 @@
             level_send[k] = levels.T[:8, :]
             level_copy(k).start()
             part_copy(k).start()
+
+    send_part(2)
+    send_part(3)
+    for g, n in ((0, 2), (1, 1), (1, 3), (1, 4), (0, 5), (1, 5), (0, 6), (1, 6), (0, 7), (1, 7)):
+        new_wait(g, n)
+
+    @pl.loop(0, jnp.where(even, 2, 0))
+    def _(step):
+        update((plane + 1,), new_keys(step), new_values(step))
+
+    send_part(1)
 
     @pl.loop(0, place // 4 + 1)
     def _(step):
@@ -544,7 +546,9 @@
             sends[k, i, m] = taken[k * CAP : (k + 1) * CAP]
 
     @pl.loop(0, 4)
-    def _(i):
+    def _(turn):
+        i = turn + (turn // 2) * (5 - 2 * turn)
+
         @pl.when(i == 0)
         def _():
             for copy in y_copies():
@@ -572,7 +576,9 @@
     loads[8].wait()
 
     @pl.loop(0, 4)
-    def _(i):
+    def _(turn):
+        i = turn + (turn // 2) * (5 - 2 * turn)
+
         for k in range(1, 4):
             go_a(k, i).wait_recv()
             go_a(k, i).wait_send()
@@ -614,7 +620,9 @@
         )
 
     @pl.loop(0, 4)
-    def _(i):
+    def _(turn):
+        i = turn + (turn // 2) * (5 - 2 * turn)
+
         for k in range(1, 4):
             ret_a(k, i).wait_recv()
         for m in range(2):

time: 145 us -> 143 us (0.986)
  Pallas kernels: 141 us -> 139 us
    pallas_call x1, Pallas kernels: 141 us -> 139 us  [layer(): pl.pallas_call(layer_kernel, out_shape=[jax.ShapeDtypeStruct((64, width),...]
where the time goes in v8:
time: 143 us
  Pallas kernels  139 us (97%)
  local copies, waits for them, and re-layouts  3.31 us (2%)
    pallas_call x1, Pallas kernels, layer(): pl.pallas_call(layer_kernel, out_shape=[jax.ShapeDtypeStruct((64, width),...  139 us
    unnamed x2, local copies, waits for them, and re-layouts  3.31 us

profile of v8, /device:TPU:0, one launch (start us, length us, event | category | flops | bytes accessed | tf_op | source)
XLA Modules:
  0.0 142.7 jit_solution(14922901710235630617)
XLA Ops:
  0.6 138.8 %layer.1 = (bf16[64,1536]{1,0:T(8,128)(2,1)}, bf16[4,32,512]{2,1,0:T(8,128)(2,1)}) custom-call(bf16[256,1536]{1,0:T(8,128)(2,1)} %hid_hbm.1, f32[1536]{0:T(1024)} %attn_gain_ref.1, bf16[1536,384]{1,0:T(8,128)(2,1)} %qw_hbm.1, bf16[1536,128]{1,0:T(8,128)(2,1)} %kw_hbm.1, bf16[1536,128]{1,0:T(8,128)(2,1)} %vw_hbm.1, bf16[512,256]{1,0:T(8,128)(2,1)} %cache_hbm.1, ...), custom_call_target="tpu_custom_call" | custom-call | tf_op jit(solution)/shard_map/layer/pallas_call | solution.py:714
  139.4 1.7 %copy.15 = bf16[32,2,2,512]{3,2,1,0:T(2,128)(2,1)} copy(bf16[32,2,2,512]{3,0,2,1:T(8,128)(2,1)} %bitcast.5) | data formatting | bytes 262144
  141.1 1.6 %copy.17 = bf16[64,1536]{1,0:T(8,128)(2,1)} copy(bf16[64,1536]{1,0:T(8,128)(2,1)} %get-tuple-element.10) | data formatting | bytes 393216
